TPU v7x, 128 devices: a whole 4x4x4 slice. The times are simulated.
128 devices in a mesh: gx: 8 (over x, core), gy: 16 (over y, z).
Axes of the slice: x: 4, y: 4, z: 4, core: 2. Of those that a mesh axis runs over, the one named last changes fastest.
Arguments:
- blocks: float32 [16, 16, 9, 128, 128], P('gx', 'gy'), may hold values from -0.0625 to 0.0625
- pair_mask: int32 [16, 16, 9, 8, 8], P('gx', 'gy'), may hold values 0 or 1
- rhs_rows: float32 [16, 16, 9, 128, 128], P('gx', 'gy'), may hold values from -6 to 6
- counts: int32 [16, 16, 8], P('gx', 'gy'), may hold values from 1 to 3, as said below
Outputs:
- solution: float32 [16, 16, 9, 128, 128], P('gx', 'gy')
Inputs may be any that keep to these rules, and one draw needn't show every extreme that they name: `counts`: cut the first block index into runs of 2 blocks. Within each second index b, run a and run a + 4 together hold at most 2 blocks that have an atom with a count of 2 or more, and some run holds 2 such blocks; at least one atom takes 3 iterations and at least one takes 1.
All inputs are finite; a program needn't handle non-finite values. No bound on the sum of `pair_mask` on one device may be relied on, other than what follows from the above.
Results may differ from a plain program's by a relative error of at most 0.0003.
Values sent between devices are 32-bit elements; how exact they have to be, the bound alone decides.
No kernel may reach another device: no remote copies, remote signals or barrier semaphores. Data moves between devices by JAX's collectives and lax.ppermute only.
A program may use at most 128 MiB of HBM per device.

v0:
```python
import jax
import jax.numpy as jnp
from jax import lax
from jax.sharding import PartitionSpec as P

ITERS = 3


def with_halo(block, sides, width):
    for axis, dim in sides:
        count = lax.axis_size(axis)
        forward = [(i, i + 1) for i in range(count - 1)]
        backward = [(target, source) for source, target in forward]
        low = lax.ppermute(
            lax.slice_in_dim(block, block.shape[dim] - width, None, axis=dim), axis, forward
        )
        high = lax.ppermute(lax.slice_in_dim(block, 0, width, axis=dim), axis, backward)
        block = jnp.concatenate([low, block, high], axis=dim)
    return block


def expand_mask(pair_mask, orbitals):
    shaped = pair_mask.astype(jnp.float32)[..., :, None, :, None]
    leading = pair_mask.shape[:-2]
    atom_count = pair_mask.shape[-1]
    expanded = jnp.broadcast_to(shaped, leading + (atom_count, orbitals, atom_count, orbitals))
    return expanded.reshape(leading + (atom_count * orbitals, atom_count * orbitals))


def cluster_apply(window, vectors):
    result = vectors
    for row_off in (-1, 0, 1):
        for col_off in (-1, 0, 1):
            offset = 3 * (row_off + 1) + (col_off + 1)
            row_low, row_high = (max(0, -row_off), min(3, 3 - row_off))
            col_low, col_high = (max(0, -col_off), min(3, 3 - col_off))
            coupled = window[..., row_low:row_high, col_low:col_high, offset, :, :]
            source = vectors[
                ...,
                row_low + row_off : row_high + row_off,
                col_low + col_off : col_high + col_off,
                :,
                :,
            ]
            product = jnp.einsum(
                "...xyij,...xyjc->...xyic", coupled, source, precision=lax.Precision.HIGHEST
            )
            result = result.at[..., row_low:row_high, col_low:col_high, :, :].add(-product)
    return result


def cluster_rhs(rhs_window):
    rows_list = []
    for row_pos in range(3):
        pieces = []
        for col_pos in range(3):
            pieces.append(rhs_window[..., row_pos, col_pos, 8 - 3 * row_pos - col_pos, :, :])
        rows_list.append(jnp.stack(pieces, axis=-3))
    return jnp.stack(rows_list, axis=-4)


def column_inner(left, other):
    return jnp.sum(left * other, axis=(-4, -3, -2))


def spread(scalar):
    return scalar[..., None, None, None, :]


def guarded(top, bottom, floor_val):
    return top * bottom / (bottom * bottom + floor_val * floor_val)


def start_state(window, right_side):
    image_first = cluster_apply(window, right_side)
    zero_field = jnp.zeros_like(right_side)
    norm_rhs = column_inner(right_side, right_side)
    zero_cols = jnp.zeros_like(norm_rhs)
    vectors = (right_side, right_side, right_side, image_first, image_first, zero_field, zero_field)
    scalars = (norm_rhs, 0.1 * norm_rhs, jnp.sqrt(norm_rhs), zero_cols, zero_cols, norm_rhs)
    return (vectors, scalars)


def iterate(window, vectors, scalars, iteration, limit_cols):
    shadow, residual, first_dir, image_first, vector, direction, solution = vectors
    rho_value, rho_floor, tau_value, theta_value, eta_value, norm_rhs = scalars
    alpha_floor = 0.1 * jnp.sqrt(norm_rhs * (column_inner(vector, vector) + 1e-06))
    alpha_value = guarded(rho_value, column_inner(shadow, vector), alpha_floor)
    step_ratio = guarded(1.0, alpha_value, 0.1)
    second = first_dir - spread(alpha_value) * vector
    image_second = cluster_apply(window, second)
    active = spread((limit_cols > iteration).astype(jnp.float32))
    for half_dir, half_image in ((first_dir, image_first), (second, image_second)):
        residual = residual - spread(alpha_value) * half_image
        direction = (
            half_dir + spread(theta_value * theta_value * eta_value * step_ratio) * direction
        )
        theta_value = jnp.sqrt(column_inner(residual, residual)) / tau_value
        cosine = 1.0 / jnp.sqrt(1.0 + theta_value * theta_value)
        tau_value = tau_value * theta_value * cosine
        eta_value = cosine * cosine * alpha_value
        solution = solution + active * spread(eta_value) * direction
    vectors = (shadow, residual, second, image_second, vector, direction, solution)
    scalars = (rho_value, rho_floor, tau_value, theta_value, eta_value, norm_rhs)
    return (vectors, scalars)


def advance(window, vectors, scalars):
    shadow, residual, second, image_second, vector, direction, solution = vectors
    rho_value, rho_floor, tau_value, theta_value, eta_value, norm_rhs = scalars
    rho_next = column_inner(shadow, residual)
    beta_value = guarded(rho_next, rho_value, rho_floor)
    next_floor = 0.1 * jnp.sqrt(norm_rhs * column_inner(residual, residual))
    first_dir = residual + spread(beta_value) * second
    image_first = cluster_apply(window, first_dir)
    vector = image_first + spread(beta_value) * (image_second + spread(beta_value) * vector)
    vectors = (shadow, residual, first_dir, image_first, vector, direction, solution)
    scalars = (rho_next, next_floor, tau_value, theta_value, eta_value, norm_rhs)
    return (vectors, scalars)


def first_section(window, right_side, limit_cols):
    vectors, scalars = start_state(window, right_side)
    return iterate(window, vectors, scalars, 0, limit_cols)


def later_section(window, vectors, scalars, limit_cols):
    for iteration in range(1, ITERS):
        vectors, scalars = advance(window, vectors, scalars)
        vectors, scalars = iterate(window, vectors, scalars, iteration, limit_cols)
    return vectors[6]


def shards(blocks, pair_mask, rhs_rows, counts):
    orbitals = blocks.shape[-1] // pair_mask.shape[-1]
    group_count = blocks.shape[0]
    rows_block = blocks.shape[-1]
    coupling = blocks * expand_mask(pair_mask, orbitals)
    padded_coupling, padded_rhs = (
        with_halo(coupling, (("gx", 0), ("gy", 1)), 1),
        with_halo(rhs_rows, (("gx", 0), ("gy", 1)), 1),
    )
    windows = jnp.stack(
        [padded_coupling[local_pos : local_pos + 3] for local_pos in range(group_count)]
    )
    rhs_windows = jnp.stack(
        [padded_rhs[local_pos : local_pos + 3] for local_pos in range(group_count)]
    )
    right_side = cluster_rhs(rhs_windows)
    limits = (
        jnp.repeat(counts, orbitals, axis=-1).reshape(group_count, rows_block).astype(jnp.float32)
    )
    vectors, scalars = first_section(windows, right_side, limits)
    solution = later_section(windows, vectors, scalars, limits)
    return solution.reshape(group_count, 1, 9, rows_block, solution.shape[-1])


def solution(mesh):
    return jax.shard_map(
        shards,
        mesh=mesh,
        in_specs=(
            P("gx", "gy", None, None, None),
            P("gx", "gy", None, None, None),
            P("gx", "gy", None, None, None),
            P("gx", "gy", None),
        ),
        out_specs=P("gx", "gy", None, None, None),
        check_vma=False,
    )
```

profile of v0, /device:TPU:5, one launch (start us, length us, event | category | flops | bytes accessed | tf_op | source)
XLA Modules:
  0.0 219.3 jit_solution(685303909633288874)
XLA Ops:
  1.0 4.3 %broadcast_in_dim.14 = f32[2,9,8,16,8,16]{5,4,3,2,0,1:T(8,128)} broadcast(f32[2,9,8,8]{3,2,0,1:T(8,128)S(1)} %copy.10), dimensions={0,1,2,4} | broadcast | bytes 1184256 | tf_op jit(solution)/shard_map/broadcast_in_dim | solution.py:26
  5.3 6.3 %broadcast_in_dim.15 = f32[2,1,9,128,128]{4,3,1,0,2:T(8,128)S(1)} reshape(f32[2,9,8,16,8,16]{5,4,3,2,0,1:T(8,128)} %broadcast_in_dim.14) | data formatting | bytes 2359296 | tf_op jit(solution)/shard_map/broadcast_in_dim | solution.py:26
  11.9 3.4 %collective-permute-start.4 = (f32[1,1,9,128,128]{4,3,1,0,2:T(8,128)S(1)}, f32[1,1,9,128,128]{4,3,1,0,2:T(8,128)S(1)}, u32[]{:S(2)}, u32[]{:S(2)}) collective-permute-start(f32[1,1,9,128,128]{4,3,1,0,2:T(8,128)S(1)} %get-tuple-element.765), channel_id=1, source_target_pairs={{0,16},{16,32},{32,48},{48,64},{64,80},{80,96},{96,112},{1,17},{17... | collective-permute-start | bytes 1769480 | tf_op jit(solution)/shard_map/ppermute | solution.py:14
  15.3 2.1 collective-permute-start.5
  17.4 4.7 %collective-permute-done.4 = f32[1,1,9,128,128]{4,3,1,0,2:T(8,128)S(1)} collective-permute-done((f32[1,1,9,128,128]{4,3,1,0,2:T(8,128)S(1)}, f32[1,1,9,128,128]{4,3,1,0,2:T(8,128)S(1)}, u32[]{:S(2)}, u32[]{:S(2)}) %collective-permute-start.4) | collective-permute-done | bytes 589856 | tf_op jit(solution)/shard_map/ppermute | solution.py:14
  22.1 4.5 %collective-permute-done.5 = f32[1,1,9,128,128]{4,3,1,0,2:T(8,128)S(1)} collective-permute-done((f32[1,1,9,128,128]{4,3,1,0,2:T(8,128)S(1)}, f32[1,1,9,128,128]{4,3,1,0,2:T(8,128)S(1)}, u32[]{:S(2)}, u32[]{:S(2)}) %collective-permute-start.5) | collective-permute-done | bytes 589856 | tf_op jit(solution)/shard_map/ppermute | solution.py:17
  26.7 1.7 pad_maximum_fusion.2
  28.3 4.9 %collective-permute-start.6 = (f32[4,1,9,128,128]{4,3,1,0,2:T(8,128)}, f32[4,1,9,128,128]{4,3,1,0,2:T(8,128)}, u32[]{:S(2)}, u32[]{:S(2)}) collective-permute-start(f32[4,1,9,128,128]{4,3,1,0,2:T(8,128)} %pad_maximum_fusion.2), channel_id=1, source_target_pairs={{0,1},{1,2},{2,3},{3,4},{4,5},{5,6},{6,7},{7,8},{8,9},{9,10},{10,1... | collective-permute-start | bytes 7077896 | tf_op jit(solution)/shard_map/ppermute | solution.py:14
  33.3 1.3 collective-permute-start.7
  34.7 2.0 collective-permute-start
  36.7 2.3 %collective-permute-start.1 = (f32[1,1,9,128,128]{4,3,2,1,0:T(8,128)S(1)}, f32[1,1,9,128,128]{4,3,2,1,0:T(8,128)S(1)}, u32[]{:S(2)}, u32[]{:S(2)}) collective-permute-start(f32[1,1,9,128,128]{4,3,2,1,0:T(8,128)S(1)} %get-tuple-element.767), channel_id=1, source_target_pairs={{16,0},{32,16},{48,32},{64,48},{80,64},{96,80},{112,96},{17,1},{33... | collective-permute-start | bytes 1769480 | tf_op jit(solution)/shard_map/ppermute | solution.py:17
  39.0 4.5 %collective-permute-done = f32[1,1,9,128,128]{4,3,2,1,0:T(8,128)S(1)} collective-permute-done((f32[1,1,9,128,128]{4,3,2,1,0:T(8,128)S(1)}, f32[1,1,9,128,128]{4,3,2,1,0:T(8,128)S(1)}, u32[]{:S(2)}, u32[]{:S(2)}) %collective-permute-start) | collective-permute-done | bytes 589856 | tf_op jit(solution)/shard_map/ppermute | solution.py:14
  44.4 1.1 constant_dynamic-update-slice_fusion.13
  45.5 2.8 %collective-permute-done.1 = f32[1,1,9,128,128]{4,3,2,1,0:T(8,128)S(1)} collective-permute-done((f32[1,1,9,128,128]{4,3,2,1,0:T(8,128)S(1)}, f32[1,1,9,128,128]{4,3,2,1,0:T(8,128)S(1)}, u32[]{:S(2)}, u32[]{:S(2)}) %collective-permute-start.1) | collective-permute-done | bytes 589856 | tf_op jit(solution)/shard_map/ppermute | solution.py:17
  49.2 5.7 %collective-permute-start.2 = (f32[4,1,9,128,128]{4,3,2,1,0:T(8,128)}, f32[4,1,9,128,128]{4,3,2,1,0:T(8,128)}, u32[]{:S(2)}, u32[]{:S(2)}) collective-permute-start(f32[4,1,9,128,128]{4,3,2,1,0:T(8,128)} %constant_dynamic-update-slice_fusion.12), channel_id=1, source_target_pairs={{0,1},{1,2},{2,3},{3,4},{4,5},{5,6},{6,7},{7,8},{8,9},{9,10},{10,1... | collective-permute-start | bytes 7077896 | tf_op jit(solution)/shard_map/ppermute | solution.py:14
  54.9 1.3 collective-permute-start.3
  57.3 25.9 %collective-permute-done.6 = f32[4,1,9,128,128]{4,3,1,0,2:T(8,128)} collective-permute-done((f32[4,1,9,128,128]{4,3,1,0,2:T(8,128)}, f32[4,1,9,128,128]{4,3,1,0,2:T(8,128)}, u32[]{:S(2)}, u32[]{:S(2)}) %collective-permute-start.6) | collective-permute-done | bytes 2359328 | tf_op jit(solution)/shard_map/ppermute | solution.py:14
  83.2 5.6 %collective-permute-done.7 = f32[4,1,9,128,128]{4,3,1,0,2:T(8,128)} collective-permute-done((f32[4,1,9,128,128]{4,3,1,0,2:T(8,128)}, f32[4,1,9,128,128]{4,3,1,0,2:T(8,128)}, u32[]{:S(2)}, u32[]{:S(2)}) %collective-permute-start.7) | collective-permute-done | bytes 2359328 | tf_op jit(solution)/shard_map/ppermute | solution.py:17
  88.7 5.2 %pad_maximum_fusion.1 = f32[4,3,9,128,128]{4,3,1,0,2:T(8,128)} fusion(f32[4,1,9,128,128]{4,3,1,0,2:T(8,128)} %collective-permute-done.7, f32[1,1,9,128,128]{4,3,1,0,2:T(8,128)S(1)} %collective-permute-done.5, f32[2,1,9,128,128]{4,3,1,0,2:T(8,128)S(1)} %copy_multiply_fusion, f32[1,1,9,128,128]{4,3,1,0,2:T(8,128)S(1)} %collective-permute-done.4, ...), kind=kLoop, calls=%fused_computation.1 | loop fusion | flops 7077888 | bytes 14155776 | tf_op jit(solution)/shard_map/concatenate | solution.py:18
  93.9 5.0 %slice_bitcast_fusion.1 = (f32[1,3,3,9,128,128]{5,4,2,1,0,3:T(8,128)S(1)}, f32[1,3,3,9,128,128]{5,4,2,1,0,3:T(8,128)S(1)}) fusion(f32[4,3,9,128,128]{4,3,1,0,2:T(8,128)} %pad_maximum_fusion.1), kind=kLoop, calls=%fused_computation.3 | loop fusion | bytes 21233664 | tf_op jit(solution)/shard_map/stack | solution.py:143
  99.0 1.0 maximum_bitcast_fusion.1
  100.0 1.4 maximum_bitcast_fusion.2
  101.4 1.4 fusion.129
  102.8 30.5 %collective-permute-done.2 = f32[4,1,9,128,128]{4,3,2,1,0:T(8,128)} collective-permute-done((f32[4,1,9,128,128]{4,3,2,1,0:T(8,128)}, f32[4,1,9,128,128]{4,3,2,1,0:T(8,128)}, u32[]{:S(2)}, u32[]{:S(2)}) %collective-permute-start.2) | collective-permute-done | bytes 2359328 | tf_op jit(solution)/shard_map/ppermute | solution.py:14
  133.3 5.6 %collective-permute-done.3 = f32[4,1,9,128,128]{4,3,2,1,0:T(8,128)} collective-permute-done((f32[4,1,9,128,128]{4,3,2,1,0:T(8,128)}, f32[4,1,9,128,128]{4,3,2,1,0:T(8,128)}, u32[]{:S(2)}, u32[]{:S(2)}) %collective-permute-start.3) | collective-permute-done | bytes 2359328 | tf_op jit(solution)/shard_map/ppermute | solution.py:17
  138.9 3.6 %pad_maximum_fusion = f32[4,3,9,128,128]{4,3,2,1,0:T(8,128)S(1)} fusion(f32[4,1,9,128,128]{4,3,2,1,0:T(8,128)} %collective-permute-done.3, f32[4,1,9,128,128]{4,3,2,1,0:T(8,128)} %constant_dynamic-update-slice_fusion.12, f32[4,1,9,128,128]{4,3,2,1,0:T(8,128)} %collective-permute-done.2), kind=kLoop, calls=%fused_computation | loop fusion | flops 3538944 | bytes 14155776 | tf_op jit(solution)/shard_map/concatenate | solution.py:18
  142.4 5.3 %slice_bitcast_fusion.3 = (f32[1,3,3,9,128,128]{5,4,0,3,2,1:T(8,128)}, f32[1,3,3,9,128,128]{5,4,0,3,2,1:T(8,128)}) fusion(f32[4,3,9,128,128]{4,3,2,1,0:T(8,128)S(1)} %pad_maximum_fusion), kind=kLoop, calls=%fused_computation.5 | loop fusion | bytes 21233664 | tf_op jit(solution)/shard_map/stack | solution.py:146
  147.8 1.4 maximum_bitcast_fusion.16
  149.5 0.9 copy-done.8
  151.6 0.9 fusion.6
  152.6 1.0 copy-done.7
  154.7 1.2 fusion.8
  155.9 1.4 fusion.5
  157.3 1.2 fusion.10
  158.5 1.8 fusion.85
  161.4 1.0 copy-done.5
  164.9 0.9 fusion.12
  166.6 1.2 fusion.14
  167.8 1.3 fusion.4
  169.1 1.2 fusion.16
  170.3 1.9 fusion.77
  175.3 0.9 fusion.18
  177.2 1.2 fusion.20
  178.3 1.3 fusion.3
  179.7 1.2 fusion.22
  180.9 1.8 fusion.69
  186.0 0.9 fusion.24
  187.7 1.2 fusion.26
  188.9 1.6 fusion.2
  190.4 1.2 fusion.28
  191.6 1.8 fusion.61
  196.8 0.9 fusion.30
  198.4 1.2 fusion.32
  199.6 1.3 fusion.1
  201.0 1.2 fusion.34
  202.2 1.8 fusion.53
  204.0 1.3 fusion.35
  207.7 0.9 fusion.36
  209.4 1.2 fusion.38
  210.6 1.4 fusion
  212.0 1.2 fusion.40
  213.1 1.8 fusion.45
  215.0 0.9 fusion.41
  217.2 1.9 multiply_add_fusion
  (110 shorter events, 26.7 us)
Async XLA Ops:
  5.3 6.3 %copy-start.10 = (f32[2,1,9,128,128]{4,3,2,1,0:T(8,128)S(1)}, f32[2,1,9,128,128]{4,3,2,1,0:T(8,128)}, u32[]{:S(2)}) copy-start(f32[2,1,9,128,128]{4,3,2,1,0:T(8,128)} %param.124) | copy-start | bytes 3538948
  11.9 10.2 %collective-permute-start.4 = (f32[1,1,9,128,128]{4,3,1,0,2:T(8,128)S(1)}, f32[1,1,9,128,128]{4,3,1,0,2:T(8,128)S(1)}, u32[]{:S(2)}, u32[]{:S(2)}) collective-permute-start(f32[1,1,9,128,128]{4,3,1,0,2:T(8,128)S(1)} %get-tuple-element.765), channel_id=1, source_target_pairs={{0,16},{16,32},{32,48},{48,64},{64,80},{80,96},{96,112},{1,17},{17... | collective-permute-start | bytes 1769480 | tf_op jit(solution)/shard_map/ppermute | solution.py:14
  15.3 19.3 %copy-start.9 = (f32[2,1,9,128,128]{4,3,2,1,0:T(8,128)S(1)}, f32[2,1,9,128,128]{4,3,2,1,0:T(8,128)}, u32[]{:S(2)}) copy-start(f32[2,1,9,128,128]{4,3,2,1,0:T(8,128)} %param.126) | copy-start | bytes 3538948
  15.3 11.3 %collective-permute-start.5 = (f32[1,1,9,128,128]{4,3,1,0,2:T(8,128)S(1)}, f32[1,1,9,128,128]{4,3,1,0,2:T(8,128)S(1)}, u32[]{:S(2)}, u32[]{:S(2)}) collective-permute-start(f32[1,1,9,128,128]{4,3,1,0,2:T(8,128)S(1)} %get-tuple-element.766), channel_id=1, source_target_pairs={{16,0},{32,16},{48,32},{64,48},{80,64},{96,80},{112,96},{17,1},{33... | collective-permute-start | bytes 1769480 | tf_op jit(solution)/shard_map/ppermute | solution.py:17
  28.3 54.8 %collective-permute-start.6 = (f32[4,1,9,128,128]{4,3,1,0,2:T(8,128)}, f32[4,1,9,128,128]{4,3,1,0,2:T(8,128)}, u32[]{:S(2)}, u32[]{:S(2)}) collective-permute-start(f32[4,1,9,128,128]{4,3,1,0,2:T(8,128)} %pad_maximum_fusion.2), channel_id=1, source_target_pairs={{0,1},{1,2},{2,3},{3,4},{4,5},{5,6},{6,7},{7,8},{8,9},{9,10},{10,1... | collective-permute-start | bytes 7077896 | tf_op jit(solution)/shard_map/ppermute | solution.py:14
  33.3 55.5 %collective-permute-start.7 = (f32[4,1,9,128,128]{4,3,1,0,2:T(8,128)}, f32[4,1,9,128,128]{4,3,1,0,2:T(8,128)}, u32[]{:S(2)}, u32[]{:S(2)}) collective-permute-start(f32[4,1,9,128,128]{4,3,1,0,2:T(8,128)} %pad_maximum_fusion.2), channel_id=1, source_target_pairs={{1,0},{2,1},{3,2},{4,3},{5,4},{6,5},{7,6},{8,7},{9,8},{10,9},{11,1... | collective-permute-start | bytes 7077896 | tf_op jit(solution)/shard_map/ppermute | solution.py:17
  34.7 8.8 %collective-permute-start = (f32[1,1,9,128,128]{4,3,2,1,0:T(8,128)S(1)}, f32[1,1,9,128,128]{4,3,2,1,0:T(8,128)S(1)}, u32[]{:S(2)}, u32[]{:S(2)}) collective-permute-start(f32[1,1,9,128,128]{4,3,2,1,0:T(8,128)S(1)} %get-tuple-element.768), channel_id=1, source_target_pairs={{0,16},{16,32},{32,48},{48,64},{64,80},{80,96},{96,112},{1,17},{17... | collective-permute-start | bytes 1769480 | tf_op jit(solution)/shard_map/ppermute | solution.py:14
  36.7 11.6 %collective-permute-start.1 = (f32[1,1,9,128,128]{4,3,2,1,0:T(8,128)S(1)}, f32[1,1,9,128,128]{4,3,2,1,0:T(8,128)S(1)}, u32[]{:S(2)}, u32[]{:S(2)}) collective-permute-start(f32[1,1,9,128,128]{4,3,2,1,0:T(8,128)S(1)} %get-tuple-element.767), channel_id=1, source_target_pairs={{16,0},{32,16},{48,32},{64,48},{80,64},{96,80},{112,96},{17,1},{33... | collective-permute-start | bytes 1769480 | tf_op jit(solution)/shard_map/ppermute | solution.py:17
  45.5 10.6 %copy-start.11 = (s32[2,1,8]{2,1,0:T(1,128)S(1)}, s32[2,1,8]{2,1,0:T(1,128)}, u32[]{:S(2)}) copy-start(s32[2,1,8]{2,1,0:T(1,128)} %param.127) | copy-start | bytes 196
  49.2 84.1 %collective-permute-start.2 = (f32[4,1,9,128,128]{4,3,2,1,0:T(8,128)}, f32[4,1,9,128,128]{4,3,2,1,0:T(8,128)}, u32[]{:S(2)}, u32[]{:S(2)}) collective-permute-start(f32[4,1,9,128,128]{4,3,2,1,0:T(8,128)} %constant_dynamic-update-slice_fusion.12), channel_id=1, source_target_pairs={{0,1},{1,2},{2,3},{3,4},{4,5},{5,6},{6,7},{7,8},{8,9},{9,10},{10,1... | collective-permute-start | bytes 7077896 | tf_op jit(solution)/shard_map/ppermute | solution.py:14
  54.9 84.0 %collective-permute-start.3 = (f32[4,1,9,128,128]{4,3,2,1,0:T(8,128)}, f32[4,1,9,128,128]{4,3,2,1,0:T(8,128)}, u32[]{:S(2)}, u32[]{:S(2)}) collective-permute-start(f32[4,1,9,128,128]{4,3,2,1,0:T(8,128)} %constant_dynamic-update-slice_fusion.12), channel_id=1, source_target_pairs={{1,0},{2,1},{3,2},{4,3},{5,4},{6,5},{7,6},{8,7},{9,8},{10,9},{11,1... | collective-permute-start | bytes 7077896 | tf_op jit(solution)/shard_map/ppermute | solution.py:17
  100.0 60.4 %copy-start = (f32[2,2,3,128,128]{4,3,2,1,0:T(8,128)}, f32[2,2,3,128,128]{4,3,2,1,0:T(8,128)S(1)}, u32[]{:S(2)}) copy-start(f32[2,2,3,128,128]{4,3,2,1,0:T(8,128)S(1)} %get-tuple-element.746) | copy-start | bytes 2359300
  149.4 1.0 copy-start.8
  150.5 1.1 copy-start.4
  152.5 1.0 copy-start.7
  153.6 1.1 copy-start.3
  155.9 1.4 copy-start.2
  157.3 1.2 copy-start.6
  161.3 1.0 copy-start.5
  170.3 1.9 copy-start.1
where the time goes:
time: 223 us; the launch traced here: 219 us
  waiting for transfers between devices  84.1 us (38%)
  matrix products  57.9 us (26%)
  local copies, waits for them, and re-layouts  30.6 us (14%)
  starting transfers between devices  22.9 us (10%)
  other arithmetic  22.1 us (10%)
    ppermute x4, waiting for transfers between devices, with_halo(): lax.ppermute(lax.slice_in_dim(block, block.shape[dim] - width, None, axis...  65.6 us
    dot_general x54, matrix products, cluster_apply(): jnp.einsum('...xyij,...xyjc->...xyic', coupled, source, precision=lax.Pre...  57.9 us
    ppermute x4, waiting for transfers between devices, with_halo(): lax.ppermute(lax.slice_in_dim(block, 0, width, axis=dim), axis, backward)  18.5 us
    ppermute x4, starting transfers between devices, with_halo(): lax.ppermute(lax.slice_in_dim(block, block.shape[dim] - width, None, axis...  16 us
    broadcast_in_dim x3, local copies, waits for them, and re-layouts, expand_mask(): jnp.broadcast_to(shaped, leading + (atom_count, orbitals, atom_count, orb...  10.8 us
    concatenate x3, other arithmetic, with_halo(): block = jnp.concatenate([low, block, high], axis=dim)  10.4 us
    ppermute x4, starting transfers between devices, with_halo(): lax.ppermute(lax.slice_in_dim(block, 0, width, axis=dim), axis, backward)  6.91 us
    unnamed x34, local copies, waits for them, and re-layouts  6.41 us
  transfers between devices with their start and end apart: 8, of which 8 were waited for; matrix products, arithmetic and copies ran while one was open for 8% of the time, Pallas kernels for 0%

commit v1 on v0

v1 whole, which is shorter than its diff:
```python
import jax
import jax.numpy as jnp
from jax import lax
from jax.experimental import pallas as pl
from jax.experimental.pallas import tpu as pltpu
from jax.sharding import PartitionSpec as P

ITERS = 3
B = 128
POWERS = 2 * ITERS + 1
F32 = jnp.float32
BF16 = jnp.bfloat16


def off(u, v):
    return 3 * (u + 1) + (v + 1)


def edge_list(v):
    low, high = min(0, v), max(0, v)
    first = []
    for row, us in ((0, (-1, 0)), (1, (0, 1))):
        first += [(row, True, off(u, w)) for u in us for w in (low, high)]
        first.append((row, False, off(-1 if row == 0 else 1, v)))
    second = []
    for row, u in ((0, 1), (1, -1)):
        second += [(row, True, off(u, w)) for w in (low, high)]
        second += [(row, False, off(0, v)), (row, False, off(u, v))]
    return first, second


def own_list(u):
    row, us = (1, (0, 1)) if u > 0 else (0, (-1, 0))
    return [(row, True, off(w, v)) for w in us for v in (-1, 0, 1)] + [(row, False, off(u, 0))]


FIRST = {v: edge_list(v)[0] for v in (1, -1)}
SECOND = {v: edge_list(v)[1] for v in (1, -1)}
OWN = {u: own_list(u) for u in (1, -1)}


def pack_kernel(blocks, mask, rhs, sap, sam, sbp, sbm, oxp, oxm, own):
    atoms = mask.shape[-1]
    orbitals = B // atoms
    lane_atom = lax.broadcasted_iota(jnp.int32, (atoms, B), 1) // orbitals
    atom = lax.broadcasted_iota(jnp.int32, (atoms, B), 0)
    spread = (lane_atom == atom).astype(BF16)
    flat = mask[...].reshape(18 * atoms, atoms).astype(F32).astype(BF16)
    wide = jnp.dot(flat, spread, preferred_element_type=F32)
    masked = {}
    for row in range(2):
        for o in range(9):
            start = (row * 9 + o) * atoms
            rows = [
                jnp.broadcast_to(wide[start + a : start + a + 1, :], (orbitals, B))
                for a in range(atoms)
            ]
            own[row, o] = blocks[row, 0, o] * jnp.concatenate(rows, axis=0)
    for ref, entries in (
        (sap, FIRST[1]),
        (sam, FIRST[-1]),
        (sbp, SECOND[1]),
        (sbm, SECOND[-1]),
        (oxp, OWN[1]),
        (oxm, OWN[-1]),
    ):
        for place, (row, is_coupling, o) in enumerate(entries):
            ref[place] = own[row, o] if is_coupling else rhs[row, 0, o]


def pack(blocks, mask, rhs):
    shapes = [10, 10, 8, 8, 7, 7]
    out = [jax.ShapeDtypeStruct((n, B, B), F32) for n in shapes]
    out.append(jax.ShapeDtypeStruct((2, 9, B, B), F32))
    return pl.pallas_call(
        pack_kernel,
        out_shape=out,
        in_specs=[pl.BlockSpec(memory_space=pltpu.VMEM)] * 3,
        out_specs=[pl.BlockSpec(memory_space=pltpu.VMEM)] * 7,
        compiler_params=pltpu.CompilerParams(vmem_limit_bytes=32 * 2**20),
        name="pack",
    )(blocks, mask, rhs)


def split(value):
    high = value.astype(BF16)
    low = (value - high.astype(F32)).astype(BF16)
    return high, low


def guarded(top, bottom, floor_val):
    return top * bottom / (bottom * bottom + floor_val * floor_val)


def poly_add(left, scale, right):
    out = []
    for i in range(max(len(left), len(right))):
        if i >= len(right):
            out.append(left[i])
        elif i >= len(left):
            out.append(scale * right[i])
        else:
            out.append(left[i] + scale * right[i])
    return out


def poly_apply(p):
    return poly_add(list(p), -1.0, [jnp.zeros_like(p[0])] + list(p))


def poly_first(gram, p):
    total = p[0] * gram[0][0]
    for i in range(1, len(p)):
        total = total + p[i] * gram[0][i]
    return total


def poly_norm(gram, p):
    total = 0.0
    for i in range(len(p)):
        inner = p[i] * gram[i][i]
        for j in range(i):
            inner = inner + 2.0 * (p[j] * gram[j][i])
        total = total + p[i] * inner
    return total


def tfqmr(gram, limits):
    one = jnp.ones_like(limits)
    zero = jnp.zeros_like(limits)
    norm = gram[0][0]
    w = [one]
    y1 = [one]
    u1 = poly_apply(y1)
    v = u1
    d = [zero]
    x = [zero]
    rho, floor_val, tau = norm, 0.1 * norm, jnp.sqrt(norm)
    theta = zero
    eta = zero
    y2 = None
    u2 = None
    ww = norm
    for iteration in range(ITERS):
        if iteration > 0:
            rho_next = poly_first(gram, w)
            beta = guarded(rho_next, rho, floor_val)
            floor_val = 0.1 * jnp.sqrt(norm * ww)
            rho = rho_next
            y1 = poly_add(w, beta, y2)
            u1 = poly_apply(y1)
            v = poly_add(u1, beta, poly_add(u2, beta, v))
        alpha_floor = 0.1 * jnp.sqrt(norm * (poly_norm(gram, v) + 1e-06))
        alpha = guarded(rho, poly_first(gram, v), alpha_floor)
        ratio = guarded(1.0, alpha, 0.1)
        y2 = poly_add(y1, -alpha, v)
        u2 = poly_apply(y2)
        active = (limits > iteration).astype(F32)
        for y, u in ((y1, u1), (y2, u2)):
            w = poly_add(w, -alpha, u)
            d = poly_add(y, theta * theta * eta * ratio, d)
            ww = poly_norm(gram, w)
            theta = jnp.sqrt(ww) / tau
            cosine = 1.0 / jnp.sqrt(1.0 + theta * theta)
            tau = tau * theta * cosine
            eta = cosine * cosine * alpha
            x = poly_add(x, active * eta, d)
    return x


def column_range(c):
    return (0, 2) if c == 0 else (0, 3) if c == 1 else (1, 3)


def solve_kernel(
    rap, ram, rbp, rbm, rxp, rxm, fxp, fxm, own, rhs, limits, out, wh, wl, vv, powers, gram_ref
):
    def put_coupling(h, c, o, value):
        high, low = split(value)
        wh[h, c, :, o * B : (o + 1) * B] = high
        wl[h, c, :, o * B : (o + 1) * B] = low

    def put_vector(slot, parity, g, r, c, value):
        high, low = split(value)
        start = ((g + r) * 3 + c) * B
        vv[parity, start : start + B, g * B : (g + 1) * B] = high
        vv[parity, start : start + B, (2 + g) * B : (3 + g) * B] = low
        powers[slot, g, (3 * r + c) * B : (3 * r + c + 1) * B, :] = value

    def put_rhs(h, c, o, value):
        r = 1 - (o // 3 - 1)
        g = h - r
        put_vector(0, 0, g, r, c, value)

    for v, ref_a, ref_b in ((1, rap, rbp), (-1, ram, rbm)):
        c = 1 - v
        for ref, entries in ((ref_a, FIRST[v]), (ref_b, SECOND[v])):
            for place, (row, is_coupling, o) in enumerate(entries):
                if is_coupling:
                    put_coupling(row + 1, c, o, ref[place])
                elif 0 <= row + (o // 3 - 1) <= 1:
                    put_rhs(row + 1, c, o, ref[place])
    for u, ref, fref in ((1, rxp, fxp), (-1, rxm, fxm)):
        h = 0 if u > 0 else 3
        for place, (row, is_coupling, o) in enumerate(OWN[u]):
            if is_coupling:
                put_coupling(h, 1, o, ref[place])
            else:
                put_rhs(h, 1, o, ref[place])
        part = 5 if u > 0 else 0
        for side, v in ((0, 1), (1, -1)):
            for place in range(5):
                row, is_coupling, o = FIRST[v][part + place]
                if is_coupling:
                    put_coupling(h, 1 - v, o, fref[side * 5 + place])
                else:
                    put_rhs(h, 1 - v, o, fref[side * 5 + place])
    for row in range(2):
        for o in range(9):
            put_coupling(row + 1, 1, o, own[row, o])
    for row, u in ((0, 0), (1, 0), (0, 1), (1, -1)):
        put_rhs(row + 1, 1, off(u, 0), rhs[row, 0, off(u, 0)])

    def dot(left, right):
        return jnp.dot(left, right, preferred_element_type=F32)

    def piece(h, c, source_low, source_high, parity, lanes):
        c_low, c_high = column_range(c)
        runs = []
        if c == 1:
            runs.append((source_low * 3, off(source_low - h, -1), 3 * (source_high - source_low)))
        else:
            for source in range(source_low, source_high):
                runs.append((source * 3 + c_low, off(source - h, c_low - c), 2))
        both = None
        for member, o, count in runs:
            left_h = wh[h, c, :, o * B : (o + count) * B]
            left_l = wl[h, c, :, o * B : (o + count) * B]
            rows = slice(member * B, (member + count) * B)
            if lanes is None:
                high = dot(left_h, vv[parity, rows, :])
                low = dot(left_l, vv[parity, rows, : 2 * B])
                term = (
                    high[:, :B] + (high[:, 2 * B : 3 * B] + low[:, :B]),
                    high[:, B : 2 * B] + (high[:, 3 * B :] + low[:, B:]),
                )
            else:
                g = lanes
                right_h = vv[parity, rows, g * B : (g + 1) * B]
                right_l = vv[parity, rows, (2 + g) * B : (3 + g) * B]
                high = dot(left_h, jnp.concatenate([right_h, right_l], axis=1))
                low = dot(left_l, right_h)
                term = (high[:, :B] + (high[:, B:] + low),)
            both = term if both is None else tuple(a + b for a, b in zip(both, term))
        return both

    def apply(slot, parity):
        for c in range(3):
            for h in (1, 2):
                shared = piece(h, c, 1, 3, parity, None)
                g = h - 1
                extra = piece(h, c, 0, 1, parity, 0) if h == 1 else piece(h, c, 3, 4, parity, 1)
                values = [shared[0], shared[1]]
                values[g] = values[g] + extra[0]
                for group in range(2):
                    put_vector(slot + 1, 1 - parity, group, h - group, c, values[group])
            put_vector(slot + 1, 1 - parity, 0, 0, c, piece(0, c, 0, 2, parity, 0)[0])
            put_vector(slot + 1, 1 - parity, 1, 2, c, piece(3, c, 2, 4, parity, 1)[0])

    def grams(slot):
        for g in range(2):
            totals = [None] * POWERS
            for m in range(9):
                rows = slice(m * B, (m + 1) * B)
                here = powers[slot, g, rows, :]
                for i in range(POWERS):
                    term = jnp.sum((here * powers[i, g, rows, :]).reshape(16, 8, B), axis=0)
                    totals[i] = term if totals[i] is None else totals[i] + term
            for i in range(POWERS):
                gram_ref[slot, i, g] = totals[i]

    def body(slot, carry):
        grams(slot)
        apply(slot, lax.rem(slot, 2))
        return carry

    lax.fori_loop(0, POWERS - 1, body, 0)
    grams(POWERS - 1)
    gram = [
        [
            jnp.concatenate(
                [jnp.sum(gram_ref[max(i, j), min(i, j), g], axis=0, keepdims=True) for g in range(2)],
                axis=0,
            )
            for j in range(POWERS)
        ]
        for i in range(POWERS)
    ]
    x = tfqmr(gram, limits[...])
    for g in range(2):
        for m in range(9):
            rows = slice(m * B, (m + 1) * B)
            total = x[0][g : g + 1, :] * powers[0, g, rows, :]
            for i in range(1, len(x)):
                total = total + x[i][g : g + 1, :] * powers[i, g, rows, :]
            out[g, 0, m] = total


def solve(*arrays):
    return pl.pallas_call(
        solve_kernel,
        out_shape=jax.ShapeDtypeStruct((2, 1, 9, B, B), F32),
        in_specs=[pl.BlockSpec(memory_space=pltpu.VMEM)] * len(arrays),
        out_specs=pl.BlockSpec(memory_space=pltpu.VMEM),
        scratch_shapes=[
            pltpu.VMEM((4, 3, B, 9 * B), BF16),
            pltpu.VMEM((4, 3, B, 9 * B), BF16),
            pltpu.VMEM((2, 12 * B, 4 * B), BF16),
            pltpu.VMEM((POWERS, 2, 9 * B, B), F32),
            pltpu.VMEM((POWERS, POWERS, 2, 8, B), F32),
        ],
        compiler_params=pltpu.CompilerParams(vmem_limit_bytes=32 * 2**20),
        name="solve",
    )(*arrays)


def shift(value, axis, step):
    count = lax.axis_size(axis)
    if step > 0:
        pairs = [(i, i + 1) for i in range(count - 1)]
    else:
        pairs = [(i + 1, i) for i in range(count - 1)]
    return lax.ppermute(value, axis, pairs)


def shards(blocks, pair_mask, rhs_rows, counts):
    sap, sam, sbp, sbm, oxp, oxm, own = pack(blocks, pair_mask, rhs_rows)
    rap = shift(sap, "gy", 1)
    ram = shift(sam, "gy", -1)
    rxp = shift(oxp, "gx", 1)
    rxm = shift(oxm, "gx", -1)
    rbp = shift(sbp, "gy", 1)
    rbm = shift(sbm, "gy", -1)
    fxp = shift(jnp.concatenate([rap[5:], ram[5:]], axis=0), "gx", 1)
    fxm = shift(jnp.concatenate([rap[:5], ram[:5]], axis=0), "gx", -1)
    orbitals = B // pair_mask.shape[-1]
    limits = jnp.repeat(counts, orbitals, axis=-1).reshape(2, B).astype(F32)
    return solve(rap, ram, rbp, rbm, rxp, rxm, fxp, fxm, own, rhs_rows, limits)


def solution(mesh):
    return jax.shard_map(
        shards,
        mesh=mesh,
        in_specs=(
            P("gx", "gy", None, None, None),
            P("gx", "gy", None, None, None),
            P("gx", "gy", None, None, None),
            P("gx", "gy", None),
        ),
        out_specs=P("gx", "gy", None, None, None),
        check_vma=False,
    )
```

time: 223 us -> 83.6 us (0.37)
  the two profiles are of different devices: /device:TPU:5 before, /device:TPU:1 now
where the time goes in v1:
time: 83.6 us; the launch traced here: 82.1 us
  Pallas kernels  27.4 us (33%)
  starting transfers between devices  23.6 us (28%)
  waiting for transfers between devices  22.3 us (27%)
  local copies, waits for them, and re-layouts  6.88 us (8%)
  other arithmetic  1.8 us (2%)
    pallas_call x1, Pallas kernels, solve(): pl.pallas_call(solve_kernel, out_shape=jax.ShapeDtypeStruct((2, 1, 9, B,...  25.9 us
    ppermute x8, starting transfers between devices, shift(): return lax.ppermute(value, axis, pairs)  23.6 us
    ppermute x8, waiting for transfers between devices, shift(): return lax.ppermute(value, axis, pairs)  22.3 us
    unnamed x17, local copies, waits for them, and re-layouts  6.64 us
  transfers between devices with their start and end apart: 8, of which 4 were waited for; matrix products, arithmetic and copies ran while one was open for 2% of the time, Pallas kernels for 0%

profile of v1, /device:TPU:1, one launch (start us, length us, event | category | flops | bytes accessed | tf_op | source)
XLA Modules:
  0.0 82.1 jit_solution(15351325550614012505)
XLA Ops:
  0.0 1.0 %copy.5.mask = s32[2,1,9,8,8]{4,3,2,1,0:T(8,128)S(1)} copy(s32[2,1,9,8,8]{2,4,3,1,0:T(8,128)} %param.5) | data formatting | bytes 9216 | tf_op args[1]
  1.0 0.0 copy-start
  1.0 1.3 %copy-done = f32[2,1,9,128,128]{4,3,2,1,0:T(8,128)S(1)} copy-done((f32[2,1,9,128,128]{4,3,2,1,0:T(8,128)S(1)}, f32[2,1,9,128,128]{4,3,2,1,0:T(8,128)}, u32[]{:S(2)}) %copy-start) | copy-done | bytes 1179672
  2.3 0.0 copy-start.2
  2.3 1.3 %copy-done.2 = f32[2,1,9,128,128]{4,3,2,1,0:T(8,128)S(1)} copy-done((f32[2,1,9,128,128]{4,3,2,1,0:T(8,128)S(1)}, f32[2,1,9,128,128]{4,3,2,1,0:T(8,128)}, u32[]{:S(2)}) %copy-start.2) | copy-done | bytes 1179672
  3.6 1.5 %pack.1 = (f32[10,128,128]{2,1,0:T(8,128)S(1)}, f32[10,128,128]{2,1,0:T(8,128)S(1)}, f32[8,128,128]{2,1,0:T(8,128)}, f32[8,128,128]{2,1,0:T(8,128)}, f32[7,128,1...) custom-call(f32[2,1,9,128,128]{4,3,2,1,0:T(8,128)S(1)} %copy-done.2, ...), custom_call_target="tpu_custom_call" | custom-call | tf_op jit(solution)/shard_map/pack/pallas_call | solution.py:75
  5.1 0.0 copy-start.3
  5.1 4.4 %collective-permute-start = (f32[10,128,128]{2,1,0:T(8,128)S(1)}, f32[10,128,128]{2,1,0:T(8,128)S(1)}, u32[]{:S(2)}, u32[]{:S(2)}) collective-permute-start(f32[10,128,128]{2,1,0:T(8,128)S(1)} %get-tuple-element.12), channel_id=1, source_target_pairs={{0,1},{1,2},{2,3},{3,4},{4,5},{5,6},{6,7},{7,8},{8,9},{9,10},{10,1... | collective-permute-start | bytes 1966088 | tf_op jit(solution)/shard_map/ppermute | solution.py:333
  9.5 1.3 %collective-permute-start.1 = (f32[10,128,128]{2,1,0:T(8,128)S(1)}, f32[10,128,128]{2,1,0:T(8,128)S(1)}, u32[]{:S(2)}, u32[]{:S(2)}) collective-permute-start(f32[10,128,128]{2,1,0:T(8,128)S(1)} %get-tuple-element.13), channel_id=1, source_target_pairs={{1,0},{2,1},{3,2},{4,3},{5,4},{6,5},{7,6},{8,7},{9,8},{10,9},{11,1... | collective-permute-start | bytes 1966088 | tf_op jit(solution)/shard_map/ppermute | solution.py:333
  10.8 4.0 %collective-permute-start.4 = (f32[7,128,128]{2,1,0:T(8,128)S(1)}, f32[7,128,128]{2,1,0:T(8,128)S(1)}, u32[]{:S(2)}, u32[]{:S(2)}) collective-permute-start(f32[7,128,128]{2,1,0:T(8,128)S(1)} %get-tuple-element.16), channel_id=1, source_target_pairs={{0,16},{16,32},{32,48},{48,64},{64,80},{80,96},{96,112},{1,17},{17... | collective-permute-start | bytes 1376264 | tf_op jit(solution)/shard_map/ppermute | solution.py:333
  14.8 8.1 %collective-permute-done.rap = f32[10,128,128]{2,1,0:T(8,128)S(1)} collective-permute-done((f32[10,128,128]{2,1,0:T(8,128)S(1)}, f32[10,128,128]{2,1,0:T(8,128)S(1)}, u32[]{:S(2)}, u32[]{:S(2)}) %collective-permute-start) | collective-permute-done | bytes 655392 | tf_op jit(solution)/shard_map/ppermute | solution.py:333
  22.9 4.1 %collective-permute-done.1.ram = f32[10,128,128]{2,1,0:T(8,128)S(1)} collective-permute-done((f32[10,128,128]{2,1,0:T(8,128)S(1)}, f32[10,128,128]{2,1,0:T(8,128)S(1)}, u32[]{:S(2)}, u32[]{:S(2)}) %collective-permute-start.1) | collective-permute-done | bytes 655392 | tf_op jit(solution)/shard_map/ppermute | solution.py:333
  27.0 0.0 copy-done.3
  27.0 0.0 copy-start.7
  27.0 0.0 copy-start.1
  27.1 0.9 %pad_maximum_fusion = f32[10,128,128]{2,1,0:T(8,128)} fusion(f32[5,128,128]{2,1,0:T(8,128)S(1)} %get-tuple-element.22, f32[5,128,128]{2,1,0:T(8,128)S(1)} %get-tuple-element.20), kind=kLoop, calls=%fused_computation | loop fusion | flops 163840 | bytes 1310720 | tf_op jit(solution)/shard_map/concatenate | solution.py:344
  28.0 4.7 %collective-permute-start.6 = (f32[10,128,128]{2,1,0:T(8,128)}, f32[10,128,128]{2,1,0:T(8,128)S(1)}, u32[]{:S(2)}, u32[]{:S(2)}) collective-permute-start(f32[10,128,128]{2,1,0:T(8,128)} %pad_maximum_fusion), channel_id=1, source_target_pairs={{0,16},{16,32},{32,48},{48,64},{64,80},{80,96},{96,112},{1,17},{17... | collective-permute-start | bytes 1966088 | tf_op jit(solution)/shard_map/ppermute | solution.py:333
  32.7 0.9 %pad_maximum_fusion.1 = f32[10,128,128]{2,1,0:T(8,128)} fusion(f32[5,128,128]{2,1,0:T(8,128)S(1)} %get-tuple-element.21, f32[5,128,128]{2,1,0:T(8,128)S(1)} %get-tuple-element.19), kind=kLoop, calls=%fused_computation.1 | loop fusion | flops 163840 | bytes 1310720 | tf_op jit(solution)/shard_map/concatenate | solution.py:345
  33.6 1.9 %collective-permute-start.7 = (f32[10,128,128]{2,1,0:T(8,128)}, f32[10,128,128]{2,1,0:T(8,128)}, u32[]{:S(2)}, u32[]{:S(2)}) collective-permute-start(f32[10,128,128]{2,1,0:T(8,128)} %pad_maximum_fusion.1), channel_id=1, source_target_pairs={{16,0},{32,16},{48,32},{64,48},{80,64},{96,80},{112,96},{17,1},{33... | collective-permute-start | bytes 1966088 | tf_op jit(solution)/shard_map/ppermute | solution.py:333
  35.5 4.2 %collective-permute-start.2 = (f32[8,128,128]{2,1,0:T(8,128)}, f32[8,128,128]{2,1,0:T(8,128)}, u32[]{:S(2)}, u32[]{:S(2)}) collective-permute-start(f32[8,128,128]{2,1,0:T(8,128)} %get-tuple-element.14), channel_id=1, source_target_pairs={{0,1},{1,2},{2,3},{3,4},{4,5},{5,6},{6,7},{7,8},{8,9},{9,10},{10,1... | collective-permute-start | bytes 1572872 | tf_op jit(solution)/shard_map/ppermute | solution.py:333
  39.6 1.3 %collective-permute-start.3 = (f32[8,128,128]{2,1,0:T(8,128)}, f32[8,128,128]{2,1,0:T(8,128)}, u32[]{:S(2)}, u32[]{:S(2)}) collective-permute-start(f32[8,128,128]{2,1,0:T(8,128)} %get-tuple-element.15), channel_id=1, source_target_pairs={{1,0},{2,1},{3,2},{4,3},{5,4},{6,5},{7,6},{8,7},{9,8},{10,9},{11,1... | collective-permute-start | bytes 1572872 | tf_op jit(solution)/shard_map/ppermute | solution.py:333
  40.9 0.0 collective-permute-done.4.rxp
  40.9 0.0 copy-start.5
  41.0 0.8 copy-done.5
  41.7 1.9 %collective-permute-start.5 = (f32[7,128,128]{2,1,0:T(8,128)}, f32[7,128,128]{2,1,0:T(8,128)}, u32[]{:S(2)}, u32[]{:S(2)}) collective-permute-start(f32[7,128,128]{2,1,0:T(8,128)} %get-tuple-element.17), channel_id=1, source_target_pairs={{16,0},{32,16},{48,32},{64,48},{80,64},{96,80},{112,96},{17,1},{33... | collective-permute-start | bytes 1376264 | tf_op jit(solution)/shard_map/ppermute | solution.py:333
  43.7 0.0 copy-done.7
  43.7 0.1 broadcast_in_dim.3
  43.7 0.1 convert_element_type.9.limits
  43.8 8.6 %collective-permute-done.5.rxm = f32[7,128,128]{2,1,0:T(8,128)} collective-permute-done((f32[7,128,128]{2,1,0:T(8,128)}, f32[7,128,128]{2,1,0:T(8,128)}, u32[]{:S(2)}, u32[]{:S(2)}) %collective-permute-start.5) | collective-permute-done | bytes 458784 | tf_op jit(solution)/shard_map/ppermute | solution.py:333
  52.4 0.0 collective-permute-done.2.rbp
  52.4 1.5 %collective-permute-done.3.rbm = f32[8,128,128]{2,1,0:T(8,128)} collective-permute-done((f32[8,128,128]{2,1,0:T(8,128)}, f32[8,128,128]{2,1,0:T(8,128)}, u32[]{:S(2)}, u32[]{:S(2)}) %collective-permute-start.3) | collective-permute-done | bytes 524320 | tf_op jit(solution)/shard_map/ppermute | solution.py:333
  53.9 0.0 collective-permute-done.6.fxp
  53.9 0.0 collective-permute-done.7.fxm
  53.9 0.0 copy-done.1
  53.9 0.0 copy-start.4
  54.0 1.3 %copy-done.4 = f32[2,9,128,128]{3,2,1,0:T(8,128)S(1)} copy-done((f32[2,9,128,128]{3,2,1,0:T(8,128)S(1)}, f32[2,9,128,128]{3,2,1,0:T(8,128)}, u32[]{:S(2)}) %copy-start.4) | copy-done | bytes 1179672
  55.2 0.0 copy-start.6
  55.2 1.0 %copy-done.6 = f32[7,128,128]{2,1,0:T(8,128)S(1)} copy-done((f32[7,128,128]{2,1,0:T(8,128)S(1)}, f32[7,128,128]{2,1,0:T(8,128)}, u32[]{:S(2)}) %copy-start.6) | copy-done | bytes 458776
  56.2 25.9 %solve.1 = f32[2,1,9,128,128]{4,3,2,1,0:T(8,128)} custom-call(f32[10,128,128]{2,1,0:T(8,128)S(1)} %collective-permute-done.rap, f32[10,128,128]{2,1,0:T(8,128)S(1)} %collective-permute-done.1.ram, f32[8,128,128]{2,1,0:T(8,128)} %collective-permute-done.2.rbp, f32[8,128,128]{2,1,0:T(8,128)} %collective-permute-done.3.rbm, f32[7,128,128]{2,1,0:T(8,128)S(1)} %copy-done.6, ...), custom_call_target="tpu_custom_call" | custom-call | tf_op jit(solution)/shard_map/solve/pallas_call | solution.py:310
  (3 shorter events, 0.1 us)
Async XLA Ops:
  1.0 1.3 %copy-start = (f32[2,1,9,128,128]{4,3,2,1,0:T(8,128)S(1)}, f32[2,1,9,128,128]{4,3,2,1,0:T(8,128)}, u32[]{:S(2)}) copy-start(f32[2,1,9,128,128]{4,3,2,1,0:T(8,128)} %rhs.3) | copy-start | bytes 3538948
  2.3 1.3 %copy-start.2 = (f32[2,1,9,128,128]{4,3,2,1,0:T(8,128)S(1)}, f32[2,1,9,128,128]{4,3,2,1,0:T(8,128)}, u32[]{:S(2)}) copy-start(f32[2,1,9,128,128]{4,3,2,1,0:T(8,128)} %blocks.1) | copy-start | bytes 3538948
  5.1 21.9 %copy-start.3 = (f32[2,9,128,128]{3,2,1,0:T(8,128)}, f32[2,9,128,128]{3,2,1,0:T(8,128)S(1)}, u32[]{:S(2)}) copy-start(f32[2,9,128,128]{3,2,1,0:T(8,128)S(1)} %get-tuple-element.18.own) | copy-start | bytes 3538948
  5.1 17.7 %collective-permute-start = (f32[10,128,128]{2,1,0:T(8,128)S(1)}, f32[10,128,128]{2,1,0:T(8,128)S(1)}, u32[]{:S(2)}, u32[]{:S(2)}) collective-permute-start(f32[10,128,128]{2,1,0:T(8,128)S(1)} %get-tuple-element.12), channel_id=1, source_target_pairs={{0,1},{1,2},{2,3},{3,4},{4,5},{5,6},{6,7},{7,8},{8,9},{9,10},{10,1... | collective-permute-start | bytes 1966088 | tf_op jit(solution)/shard_map/ppermute | solution.py:333
  9.5 17.5 %collective-permute-start.1 = (f32[10,128,128]{2,1,0:T(8,128)S(1)}, f32[10,128,128]{2,1,0:T(8,128)S(1)}, u32[]{:S(2)}, u32[]{:S(2)}) collective-permute-start(f32[10,128,128]{2,1,0:T(8,128)S(1)} %get-tuple-element.13), channel_id=1, source_target_pairs={{1,0},{2,1},{3,2},{4,3},{5,4},{6,5},{7,6},{8,7},{9,8},{10,9},{11,1... | collective-permute-start | bytes 1966088 | tf_op jit(solution)/shard_map/ppermute | solution.py:333
  10.8 30.1 %collective-permute-start.4 = (f32[7,128,128]{2,1,0:T(8,128)S(1)}, f32[7,128,128]{2,1,0:T(8,128)S(1)}, u32[]{:S(2)}, u32[]{:S(2)}) collective-permute-start(f32[7,128,128]{2,1,0:T(8,128)S(1)} %get-tuple-element.16), channel_id=1, source_target_pairs={{0,16},{16,32},{32,48},{48,64},{64,80},{80,96},{96,112},{1,17},{17... | collective-permute-start | bytes 1376264 | tf_op jit(solution)/shard_map/ppermute | solution.py:333
  27.0 16.6 %copy-start.7 = (s32[2,1,8]{2,1,0:T(1,128)S(1)}, s32[2,1,8]{2,1,0:T(1,128)}, u32[]{:S(2)}) copy-start(s32[2,1,8]{2,1,0:T(1,128)} %param.7) | copy-start | bytes 196
  27.0 26.9 %copy-start.1 = (f32[2,1,9,128,128]{4,3,2,1,0:T(8,128)S(1)}, f32[2,1,9,128,128]{4,3,2,1,0:T(8,128)}, u32[]{:S(2)}) copy-start(f32[2,1,9,128,128]{4,3,2,1,0:T(8,128)} %rhs.3) | copy-start | bytes 3538948
  28.0 26.0 %collective-permute-start.6 = (f32[10,128,128]{2,1,0:T(8,128)}, f32[10,128,128]{2,1,0:T(8,128)S(1)}, u32[]{:S(2)}, u32[]{:S(2)}) collective-permute-start(f32[10,128,128]{2,1,0:T(8,128)} %pad_maximum_fusion), channel_id=1, source_target_pairs={{0,16},{16,32},{32,48},{48,64},{64,80},{80,96},{96,112},{1,17},{17... | collective-permute-start | bytes 1966088 | tf_op jit(solution)/shard_map/ppermute | solution.py:333
  33.6 20.4 %collective-permute-start.7 = (f32[10,128,128]{2,1,0:T(8,128)}, f32[10,128,128]{2,1,0:T(8,128)}, u32[]{:S(2)}, u32[]{:S(2)}) collective-permute-start(f32[10,128,128]{2,1,0:T(8,128)} %pad_maximum_fusion.1), channel_id=1, source_target_pairs={{16,0},{32,16},{48,32},{64,48},{80,64},{96,80},{112,96},{17,1},{33... | collective-permute-start | bytes 1966088 | tf_op jit(solution)/shard_map/ppermute | solution.py:333
  35.5 16.9 %collective-permute-start.2 = (f32[8,128,128]{2,1,0:T(8,128)}, f32[8,128,128]{2,1,0:T(8,128)}, u32[]{:S(2)}, u32[]{:S(2)}) collective-permute-start(f32[8,128,128]{2,1,0:T(8,128)} %get-tuple-element.14), channel_id=1, source_target_pairs={{0,1},{1,2},{2,3},{3,4},{4,5},{5,6},{6,7},{7,8},{8,9},{9,10},{10,1... | collective-permute-start | bytes 1572872 | tf_op jit(solution)/shard_map/ppermute | solution.py:333
  39.6 14.3 %collective-permute-start.3 = (f32[8,128,128]{2,1,0:T(8,128)}, f32[8,128,128]{2,1,0:T(8,128)}, u32[]{:S(2)}, u32[]{:S(2)}) collective-permute-start(f32[8,128,128]{2,1,0:T(8,128)} %get-tuple-element.15), channel_id=1, source_target_pairs={{1,0},{2,1},{3,2},{4,3},{5,4},{6,5},{7,6},{8,7},{9,8},{10,9},{11,1... | collective-permute-start | bytes 1572872 | tf_op jit(solution)/shard_map/ppermute | solution.py:333
  40.9 0.8 copy-start.5
  41.7 10.7 %collective-permute-start.5 = (f32[7,128,128]{2,1,0:T(8,128)}, f32[7,128,128]{2,1,0:T(8,128)}, u32[]{:S(2)}, u32[]{:S(2)}) collective-permute-start(f32[7,128,128]{2,1,0:T(8,128)} %get-tuple-element.17), channel_id=1, source_target_pairs={{16,0},{32,16},{48,32},{64,48},{80,64},{96,80},{112,96},{17,1},{33... | collective-permute-start | bytes 1376264 | tf_op jit(solution)/shard_map/ppermute | solution.py:333
  53.9 1.3 %copy-start.4 = (f32[2,9,128,128]{3,2,1,0:T(8,128)S(1)}, f32[2,9,128,128]{3,2,1,0:T(8,128)}, u32[]{:S(2)}) copy-start(f32[2,9,128,128]{3,2,1,0:T(8,128)} %copy-done.3) | copy-start | bytes 3538948
  55.2 1.0 %copy-start.6 = (f32[7,128,128]{2,1,0:T(8,128)S(1)}, f32[7,128,128]{2,1,0:T(8,128)}, u32[]{:S(2)}) copy-start(f32[7,128,128]{2,1,0:T(8,128)} %copy-done.5) | copy-start | bytes 1376260

commit v2 on v1

v2 whole, which is shorter than its diff:
```python
import jax
import jax.numpy as jnp
from jax import lax
from jax.experimental import pallas as pl
from jax.experimental.pallas import tpu as pltpu
from jax.sharding import PartitionSpec as P

ITERS = 3
B = 128
POWERS = 2 * ITERS + 1
F32 = jnp.float32
BF16 = jnp.bfloat16
PREPARE_BYTES = 80 * 2**20


def off(u, v):
    return 3 * (u + 1) + (v + 1)


def edge_list(v):
    low, high = min(0, v), max(0, v)
    first = []
    for row, us in ((0, (-1, 0)), (1, (0, 1))):
        first += [(row, True, off(u, w)) for u in us for w in (low, high)]
        first.append((row, False, off(-1 if row == 0 else 1, v)))
    second = []
    for row, u in ((0, 1), (1, -1)):
        second += [(row, True, off(u, w)) for w in (low, high)]
        second += [(row, False, off(0, v)), (row, False, off(u, v))]
    return first, second


def own_list(u):
    row, us = (1, (0, 1)) if u > 0 else (0, (-1, 0))
    return [(row, True, off(w, v)) for w in us for v in (-1, 0, 1)] + [(row, False, off(u, 0))]


FIRST = {v: edge_list(v)[0] for v in (1, -1)}
SECOND = {v: edge_list(v)[1] for v in (1, -1)}
OWN = {u: own_list(u) for u in (1, -1)}


PACKED = (FIRST[1], FIRST[-1], SECOND[1], SECOND[-1], OWN[1], OWN[-1])
TOTAL_COPIES = sum(len(entries) for entries in PACKED)


def pack_kernel(mask, blocks, rhs, *refs):
    sends, own, held, masked, in_sems, out_sems, own_sem = refs[:6], refs[6], *refs[7:]
    block_copies = []
    for row in range(2):
        for part in range(3):
            offsets = pl.ds(3 * part, 3)
            block_copies.append(
                pltpu.make_async_copy(
                    blocks.at[row, 0, offsets], held.at[row, offsets], in_sems.at[3 * row + part]
                )
            )
            block_copies[-1].start()
    out_copies = []

    def send(source, ref, place):
        out_copies.append(pltpu.make_async_copy(source, ref.at[place], out_sems.at[len(out_copies)]))
        out_copies[-1].start()

    for ref, entries in zip(sends, PACKED):
        for place, (row, is_coupling, o) in enumerate(entries):
            if not is_coupling:
                send(rhs.at[row, 0, o], ref, place)
    atoms = mask.shape[0] // 16
    orbitals = B // (mask.shape[0] // 16)
    lane = lax.broadcasted_iota(jnp.int32, (mask.shape[0], 2 * atoms * B), 1)
    entry = lax.broadcasted_iota(jnp.int32, (mask.shape[0], 2 * atoms * B), 0)
    select = (entry == lane // orbitals).astype(F32).astype(BF16)
    wide = lax.dot_general(
        mask[...].astype(F32).astype(BF16),
        select,
        (((0,), (0,)), ((), ())),
        preferred_element_type=F32,
    )
    for row in range(2):
        for o in range(9):
            if o % 3 == 0:
                block_copies[3 * row + o // 3].wait()
            for a in range(atoms):
                start = (row * atoms + a) * B
                factor = jnp.broadcast_to(wide[o : o + 1, start : start + B], (orbitals, B))
                rows = slice(a * orbitals, (a + 1) * orbitals)
                masked[row, o, rows, :] = held[row, o, rows, :] * factor
            for ref, entries in zip(sends, PACKED):
                for place, listed in enumerate(entries):
                    if listed == (row, True, o):
                        send(masked.at[row, o], ref, place)
    own_copy = pltpu.make_async_copy(masked, own, own_sem)
    own_copy.start()
    for copy in out_copies:
        copy.wait()
    own_copy.wait()


def pack(blocks, mask, rhs):
    out = [jax.ShapeDtypeStruct((len(entries), B, B), F32) for entries in PACKED]
    out.append(jax.ShapeDtypeStruct((2, 9, B, B), F32))
    flat = jnp.transpose(mask, (0, 1, 3, 4, 2)).reshape(-1, 9)
    return pl.pallas_call(
        pack_kernel,
        out_shape=out,
        in_specs=[pl.BlockSpec(memory_space=pltpu.VMEM)] + [pl.BlockSpec(memory_space=pl.ANY)] * 2,
        out_specs=[pl.BlockSpec(memory_space=pl.ANY)] * 7,
        scratch_shapes=[
            pltpu.VMEM((2, 9, B, B), F32),
            pltpu.VMEM((2, 9, B, B), F32),
            pltpu.SemaphoreType.DMA((6,)),
            pltpu.SemaphoreType.DMA((TOTAL_COPIES,)),
            pltpu.SemaphoreType.DMA,
        ],
        compiler_params=pltpu.CompilerParams(vmem_limit_bytes=60 * 2**20),
        name="pack",
    )(flat, blocks, rhs)


def split(value):
    high = value.astype(BF16)
    low = (value - high.astype(F32)).astype(BF16)
    return high, low


def guarded(top, bottom, floor_val):
    return top * bottom / (bottom * bottom + floor_val * floor_val)


def poly_add(left, scale, right):
    out = []
    for i in range(max(len(left), len(right))):
        if i >= len(right):
            out.append(left[i])
        elif i >= len(left):
            out.append(scale * right[i])
        else:
            out.append(left[i] + scale * right[i])
    return out


def poly_apply(p):
    return poly_add(list(p), -1.0, [jnp.zeros_like(p[0])] + list(p))


def poly_first(gram, p):
    total = p[0] * gram[0][0]
    for i in range(1, len(p)):
        total = total + p[i] * gram[0][i]
    return total


def poly_norm(gram, p):
    total = 0.0
    for i in range(len(p)):
        inner = p[i] * gram[i][i]
        for j in range(i):
            inner = inner + 2.0 * (p[j] * gram[j][i])
        total = total + p[i] * inner
    return total


def tfqmr(gram, limits):
    one = jnp.ones_like(limits)
    zero = jnp.zeros_like(limits)
    norm = gram[0][0]
    w = [one]
    y1 = [one]
    u1 = poly_apply(y1)
    v = u1
    d = [zero]
    x = [zero]
    rho, floor_val, tau = norm, 0.1 * norm, jnp.sqrt(norm)
    theta = zero
    eta = zero
    y2 = None
    u2 = None
    ww = norm
    for iteration in range(ITERS):
        if iteration > 0:
            rho_next = poly_first(gram, w)
            beta = guarded(rho_next, rho, floor_val)
            floor_val = 0.1 * jnp.sqrt(norm * ww)
            rho = rho_next
            y1 = poly_add(w, beta, y2)
            u1 = poly_apply(y1)
            v = poly_add(u1, beta, poly_add(u2, beta, v))
        alpha_floor = 0.1 * jnp.sqrt(norm * (poly_norm(gram, v) + 1e-06))
        alpha = guarded(rho, poly_first(gram, v), alpha_floor)
        ratio = guarded(1.0, alpha, 0.1)
        y2 = poly_add(y1, -alpha, v)
        u2 = poly_apply(y2)
        active = (limits > iteration).astype(F32)
        for y, u in ((y1, u1), (y2, u2)):
            w = poly_add(w, -alpha, u)
            d = poly_add(y, theta * theta * eta * ratio, d)
            ww = poly_norm(gram, w)
            theta = jnp.sqrt(ww) / tau
            cosine = 1.0 / jnp.sqrt(1.0 + theta * theta)
            tau = tau * theta * cosine
            eta = cosine * cosine * alpha
            x = poly_add(x, active * eta, d)
    return x


COLUMNS = ((0, 2), (0, 3), (1, 3))
ROWS = ((0, 2), (0, 3), (1, 4), (2, 4))


def coupling_lanes(h, c, o):
    source_row, source_col = h + o // 3 - 1, c + o % 3 - 1
    c_low, c_high = COLUMNS[c]
    place = (source_row - ROWS[h][0]) * (c_high - c_low) + source_col - c_low
    return slice(place * B, (place + 1) * B)


def prepare_kernel(rap, ram, rbp, rbm, rxp, rxm, own, rhs, middle_h, middle_l, outer_h, outer_l, start):
    def put(h, c, is_coupling, o, value):
        if is_coupling:
            high, low = split(value)
            lanes = coupling_lanes(h, c, o)
            if h in (1, 2):
                middle_h[h - 1, c, :, lanes] = high
                middle_l[h - 1, c, :, lanes] = low
            else:
                outer_h[h // 3, :, lanes] = high
                outer_l[h // 3, :, lanes] = low
        else:
            g = h + o // 3 - 2
            if 0 <= g <= 1:
                start[g, 3 * (h - g) + c] = value

    for v, ref_a, ref_b in ((1, rap, rbp), (-1, ram, rbm)):
        for ref, entries in ((ref_a, FIRST[v]), (ref_b, SECOND[v])):
            for place, (row, is_coupling, o) in enumerate(entries):
                put(row + 1, 1 - v, is_coupling, o, ref[place])
    for u, ref in ((1, rxp), (-1, rxm)):
        for place, (row, is_coupling, o) in enumerate(OWN[u]):
            put(0 if u > 0 else 3, 1, is_coupling, o, ref[place])
    for row in range(2):
        for o in range(9):
            put(row + 1, 1, True, o, own[row, o])
    for row, u in ((0, 0), (1, 0), (0, 1), (1, -1)):
        put(row + 1, 1, False, off(u, 0), rhs[row, 0, off(u, 0)])


def prepare(*arrays):
    shapes = [((2, 3, B, 9 * B), BF16)] * 2 + [((2, B, 6 * B), BF16)] * 2 + [((2, 9, B, B), F32)]
    return pl.pallas_call(
        prepare_kernel,
        out_shape=[jax.ShapeDtypeStruct(*shape) for shape in shapes],
        in_specs=[pl.BlockSpec(memory_space=pltpu.VMEM)] * len(arrays),
        out_specs=[pl.BlockSpec(memory_space=pltpu.VMEM)] * len(shapes),
        compiler_params=pltpu.CompilerParams(vmem_limit_bytes=16 * 2**20),
        cost_estimate=pl.CostEstimate(flops=0, bytes_accessed=PREPARE_BYTES, transcendentals=0),
        name="prepare",
    )(*arrays)


def solve_kernel(
    middle_h, middle_l, outer_h, outer_l, start, fpl, fpr, fml, fmr, limits, out, corner_h, corner_l, *scratch
):
    fields = (scratch[0:3], scratch[3:6])
    later = scratch[6:]
    corners = {}
    for u, refs in ((1, (fpl, fpr)), (-1, (fml, fmr))):
        part = 5 if u > 0 else 0
        for side, v in ((0, 1), (1, -1)):
            for place in range(5):
                corners[0 if u > 0 else 3, 1 - v, *FIRST[v][part + place][1:]] = (refs[side], place)

    def power(slot, g, m):
        if slot > 0:
            return later[slot - 1][g, m * B : (m + 1) * B, :]
        h, c = g + m // 3, m % 3
        found = corners.get((h, c, False, off(1 - m // 3, 1 - c)))
        if found is not None and h in (0, 3):
            return found[0][found[1]]
        return start[g, m]

    def put_field(slot, g, h, c, value):
        high, low = split(value)
        for target in range(3):
            c_low, c_high = COLUMNS[target]
            if c_low <= c < c_high:
                first = (h * (c_high - c_low) + c - c_low) * B
                ref = fields[slot % 2][target]
                ref[first : first + B, (1 + g) * B : (2 + g) * B] = high
                ref[first : first + B, 3 * g * B : (3 * g + 1) * B] = low

    def put_vector(slot, g, h, c, value):
        m = 3 * (h - g) + c
        later[slot - 1][g, m * B : (m + 1) * B, :] = value
        if slot < POWERS - 1:
            put_field(slot, g, h, c, value)

    for (h, c, is_coupling, o), (ref, place) in corners.items():
        if is_coupling:
            high, low = split(ref[place])
            corner_h[h // 3, c // 2, :, coupling_lanes(h, c, o)] = high
            corner_l[h // 3, c // 2, :, coupling_lanes(h, c, o)] = low
    for g in range(2):
        for m in range(9):
            put_field(0, g, g + m // 3, m % 3, power(0, g, m))

    def weights(h, c):
        if h in (1, 2):
            return middle_h.at[h - 1, c], middle_l.at[h - 1, c]
        if c == 1:
            return outer_h.at[h // 3], outer_l.at[h // 3]
        return corner_h.at[h // 3, c // 2], corner_l.at[h // 3, c // 2]

    def apply(slot):
        for h in range(4):
            for c in range(3):
                field = fields[slot % 2][c]
                count = COLUMNS[c][1] - COLUMNS[c][0]
                first = ROWS[h][0]
                wh, wl = weights(h, c)

                def product(weight, low, high, lanes_low, lanes_high):
                    left = weight[:, (low - first) * count * B : (high - first) * count * B]
                    right = field[low * count * B : high * count * B, lanes_low * B : lanes_high * B]
                    return jnp.dot(left, right, preferred_element_type=F32)

                values = {}
                for g in range(2):
                    if 0 <= h - g <= 2:
                        low, high = max(ROWS[h][0], g), min(ROWS[h][1], g + 3)
                        both = product(wh, low, high, 2 * g, 2 * g + 2)
                        values[g] = both[:, :B] + both[:, B:]
                if len(values) == 2:
                    both = product(wl, 1, 3, 1, 3)
                    values[0] = values[0] + both[:, :B]
                    values[1] = values[1] + both[:, B:]
                    g, other = (0, 0) if h == 1 else (1, 3)
                    values[g] = values[g] + product(wl, other, other + 1, 1 + g, 2 + g)
                else:
                    for g in values:
                        values[g] = values[g] + product(wl, *ROWS[h], 1 + g, 2 + g)
                for g in values:
                    put_vector(slot + 1, g, h, c, values[g])

    partial = {}

    def grams(slot):
        for g in range(2):
            totals = [None] * (slot + 1)
            for m in range(9):
                here = power(slot, g, m)
                for i in range(slot + 1):
                    term = jnp.sum((here * power(i, g, m)).reshape(16, 8, B), axis=0)
                    totals[i] = term if totals[i] is None else totals[i] + term
            for i in range(slot + 1):
                partial[slot, i, g] = jnp.sum(totals[i], axis=0, keepdims=True)

    for slot in range(POWERS - 1):
        apply(slot)
        grams(slot)
    grams(POWERS - 1)
    gram = [
        [
            jnp.concatenate([partial[max(i, j), min(i, j), g] for g in range(2)], axis=0)
            for j in range(POWERS)
        ]
        for i in range(POWERS)
    ]
    x = tfqmr(gram, limits[...])
    for g in range(2):
        for m in range(9):
            total = x[0][g : g + 1, :] * power(0, g, m)
            for i in range(1, len(x)):
                total = total + x[i][g : g + 1, :] * power(i, g, m)
            out[g, 0, m] = total


def solve(*arrays):
    fields = [pltpu.VMEM((4 * (high - low) * B, 4 * B), BF16) for low, high in COLUMNS]
    return pl.pallas_call(
        solve_kernel,
        out_shape=jax.ShapeDtypeStruct((2, 1, 9, B, B), F32),
        in_specs=[pl.BlockSpec(memory_space=pltpu.VMEM)] * len(arrays),
        out_specs=pl.BlockSpec(memory_space=pltpu.VMEM),
        scratch_shapes=[
            pltpu.VMEM((2, 2, B, 4 * B), BF16),
            pltpu.VMEM((2, 2, B, 4 * B), BF16),
            *fields,
            *fields,
            *[pltpu.VMEM((2, 9 * B, B), F32) for _ in range(POWERS - 1)],
        ],
        compiler_params=pltpu.CompilerParams(vmem_limit_bytes=24 * 2**20),
        name="solve",
    )(*arrays)


def shift(value, axis, step):
    count = lax.axis_size(axis)
    if step > 0:
        pairs = [(i, i + 1) for i in range(count - 1)]
    else:
        pairs = [(i + 1, i) for i in range(count - 1)]
    return lax.ppermute(value, axis, pairs)


def shards(blocks, pair_mask, rhs_rows, counts):
    sap, sam, sbp, sbm, oxp, oxm, own = pack(blocks, pair_mask, rhs_rows)
    rap = shift(sap, "gy", 1)
    ram = shift(sam, "gy", -1)
    rxp = shift(oxp, "gx", 1)
    rxm = shift(oxm, "gx", -1)
    rbp = shift(sbp, "gy", 1)
    rbm = shift(sbm, "gy", -1)
    fxp = (shift(rap[5:], "gx", 1), shift(ram[5:], "gx", 1))
    fxm = (shift(rap[:5], "gx", -1), shift(ram[:5], "gx", -1))
    prepared = prepare(rap, ram, rbp, rbm, rxp, rxm, own, rhs_rows)
    orbitals = B // pair_mask.shape[-1]
    limits = jnp.repeat(counts, orbitals, axis=-1).reshape(2, B).astype(F32)
    return solve(*prepared, *fxp, *fxm, limits)


def solution(mesh):
    return jax.shard_map(
        shards,
        mesh=mesh,
        in_specs=(
            P("gx", "gy", None, None, None),
            P("gx", "gy", None, None, None),
            P("gx", "gy", None, None, None),
            P("gx", "gy", None),
        ),
        out_specs=P("gx", "gy", None, None, None),
        check_vma=False,
    )
```

time: 83.6 us -> 90.9 us (1.087)
  Pallas kernels: 27.4 us -> 45.3 us
  waiting for transfers between devices: 22.3 us -> 5.52 us
  starting transfers between devices: 23.6 us -> 31.6 us
  other arithmetic: 1.8 us -> 0.01 us
    pallas_call x1, Pallas kernels: 1.52 us -> 30.3 us  [pack(): pl.pallas_call(pack_kernel, out_shape=out, in_specs=[pl.BlockSpec(memory_...]
    ppermute x8 -> x10, waiting for transfers between devices: 22.3 us -> 5.52 us  [shift(): return lax.ppermute(value, axis, pairs)]
    pallas_call x1, Pallas kernels: 25.9 us -> 14.4 us  [solve(): pl.pallas_call(solve_kernel, out_shape=jax.ShapeDtypeStruct((2, 1, 9, B,...]
    ppermute x8 -> x10, starting transfers between devices: 23.6 us -> 31.6 us  [shift(): return lax.ppermute(value, axis, pairs)]
    concatenate x2 -> x0, other arithmetic: 1.8 us -> none  [the longest x1 0.9 us: shards(): fxp = shift(jnp.concatenate([rap[5:], ram[5:]], axis=0), 'gx', 1)]
    unnamed x17 -> x14, local copies, waits for them, and re-layouts: 6.64 us -> 4.84 us
    slice x2, local copies, waits for them, and re-layouts: 0.09 us -> 1.78 us  [shards(): fxm = (shift(rap[:5], 'gx', -1), shift(ram[:5], 'gx', -1))]
  transfers between devices with their start and end apart: 8 -> 10, of which waited for: 4 -> 2; matrix products, arithmetic and copies ran while one was open for 2% -> 2% of each run, Pallas kernels for 0% -> 1%
where the time goes in v2:
time: 90.9 us; the launch traced here: 89.5 us
  Pallas kernels  45.3 us (50%)
  starting transfers between devices  31.6 us (35%)
  local copies, waits for them, and re-layouts  6.78 us (7%)
  waiting for transfers between devices  5.52 us (6%)
    ppermute x10, starting transfers between devices, shift(): return lax.ppermute(value, axis, pairs)  31.6 us
    pallas_call x1, Pallas kernels, pack(): pl.pallas_call(pack_kernel, out_shape=out, in_specs=[pl.BlockSpec(memory_...  30.3 us
    pallas_call x1, Pallas kernels, solve(): pl.pallas_call(solve_kernel, out_shape=jax.ShapeDtypeStruct((2, 1, 9, B,...  14.4 us
    ppermute x10, waiting for transfers between devices, shift(): return lax.ppermute(value, axis, pairs)  5.52 us
    unnamed x14, local copies, waits for them, and re-layouts  4.84 us
  transfers between devices with their start and end apart: 10, of which 2 were waited for; matrix products, arithmetic and copies ran while one was open for 2% of the time, Pallas kernels for 1%

profile of v2, /device:TPU:1, one launch (start us, length us, event | category | flops | bytes accessed | tf_op | source)
XLA Modules:
  0.0 89.5 jit_solution(11624253318796611484)
XLA Ops:
  0.0 30.3 %pack.1 = (f32[10,128,128]{2,1,0:T(8,128)}, f32[10,128,128]{2,1,0:T(8,128)}, f32[8,128,128]{2,1,0:T(8,128)}, f32[8,128,128]{2,1,0:T(8,128)}, f32[7,128,128]{2,1,...) custom-call(s32[128,9]{1,0:T(8,128)} %bitcast.4, f32[2,1,9,128,128]{4,3,2,1,0:T(8,128)} %blocks.1, ...), custom_call_target="tpu_custom_call" | custom-call | tf_op jit(solution)/shard_map/pack/pallas_call | solution.py:104
  30.3 4.4 %collective-permute-start = (f32[10,128,128]{2,1,0:T(8,128)}, f32[10,128,128]{2,1,0:T(8,128)S(1)}, u32[]{:S(2)}, u32[]{:S(2)}) collective-permute-start(f32[10,128,128]{2,1,0:T(8,128)} %get-tuple-element.17), channel_id=1, source_target_pairs={{0,1},{1,2},{2,3},{3,4},{4,5},{5,6},{6,7},{7,8},{8,9},{9,10},{10,1... | collective-permute-start | bytes 1966088 | tf_op jit(solution)/shard_map/ppermute | solution.py:403
  34.7 1.3 %collective-permute-start.1 = (f32[10,128,128]{2,1,0:T(8,128)}, f32[10,128,128]{2,1,0:T(8,128)S(1)}, u32[]{:S(2)}, u32[]{:S(2)}) collective-permute-start(f32[10,128,128]{2,1,0:T(8,128)} %get-tuple-element.18), channel_id=1, source_target_pairs={{1,0},{2,1},{3,2},{4,3},{5,4},{6,5},{7,6},{8,7},{9,8},{10,9},{11,1... | collective-permute-start | bytes 1966088 | tf_op jit(solution)/shard_map/ppermute | solution.py:403
  36.0 4.2 %collective-permute-start.2 = (f32[8,128,128]{2,1,0:T(8,128)}, f32[8,128,128]{2,1,0:T(8,128)S(1)}, u32[]{:S(2)}, u32[]{:S(2)}) collective-permute-start(f32[8,128,128]{2,1,0:T(8,128)} %get-tuple-element.19), channel_id=1, source_target_pairs={{0,1},{1,2},{2,3},{3,4},{4,5},{5,6},{6,7},{7,8},{8,9},{9,10},{10,1... | collective-permute-start | bytes 1572872 | tf_op jit(solution)/shard_map/ppermute | solution.py:403
  40.2 1.3 %collective-permute-start.3 = (f32[8,128,128]{2,1,0:T(8,128)}, f32[8,128,128]{2,1,0:T(8,128)S(1)}, u32[]{:S(2)}, u32[]{:S(2)}) collective-permute-start(f32[8,128,128]{2,1,0:T(8,128)} %get-tuple-element.20), channel_id=1, source_target_pairs={{1,0},{2,1},{3,2},{4,3},{5,4},{6,5},{7,6},{8,7},{9,8},{10,9},{11,1... | collective-permute-start | bytes 1572872 | tf_op jit(solution)/shard_map/ppermute | solution.py:403
  41.5 4.4 %collective-permute-start.4 = (f32[7,128,128]{2,1,0:T(8,128)}, f32[7,128,128]{2,1,0:T(8,128)S(1)}, u32[]{:S(2)}, u32[]{:S(2)}) collective-permute-start(f32[7,128,128]{2,1,0:T(8,128)} %get-tuple-element.21), channel_id=1, source_target_pairs={{0,16},{16,32},{32,48},{48,64},{64,80},{80,96},{96,112},{1,17},{17... | collective-permute-start | bytes 1376264 | tf_op jit(solution)/shard_map/ppermute | solution.py:403
  45.9 2.5 %collective-permute-done.rap = f32[10,128,128]{2,1,0:T(8,128)S(1)} collective-permute-done((f32[10,128,128]{2,1,0:T(8,128)}, f32[10,128,128]{2,1,0:T(8,128)S(1)}, u32[]{:S(2)}, u32[]{:S(2)}) %collective-permute-start) | collective-permute-done | bytes 655392 | tf_op jit(solution)/shard_map/ppermute | solution.py:403
  48.4 0.0 copy-start.6
  48.4 0.0 copy-start
  48.4 4.7 %collective-permute-start.5 = (f32[7,128,128]{2,1,0:T(8,128)}, f32[7,128,128]{2,1,0:T(8,128)S(1)}, u32[]{:S(2)}, u32[]{:S(2)}) collective-permute-start(f32[7,128,128]{2,1,0:T(8,128)} %get-tuple-element.22), channel_id=1, source_target_pairs={{16,0},{32,16},{48,32},{64,48},{80,64},{96,80},{112,96},{17,1},{33... | collective-permute-start | bytes 1376264 | tf_op jit(solution)/shard_map/ppermute | solution.py:403
  53.1 0.9 fusion.1
  54.0 0.0 collective-permute-done.1.ram
  54.0 4.4 %collective-permute-start.6 = (f32[5,128,128]{2,1,0:T(8,128)}, f32[5,128,128]{2,1,0:T(8,128)}, u32[]{:S(2)}, u32[]{:S(2)}) collective-permute-start(f32[5,128,128]{2,1,0:T(8,128)} %get-tuple-element.32), channel_id=1, source_target_pairs={{0,16},{16,32},{32,48},{48,64},{64,80},{80,96},{96,112},{1,17},{17... | collective-permute-start | bytes 983048 | tf_op jit(solution)/shard_map/ppermute | solution.py:403
  58.4 0.9 fusion
  59.3 0.0 collective-permute-done.4.rxp
  59.3 0.0 copy-start.2
  59.3 0.8 copy-done.2
  60.1 1.9 %collective-permute-start.7 = (f32[5,128,128]{2,1,0:T(8,128)}, f32[5,128,128]{2,1,0:T(8,128)}, u32[]{:S(2)}, u32[]{:S(2)}) collective-permute-start(f32[5,128,128]{2,1,0:T(8,128)} %get-tuple-element.30), channel_id=1, source_target_pairs={{0,16},{16,32},{32,48},{48,64},{64,80},{80,96},{96,112},{1,17},{17... | collective-permute-start | bytes 983048 | tf_op jit(solution)/shard_map/ppermute | solution.py:403
  62.0 0.0 collective-permute-done.5.rxm
  62.0 0.0 copy-start.4
  62.0 0.8 copy-done.4
  62.8 3.1 %collective-permute-start.8 = (f32[5,128,128]{2,1,0:T(8,128)}, f32[5,128,128]{2,1,0:T(8,128)}, u32[]{:S(2)}, u32[]{:S(2)}) collective-permute-start(f32[5,128,128]{2,1,0:T(8,128)} %get-tuple-element.31), channel_id=1, source_target_pairs={{16,0},{32,16},{48,32},{64,48},{80,64},{96,80},{112,96},{17,1},{33... | collective-permute-start | bytes 983048 | tf_op jit(solution)/shard_map/ppermute | solution.py:403
  65.9 0.0 collective-permute-done.2.rbp
  66.0 1.9 %collective-permute-start.9 = (f32[5,128,128]{2,1,0:T(8,128)}, f32[5,128,128]{2,1,0:T(8,128)}, u32[]{:S(2)}, u32[]{:S(2)}) collective-permute-start(f32[5,128,128]{2,1,0:T(8,128)} %get-tuple-element.29), channel_id=1, source_target_pairs={{16,0},{32,16},{48,32},{64,48},{80,64},{96,80},{112,96},{17,1},{33... | collective-permute-start | bytes 983048 | tf_op jit(solution)/shard_map/ppermute | solution.py:403
  67.9 0.0 copy-done.6
  67.9 0.1 broadcast_in_dim.3
  68.0 0.1 convert_element_type.9.limits
  68.1 0.0 collective-permute-done.3.rbm
  68.1 0.0 copy-done
  68.1 0.0 copy-start.1
  68.1 1.3 %copy-done.1 = f32[2,9,128,128]{3,2,1,0:T(8,128)S(1)} copy-done((f32[2,9,128,128]{3,2,1,0:T(8,128)S(1)}, f32[2,9,128,128]{3,2,1,0:T(8,128)}, u32[]{:S(2)}) %copy-start.1) | copy-done | bytes 1179672
  69.3 0.0 copy-start.3
  69.3 1.0 %copy-done.3 = f32[7,128,128]{2,1,0:T(8,128)S(1)} copy-done((f32[7,128,128]{2,1,0:T(8,128)S(1)}, f32[7,128,128]{2,1,0:T(8,128)}, u32[]{:S(2)}) %copy-start.3) | copy-done | bytes 458776
  70.4 0.0 copy-start.5
  70.4 1.0 %copy-done.5 = f32[7,128,128]{2,1,0:T(8,128)S(1)} copy-done((f32[7,128,128]{2,1,0:T(8,128)S(1)}, f32[7,128,128]{2,1,0:T(8,128)}, u32[]{:S(2)}) %copy-start.5) | copy-done | bytes 458776
  71.4 0.6 prepare.1
  72.0 0.0 collective-permute-done.6.fpl
  72.0 0.0 collective-permute-done.7.fpr
  72.0 0.0 collective-permute-done.8.fml
  72.0 3.0 %collective-permute-done.9.fmr = f32[5,128,128]{2,1,0:T(8,128)} collective-permute-done((f32[5,128,128]{2,1,0:T(8,128)}, f32[5,128,128]{2,1,0:T(8,128)}, u32[]{:S(2)}, u32[]{:S(2)}) %collective-permute-start.9) | collective-permute-done | bytes 327712 | tf_op jit(solution)/shard_map/ppermute | solution.py:403
  75.0 14.4 %solve.1 = f32[2,1,9,128,128]{4,3,2,1,0:T(8,128)} custom-call(bf16[2,3,128,1152]{3,2,1,0:T(8,128)(2,1)S(1)} %get-tuple-element.24.middle_h, bf16[2,3,128,1152]{3,2,1,0:T(8,128)(2,1)S(1)} %get-tuple-element.25.middle_l, bf16[2,128,768]{2,1,0:T(8,128)(2,1)S(1)} %get-tuple-element.26.outer_h, bf16[2,128,768]{2,1,0:T(8,128)(2,1)S(1)} %get-tuple-element.27.outer_l, ...), custom_call_target="tpu_custom_call" | custom-call | tf_op jit(solution)/shard_map/solve/pallas_call | solution.py:380
  (1 shorter events, 0.0 us)
Async XLA Ops:
  30.3 18.1 %collective-permute-start = (f32[10,128,128]{2,1,0:T(8,128)}, f32[10,128,128]{2,1,0:T(8,128)S(1)}, u32[]{:S(2)}, u32[]{:S(2)}) collective-permute-start(f32[10,128,128]{2,1,0:T(8,128)} %get-tuple-element.17), channel_id=1, source_target_pairs={{0,1},{1,2},{2,3},{3,4},{4,5},{5,6},{6,7},{7,8},{8,9},{9,10},{10,1... | collective-permute-start | bytes 1966088 | tf_op jit(solution)/shard_map/ppermute | solution.py:403
  34.7 19.3 %collective-permute-start.1 = (f32[10,128,128]{2,1,0:T(8,128)}, f32[10,128,128]{2,1,0:T(8,128)S(1)}, u32[]{:S(2)}, u32[]{:S(2)}) collective-permute-start(f32[10,128,128]{2,1,0:T(8,128)} %get-tuple-element.18), channel_id=1, source_target_pairs={{1,0},{2,1},{3,2},{4,3},{5,4},{6,5},{7,6},{8,7},{9,8},{10,9},{11,1... | collective-permute-start | bytes 1966088 | tf_op jit(solution)/shard_map/ppermute | solution.py:403
  36.0 29.9 %collective-permute-start.2 = (f32[8,128,128]{2,1,0:T(8,128)}, f32[8,128,128]{2,1,0:T(8,128)S(1)}, u32[]{:S(2)}, u32[]{:S(2)}) collective-permute-start(f32[8,128,128]{2,1,0:T(8,128)} %get-tuple-element.19), channel_id=1, source_target_pairs={{0,1},{1,2},{2,3},{3,4},{4,5},{5,6},{6,7},{7,8},{8,9},{9,10},{10,1... | collective-permute-start | bytes 1572872 | tf_op jit(solution)/shard_map/ppermute | solution.py:403
  40.2 27.9 %collective-permute-start.3 = (f32[8,128,128]{2,1,0:T(8,128)}, f32[8,128,128]{2,1,0:T(8,128)S(1)}, u32[]{:S(2)}, u32[]{:S(2)}) collective-permute-start(f32[8,128,128]{2,1,0:T(8,128)} %get-tuple-element.20), channel_id=1, source_target_pairs={{1,0},{2,1},{3,2},{4,3},{5,4},{6,5},{7,6},{8,7},{9,8},{10,9},{11,1... | collective-permute-start | bytes 1572872 | tf_op jit(solution)/shard_map/ppermute | solution.py:403
  41.5 17.8 %collective-permute-start.4 = (f32[7,128,128]{2,1,0:T(8,128)}, f32[7,128,128]{2,1,0:T(8,128)S(1)}, u32[]{:S(2)}, u32[]{:S(2)}) collective-permute-start(f32[7,128,128]{2,1,0:T(8,128)} %get-tuple-element.21), channel_id=1, source_target_pairs={{0,16},{16,32},{32,48},{48,64},{64,80},{80,96},{96,112},{1,17},{17... | collective-permute-start | bytes 1376264 | tf_op jit(solution)/shard_map/ppermute | solution.py:403
  48.4 19.5 %copy-start.6 = (s32[2,1,8]{2,1,0:T(1,128)S(1)}, s32[2,1,8]{2,1,0:T(1,128)}, u32[]{:S(2)}) copy-start(s32[2,1,8]{2,1,0:T(1,128)} %param.7) | copy-start | bytes 196
  48.4 19.7 %copy-start = (f32[2,1,9,128,128]{4,3,2,1,0:T(8,128)S(1)}, f32[2,1,9,128,128]{4,3,2,1,0:T(8,128)}, u32[]{:S(2)}) copy-start(f32[2,1,9,128,128]{4,3,2,1,0:T(8,128)} %rhs.3) | copy-start | bytes 3538948
  48.4 13.6 %collective-permute-start.5 = (f32[7,128,128]{2,1,0:T(8,128)}, f32[7,128,128]{2,1,0:T(8,128)S(1)}, u32[]{:S(2)}, u32[]{:S(2)}) collective-permute-start(f32[7,128,128]{2,1,0:T(8,128)} %get-tuple-element.22), channel_id=1, source_target_pairs={{16,0},{32,16},{48,32},{64,48},{80,64},{96,80},{112,96},{17,1},{33... | collective-permute-start | bytes 1376264 | tf_op jit(solution)/shard_map/ppermute | solution.py:403
  54.0 18.0 %collective-permute-start.6 = (f32[5,128,128]{2,1,0:T(8,128)}, f32[5,128,128]{2,1,0:T(8,128)}, u32[]{:S(2)}, u32[]{:S(2)}) collective-permute-start(f32[5,128,128]{2,1,0:T(8,128)} %get-tuple-element.32), channel_id=1, source_target_pairs={{0,16},{16,32},{32,48},{48,64},{64,80},{80,96},{96,112},{1,17},{17... | collective-permute-start | bytes 983048 | tf_op jit(solution)/shard_map/ppermute | solution.py:403
  59.3 0.8 copy-start.2
  60.1 11.9 %collective-permute-start.7 = (f32[5,128,128]{2,1,0:T(8,128)}, f32[5,128,128]{2,1,0:T(8,128)}, u32[]{:S(2)}, u32[]{:S(2)}) collective-permute-start(f32[5,128,128]{2,1,0:T(8,128)} %get-tuple-element.30), channel_id=1, source_target_pairs={{0,16},{16,32},{32,48},{48,64},{64,80},{80,96},{96,112},{1,17},{17... | collective-permute-start | bytes 983048 | tf_op jit(solution)/shard_map/ppermute | solution.py:403
  62.0 0.8 copy-start.4
  62.8 9.2 %collective-permute-start.8 = (f32[5,128,128]{2,1,0:T(8,128)}, f32[5,128,128]{2,1,0:T(8,128)}, u32[]{:S(2)}, u32[]{:S(2)}) collective-permute-start(f32[5,128,128]{2,1,0:T(8,128)} %get-tuple-element.31), channel_id=1, source_target_pairs={{16,0},{32,16},{48,32},{64,48},{80,64},{96,80},{112,96},{17,1},{33... | collective-permute-start | bytes 983048 | tf_op jit(solution)/shard_map/ppermute | solution.py:403
  66.0 9.1 %collective-permute-start.9 = (f32[5,128,128]{2,1,0:T(8,128)}, f32[5,128,128]{2,1,0:T(8,128)}, u32[]{:S(2)}, u32[]{:S(2)}) collective-permute-start(f32[5,128,128]{2,1,0:T(8,128)} %get-tuple-element.29), channel_id=1, source_target_pairs={{16,0},{32,16},{48,32},{64,48},{80,64},{96,80},{112,96},{17,1},{33... | collective-permute-start | bytes 983048 | tf_op jit(solution)/shard_map/ppermute | solution.py:403
  68.1 1.3 %copy-start.1 = (f32[2,9,128,128]{3,2,1,0:T(8,128)S(1)}, f32[2,9,128,128]{3,2,1,0:T(8,128)}, u32[]{:S(2)}) copy-start(f32[2,9,128,128]{3,2,1,0:T(8,128)} %get-tuple-element.23.own) | copy-start | bytes 3538948
  69.3 1.0 %copy-start.3 = (f32[7,128,128]{2,1,0:T(8,128)S(1)}, f32[7,128,128]{2,1,0:T(8,128)}, u32[]{:S(2)}) copy-start(f32[7,128,128]{2,1,0:T(8,128)} %copy-done.2) | copy-start | bytes 1376260
  70.4 1.0 %copy-start.5 = (f32[7,128,128]{2,1,0:T(8,128)S(1)}, f32[7,128,128]{2,1,0:T(8,128)}, u32[]{:S(2)}) copy-start(f32[7,128,128]{2,1,0:T(8,128)} %copy-done.4) | copy-start | bytes 1376260

commit v3 on v2

--- a/solution.py
+++ b/solution.py
@@ -10,7 +10,6 @@
 POWERS = 2 * ITERS + 1
 F32 = jnp.float32
 BF16 = jnp.bfloat16
-PREPARE_BYTES = 80 * 2**20
 
 
 def off(u, v):
@@ -41,33 +40,11 @@
 
 
 PACKED = (FIRST[1], FIRST[-1], SECOND[1], SECOND[-1], OWN[1], OWN[-1])
-TOTAL_COPIES = sum(len(entries) for entries in PACKED)
-
-
-def pack_kernel(mask, blocks, rhs, *refs):
-    sends, own, held, masked, in_sems, out_sems, own_sem = refs[:6], refs[6], *refs[7:]
-    block_copies = []
-    for row in range(2):
-        for part in range(3):
-            offsets = pl.ds(3 * part, 3)
-            block_copies.append(
-                pltpu.make_async_copy(
-                    blocks.at[row, 0, offsets], held.at[row, offsets], in_sems.at[3 * row + part]
-                )
-            )
-            block_copies[-1].start()
-    out_copies = []
-
-    def send(source, ref, place):
-        out_copies.append(pltpu.make_async_copy(source, ref.at[place], out_sems.at[len(out_copies)]))
-        out_copies[-1].start()
-
-    for ref, entries in zip(sends, PACKED):
-        for place, (row, is_coupling, o) in enumerate(entries):
-            if not is_coupling:
-                send(rhs.at[row, 0, o], ref, place)
+
+
+def masked_blocks(mask, blocks):
     atoms = mask.shape[0] // 16
-    orbitals = B // (mask.shape[0] // 16)
+    orbitals = B // atoms
     lane = lax.broadcasted_iota(jnp.int32, (mask.shape[0], 2 * atoms * B), 1)
     entry = lax.broadcasted_iota(jnp.int32, (mask.shape[0], 2 * atoms * B), 0)
     select = (entry == lane // orbitals).astype(F32).astype(BF16)
@@ -79,43 +56,53 @@
     )
     for row in range(2):
         for o in range(9):
-            if o % 3 == 0:
-                block_copies[3 * row + o // 3].wait()
+            rows = []
             for a in range(atoms):
                 start = (row * atoms + a) * B
-                factor = jnp.broadcast_to(wide[o : o + 1, start : start + B], (orbitals, B))
-                rows = slice(a * orbitals, (a + 1) * orbitals)
-                masked[row, o, rows, :] = held[row, o, rows, :] * factor
-            for ref, entries in zip(sends, PACKED):
-                for place, listed in enumerate(entries):
-                    if listed == (row, True, o):
-                        send(masked.at[row, o], ref, place)
-    own_copy = pltpu.make_async_copy(masked, own, own_sem)
-    own_copy.start()
-    for copy in out_copies:
-        copy.wait()
-    own_copy.wait()
+                rows.append(jnp.broadcast_to(wide[o : o + 1, start : start + B], (orbitals, B)))
+            yield row, o, blocks[row, 0, o] * jnp.concatenate(rows, axis=0)
+
+
+def pack_kernel(mask, blocks, rhs, *sends):
+    for row, o, value in masked_blocks(mask, blocks):
+        for ref, entries in zip(sends, PACKED):
+            for place, listed in enumerate(entries):
+                if listed == (row, True, o):
+                    ref[place] = value
+    for ref, entries in zip(sends, PACKED):
+        for place, (row, is_coupling, o) in enumerate(entries):
+            if not is_coupling:
+                ref[place] = rhs[row, 0, o]
 
 
 def pack(blocks, mask, rhs):
     out = [jax.ShapeDtypeStruct((len(entries), B, B), F32) for entries in PACKED]
-    out.append(jax.ShapeDtypeStruct((2, 9, B, B), F32))
-    flat = jnp.transpose(mask, (0, 1, 3, 4, 2)).reshape(-1, 9)
     return pl.pallas_call(
         pack_kernel,
         out_shape=out,
-        in_specs=[pl.BlockSpec(memory_space=pltpu.VMEM)] + [pl.BlockSpec(memory_space=pl.ANY)] * 2,
-        out_specs=[pl.BlockSpec(memory_space=pl.ANY)] * 7,
-        scratch_shapes=[
-            pltpu.VMEM((2, 9, B, B), F32),
-            pltpu.VMEM((2, 9, B, B), F32),
-            pltpu.SemaphoreType.DMA((6,)),
-            pltpu.SemaphoreType.DMA((TOTAL_COPIES,)),
-            pltpu.SemaphoreType.DMA,
-        ],
-        compiler_params=pltpu.CompilerParams(vmem_limit_bytes=60 * 2**20),
+        in_specs=[pl.BlockSpec(memory_space=pltpu.VMEM)] + [pl.BlockSpec(memory_space=pltpu.VMEM)] * 2,
+        out_specs=[pl.BlockSpec(memory_space=pltpu.VMEM)] * 6,
+        compiler_params=pltpu.CompilerParams(vmem_limit_bytes=8 * 2**20),
         name="pack",
-    )(flat, blocks, rhs)
+    )(mask, blocks, rhs)
+
+
+def relay_kernel(rap, ram, up, down):
+    up[:5] = rap[5:]
+    up[5:] = ram[5:]
+    down[:5] = rap[:5]
+    down[5:] = ram[:5]
+
+
+def relay(rap, ram):
+    return pl.pallas_call(
+        relay_kernel,
+        out_shape=[jax.ShapeDtypeStruct((10, B, B), F32)] * 2,
+        in_specs=[pl.BlockSpec(memory_space=pltpu.VMEM)] * 2,
+        out_specs=[pl.BlockSpec(memory_space=pltpu.VMEM)] * 2,
+        compiler_params=pltpu.CompilerParams(vmem_limit_bytes=8 * 2**20),
+        name="relay",
+    )(rap, ram)
 
 
 def split(value):
@@ -215,7 +202,7 @@
     return slice(place * B, (place + 1) * B)
 
 
-def prepare_kernel(rap, ram, rbp, rbm, rxp, rxm, own, rhs, middle_h, middle_l, outer_h, outer_l, start):
+def prepare_kernel(rap, ram, rbp, rbm, rxp, rxm, mask, blocks, rhs, middle_h, middle_l, outer_h, outer_l, start):
     def put(h, c, is_coupling, o, value):
         if is_coupling:
             high, low = split(value)
@@ -238,9 +225,8 @@
     for u, ref in ((1, rxp), (-1, rxm)):
         for place, (row, is_coupling, o) in enumerate(OWN[u]):
             put(0 if u > 0 else 3, 1, is_coupling, o, ref[place])
-    for row in range(2):
-        for o in range(9):
-            put(row + 1, 1, True, o, own[row, o])
+    for row, o, value in masked_blocks(mask, blocks):
+        put(row + 1, 1, True, o, value)
     for row, u in ((0, 0), (1, 0), (0, 1), (1, -1)):
         put(row + 1, 1, False, off(u, 0), rhs[row, 0, off(u, 0)])
 
@@ -253,22 +239,22 @@
         in_specs=[pl.BlockSpec(memory_space=pltpu.VMEM)] * len(arrays),
         out_specs=[pl.BlockSpec(memory_space=pltpu.VMEM)] * len(shapes),
         compiler_params=pltpu.CompilerParams(vmem_limit_bytes=16 * 2**20),
-        cost_estimate=pl.CostEstimate(flops=0, bytes_accessed=PREPARE_BYTES, transcendentals=0),
+        cost_estimate=pl.CostEstimate(flops=10**12, bytes_accessed=10**9, transcendentals=10**9),
         name="prepare",
     )(*arrays)
 
 
 def solve_kernel(
-    middle_h, middle_l, outer_h, outer_l, start, fpl, fpr, fml, fmr, limits, out, corner_h, corner_l, *scratch
+    middle_h, middle_l, outer_h, outer_l, start, fxp, fxm, limits, out, corner_h, corner_l, *scratch
 ):
     fields = (scratch[0:3], scratch[3:6])
     later = scratch[6:]
     corners = {}
-    for u, refs in ((1, (fpl, fpr)), (-1, (fml, fmr))):
+    for u, ref in ((1, fxp), (-1, fxm)):
         part = 5 if u > 0 else 0
         for side, v in ((0, 1), (1, -1)):
             for place in range(5):
-                corners[0 if u > 0 else 3, 1 - v, *FIRST[v][part + place][1:]] = (refs[side], place)
+                corners[0 if u > 0 else 3, 1 - v, *FIRST[v][part + place][1:]] = (ref, side * 5 + place)
 
     def power(slot, g, m):
         if slot > 0:
@@ -404,19 +390,21 @@
 
 
 def shards(blocks, pair_mask, rhs_rows, counts):
-    sap, sam, sbp, sbm, oxp, oxm, own = pack(blocks, pair_mask, rhs_rows)
+    mask = jnp.transpose(pair_mask, (0, 1, 3, 4, 2)).reshape(-1, 9)
+    sap, sam, sbp, sbm, oxp, oxm = pack(blocks, mask, rhs_rows)
     rap = shift(sap, "gy", 1)
     ram = shift(sam, "gy", -1)
     rxp = shift(oxp, "gx", 1)
     rxm = shift(oxm, "gx", -1)
     rbp = shift(sbp, "gy", 1)
     rbm = shift(sbm, "gy", -1)
-    fxp = (shift(rap[5:], "gx", 1), shift(ram[5:], "gx", 1))
-    fxm = (shift(rap[:5], "gx", -1), shift(ram[:5], "gx", -1))
-    prepared = prepare(rap, ram, rbp, rbm, rxp, rxm, own, rhs_rows)
+    up, down = relay(rap, ram)
+    fxp = shift(up, "gx", 1)
+    fxm = shift(down, "gx", -1)
+    prepared = prepare(rap, ram, rbp, rbm, rxp, rxm, mask, blocks, rhs_rows)
     orbitals = B // pair_mask.shape[-1]
     limits = jnp.repeat(counts, orbitals, axis=-1).reshape(2, B).astype(F32)
-    return solve(*prepared, *fxp, *fxm, limits)
+    return solve(*prepared, fxp, fxm, limits)
 
 
 def solution(mesh):

time: 90.9 us -> 62.9 us (0.69)
  Pallas kernels: 45.3 us -> 20.9 us
  waiting for transfers between devices: 5.52 us -> 9.2 us
  local copies, waits for them, and re-layouts: 6.78 us -> 3.55 us
  starting transfers between devices: 31.6 us -> 28.6 us
    pallas_call x1, Pallas kernels: 30.3 us -> 1.7 us  [pack(): pl.pallas_call(pack_kernel, out_shape=out, in_specs=[pl.BlockSpec(memory_...]
    ppermute x10 -> x8, waiting for transfers between devices: 5.52 us -> 9.2 us  [shift(): return lax.ppermute(value, axis, pairs)]
    ppermute x10 -> x8, starting transfers between devices: 31.6 us -> 28.6 us  [shift(): return lax.ppermute(value, axis, pairs)]
    pallas_call x0 -> x1, Pallas kernels: none -> 2.23 us  [relay(): pl.pallas_call(relay_kernel, out_shape=[jax.ShapeDtypeStruct((10, B, B),...]
    pallas_call x1, Pallas kernels: 0.59 us -> 2.49 us  [prepare(): pl.pallas_call(prepare_kernel, out_shape=[jax.ShapeDtypeStruct(*shape) fo...]
    slice x2 -> x0, local copies, waits for them, and re-layouts: 1.78 us -> none  [shards(): fxm = (shift(rap[:5], 'gx', -1), shift(ram[:5], 'gx', -1))]
    unnamed x14, local copies, waits for them, and re-layouts: 4.84 us -> 3.39 us
  transfers between devices with their start and end apart: 10 -> 8, of which waited for: 2 -> 4; matrix products, arithmetic and copies ran while one was open for 2% -> 0% of each run, Pallas kernels for 1% -> 8%
where the time goes in v3:
time: 62.9 us; the launch traced here: 62.4 us
  starting transfers between devices  28.6 us (45%)
  Pallas kernels  20.9 us (33%)
  waiting for transfers between devices  9.2 us (15%)
  local copies, waits for them, and re-layouts  3.55 us (6%)
    ppermute x8, starting transfers between devices, shift(): return lax.ppermute(value, axis, pairs)  28.6 us
    pallas_call x1, Pallas kernels, solve(): pl.pallas_call(solve_kernel, out_shape=jax.ShapeDtypeStruct((2, 1, 9, B,...  14.5 us
    ppermute x8, waiting for transfers between devices, shift(): return lax.ppermute(value, axis, pairs)  9.2 us
    unnamed x14, local copies, waits for them, and re-layouts  3.39 us
    pallas_call x1, Pallas kernels, prepare(): pl.pallas_call(prepare_kernel, out_shape=[jax.ShapeDtypeStruct(*shape) fo...  2.49 us
    pallas_call x1, Pallas kernels, relay(): pl.pallas_call(relay_kernel, out_shape=[jax.ShapeDtypeStruct((10, B, B),...  2.23 us
    pallas_call x1, Pallas kernels, pack(): pl.pallas_call(pack_kernel, out_shape=out, in_specs=[pl.BlockSpec(memory_...  1.7 us
  transfers between devices with their start and end apart: 8, of which 4 were waited for; matrix products, arithmetic and copies ran while one was open for 0% of the time, Pallas kernels for 8%

profile of v3, /device:TPU:1, one launch (start us, length us, event | category | flops | bytes accessed | tf_op | source)
XLA Modules:
  0.0 62.4 jit_solution(12990945636126832281)
XLA Ops:
  0.0 0.0 copy-start
  0.0 1.3 %copy-done = f32[2,1,9,128,128]{4,3,2,1,0:T(8,128)S(1)} copy-done((f32[2,1,9,128,128]{4,3,2,1,0:T(8,128)S(1)}, f32[2,1,9,128,128]{4,3,2,1,0:T(8,128)}, u32[]{:S(2)}) %copy-start) | copy-done | bytes 1179672
  1.3 0.0 copy-start.2
  1.3 1.3 %copy-done.2 = f32[2,1,9,128,128]{4,3,2,1,0:T(8,128)S(1)} copy-done((f32[2,1,9,128,128]{4,3,2,1,0:T(8,128)S(1)}, f32[2,1,9,128,128]{4,3,2,1,0:T(8,128)}, u32[]{:S(2)}) %copy-start.2) | copy-done | bytes 1179672
  2.5 0.0 copy-start.4
  2.5 0.8 %copy-done.4 = s32[2,1,9,8,8]{2,4,3,1,0:T(8,128)S(1)} copy-done((s32[2,1,9,8,8]{2,4,3,1,0:T(8,128)S(1)}, s32[2,1,9,8,8]{2,4,3,1,0:T(8,128)}, u32[]{:S(2)}) %copy-start.4) | copy-done | bytes 4632
  3.4 0.0 copy-start.6
  3.4 0.0 copy-start.3
  3.4 1.7 %pack.1 = (f32[10,128,128]{2,1,0:T(8,128)S(1)}, f32[10,128,128]{2,1,0:T(8,128)}, f32[8,128,128]{2,1,0:T(8,128)}, f32[8,128,128]{2,1,0:T(8,128)}, f32[7,128,128]{2,1,0:T(8,128)}, /*index=5*/f32[7,128,128]{2,1,0:T(8,128)S(1)}) custom-call(s32[128,9]{1,0:T(8,128)S(1)} %bitcast.4, f32[2,1,9,128,128]{4,3,2,1,0:T(8,128)S(1)} %copy-done, ...), custom_call_target="tpu_custom_call" | custom-call | tf_op jit(solution)/shard_map/pack/pallas_call | solution.py:80
  5.1 0.0 copy-start.1
  5.1 0.0 copy-start.5
  5.1 4.5 %collective-permute-start = (f32[10,128,128]{2,1,0:T(8,128)S(1)}, f32[10,128,128]{2,1,0:T(8,128)S(1)}, u32[]{:S(2)}, u32[]{:S(2)}) collective-permute-start(f32[10,128,128]{2,1,0:T(8,128)S(1)} %get-tuple-element.18), channel_id=1, source_target_pairs={{0,1},{1,2},{2,3},{3,4},{4,5},{5,6},{6,7},{7,8},{8,9},{9,10},{10,1... | collective-permute-start | bytes 1966088 | tf_op jit(solution)/shard_map/ppermute | solution.py:389
  9.6 1.3 %collective-permute-start.1 = (f32[10,128,128]{2,1,0:T(8,128)}, f32[10,128,128]{2,1,0:T(8,128)}, u32[]{:S(2)}, u32[]{:S(2)}) collective-permute-start(f32[10,128,128]{2,1,0:T(8,128)} %get-tuple-element.19), channel_id=1, source_target_pairs={{1,0},{2,1},{3,2},{4,3},{5,4},{6,5},{7,6},{8,7},{9,8},{10,9},{11,1... | collective-permute-start | bytes 1966088 | tf_op jit(solution)/shard_map/ppermute | solution.py:389
  10.9 4.9 %collective-permute-start.2 = (f32[8,128,128]{2,1,0:T(8,128)}, f32[8,128,128]{2,1,0:T(8,128)}, u32[]{:S(2)}, u32[]{:S(2)}) collective-permute-start(f32[8,128,128]{2,1,0:T(8,128)} %get-tuple-element.20), channel_id=1, source_target_pairs={{0,1},{1,2},{2,3},{3,4},{4,5},{5,6},{6,7},{7,8},{8,9},{9,10},{10,1... | collective-permute-start | bytes 1572872 | tf_op jit(solution)/shard_map/ppermute | solution.py:389
  15.9 1.3 %collective-permute-start.3 = (f32[8,128,128]{2,1,0:T(8,128)}, f32[8,128,128]{2,1,0:T(8,128)}, u32[]{:S(2)}, u32[]{:S(2)}) collective-permute-start(f32[8,128,128]{2,1,0:T(8,128)} %get-tuple-element.21), channel_id=1, source_target_pairs={{1,0},{2,1},{3,2},{4,3},{5,4},{6,5},{7,6},{8,7},{9,8},{10,9},{11,1... | collective-permute-start | bytes 1572872 | tf_op jit(solution)/shard_map/ppermute | solution.py:389
  17.2 4.4 %collective-permute-start.4 = (f32[7,128,128]{2,1,0:T(8,128)}, f32[7,128,128]{2,1,0:T(8,128)}, u32[]{:S(2)}, u32[]{:S(2)}) collective-permute-start(f32[7,128,128]{2,1,0:T(8,128)} %get-tuple-element.22), channel_id=1, source_target_pairs={{0,16},{16,32},{32,48},{48,64},{64,80},{80,96},{96,112},{1,17},{17... | collective-permute-start | bytes 1376264 | tf_op jit(solution)/shard_map/ppermute | solution.py:389
  21.6 1.4 %collective-permute-done.rap = f32[10,128,128]{2,1,0:T(8,128)S(1)} collective-permute-done((f32[10,128,128]{2,1,0:T(8,128)S(1)}, f32[10,128,128]{2,1,0:T(8,128)S(1)}, u32[]{:S(2)}, u32[]{:S(2)}) %collective-permute-start) | collective-permute-done | bytes 655392 | tf_op jit(solution)/shard_map/ppermute | solution.py:389
  23.0 4.6 %collective-permute-start.5 = (f32[7,128,128]{2,1,0:T(8,128)S(1)}, f32[7,128,128]{2,1,0:T(8,128)}, u32[]{:S(2)}, u32[]{:S(2)}) collective-permute-start(f32[7,128,128]{2,1,0:T(8,128)S(1)} %get-tuple-element.23), channel_id=1, source_target_pairs={{16,0},{32,16},{48,32},{64,48},{80,64},{96,80},{112,96},{17,1},{33... | collective-permute-start | bytes 1376264 | tf_op jit(solution)/shard_map/ppermute | solution.py:389
  27.6 0.0 copy-done.6
  27.6 0.1 broadcast_in_dim.3
  27.7 0.1 convert_element_type.9.limits
  27.7 0.0 collective-permute-done.1.ram
  27.8 2.2 %relay.1 = (f32[10,128,128]{2,1,0:T(8,128)}, f32[10,128,128]{2,1,0:T(8,128)}) custom-call(f32[10,128,128]{2,1,0:T(8,128)S(1)} %collective-permute-done.rap, f32[10,128,128]{2,1,0:T(8,128)} %collective-permute-done.1.ram), custom_call_target="tpu_custom_call" | custom-call | tf_op jit(solution)/shard_map/relay/pallas_call | solution.py:98
  30.0 5.7 %collective-permute-start.6 = (f32[10,128,128]{2,1,0:T(8,128)}, f32[10,128,128]{2,1,0:T(8,128)}, u32[]{:S(2)}, u32[]{:S(2)}) collective-permute-start(f32[10,128,128]{2,1,0:T(8,128)} %get-tuple-element.29), channel_id=1, source_target_pairs={{0,16},{16,32},{32,48},{48,64},{64,80},{80,96},{96,112},{1,17},{17... | collective-permute-start | bytes 1966088 | tf_op jit(solution)/shard_map/ppermute | solution.py:389
  35.7 0.0 collective-permute-done.4.rxp
  35.7 1.9 %collective-permute-start.7 = (f32[10,128,128]{2,1,0:T(8,128)}, f32[10,128,128]{2,1,0:T(8,128)}, u32[]{:S(2)}, u32[]{:S(2)}) collective-permute-start(f32[10,128,128]{2,1,0:T(8,128)} %get-tuple-element.30), channel_id=1, source_target_pairs={{16,0},{32,16},{48,32},{64,48},{80,64},{96,80},{112,96},{17,1},{33... | collective-permute-start | bytes 1966088 | tf_op jit(solution)/shard_map/ppermute | solution.py:389
  37.6 0.0 collective-permute-done.5.rxm
  37.6 0.0 collective-permute-done.2.rbp
  37.6 1.0 %collective-permute-done.3.rbm = f32[8,128,128]{2,1,0:T(8,128)} collective-permute-done((f32[8,128,128]{2,1,0:T(8,128)}, f32[8,128,128]{2,1,0:T(8,128)}, u32[]{:S(2)}, u32[]{:S(2)}) %collective-permute-start.3) | collective-permute-done | bytes 524320 | tf_op jit(solution)/shard_map/ppermute | solution.py:389
  38.7 0.0 copy-done.3
  38.7 0.0 copy-done.1
  38.7 0.0 copy-done.5
  38.7 2.5 %prepare.1 = (bf16[2,3,128,1152]{3,2,1,0:T(8,128)(2,1)S(1)}, bf16[2,3,128,1152]{3,2,1,0:T(8,128)(2,1)S(1)}, bf16[2,128,768]{2,1,0:T(8,128)(2,1)S(1)}, bf16[2,128...) custom-call(f32[10,128,128]{2,1,0:T(8,128)S(1)} %collective-permute-done.rap, f32[10,128,128]{2,1,0:T(8,128)} %collective-permute-done.1.ram, ...), custom_call_target="tpu_custom_call" | custom-call | flops 999999995904 | bytes 1000000000 | tf_op jit(solution)/shard_map/prepare/pallas_call | solution.py:236
  41.2 2.3 %collective-permute-done.6.fxp = f32[10,128,128]{2,1,0:T(8,128)} collective-permute-done((f32[10,128,128]{2,1,0:T(8,128)}, f32[10,128,128]{2,1,0:T(8,128)}, u32[]{:S(2)}, u32[]{:S(2)}) %collective-permute-start.6) | collective-permute-done | bytes 655392 | tf_op jit(solution)/shard_map/ppermute | solution.py:389
  43.5 4.4 %collective-permute-done.7.fxm = f32[10,128,128]{2,1,0:T(8,128)} collective-permute-done((f32[10,128,128]{2,1,0:T(8,128)}, f32[10,128,128]{2,1,0:T(8,128)}, u32[]{:S(2)}, u32[]{:S(2)}) %collective-permute-start.7) | collective-permute-done | bytes 655392 | tf_op jit(solution)/shard_map/ppermute | solution.py:389
  47.9 14.5 %solve.1 = f32[2,1,9,128,128]{4,3,2,1,0:T(8,128)} custom-call(bf16[2,3,128,1152]{3,2,1,0:T(8,128)(2,1)S(1)} %get-tuple-element.24.middle_h, bf16[2,3,128,1152]{3,2,1,0:T(8,128)(2,1)S(1)} %get-tuple-element.25.middle_l, bf16[2,128,768]{2,1,0:T(8,128)(2,1)S(1)} %get-tuple-element.26.outer_h, bf16[2,128,768]{2,1,0:T(8,128)(2,1)S(1)} %get-tuple-element.27.outer_l, ...), custom_call_target="tpu_custom_call" | custom-call | tf_op jit(solution)/shard_map/solve/pallas_call | solution.py:366
  (1 shorter events, 0.0 us)
Async XLA Ops:
  0.0 1.3 %copy-start = (f32[2,1,9,128,128]{4,3,2,1,0:T(8,128)S(1)}, f32[2,1,9,128,128]{4,3,2,1,0:T(8,128)}, u32[]{:S(2)}) copy-start(f32[2,1,9,128,128]{4,3,2,1,0:T(8,128)} %blocks.3) | copy-start | bytes 3538948
  1.3 1.3 %copy-start.2 = (f32[2,1,9,128,128]{4,3,2,1,0:T(8,128)S(1)}, f32[2,1,9,128,128]{4,3,2,1,0:T(8,128)}, u32[]{:S(2)}) copy-start(f32[2,1,9,128,128]{4,3,2,1,0:T(8,128)} %rhs.3) | copy-start | bytes 3538948
  2.5 0.8 %copy-start.4 = (s32[2,1,9,8,8]{2,4,3,1,0:T(8,128)S(1)}, s32[2,1,9,8,8]{2,4,3,1,0:T(8,128)}, u32[]{:S(2)}) copy-start(s32[2,1,9,8,8]{2,4,3,1,0:T(8,128)} %param.5) | copy-start | bytes 13828
  3.4 24.2 %copy-start.6 = (s32[2,1,8]{2,1,0:T(1,128)S(1)}, s32[2,1,8]{2,1,0:T(1,128)}, u32[]{:S(2)}) copy-start(s32[2,1,8]{2,1,0:T(1,128)} %param.7) | copy-start | bytes 196
  3.4 35.3 %copy-start.3 = (f32[2,1,9,128,128]{4,3,2,1,0:T(8,128)S(1)}, f32[2,1,9,128,128]{4,3,2,1,0:T(8,128)}, u32[]{:S(2)}) copy-start(f32[2,1,9,128,128]{4,3,2,1,0:T(8,128)} %rhs.3) | copy-start | bytes 3538948
  5.1 33.6 %copy-start.1 = (f32[2,1,9,128,128]{4,3,2,1,0:T(8,128)S(1)}, f32[2,1,9,128,128]{4,3,2,1,0:T(8,128)}, u32[]{:S(2)}) copy-start(f32[2,1,9,128,128]{4,3,2,1,0:T(8,128)} %blocks.3) | copy-start | bytes 3538948
  5.1 33.6 %copy-start.5 = (s32[2,1,9,8,8]{2,4,3,1,0:T(8,128)S(1)}, s32[2,1,9,8,8]{2,4,3,1,0:T(8,128)}, u32[]{:S(2)}) copy-start(s32[2,1,9,8,8]{2,4,3,1,0:T(8,128)} %param.5) | copy-start | bytes 13828
  5.1 17.9 %collective-permute-start = (f32[10,128,128]{2,1,0:T(8,128)S(1)}, f32[10,128,128]{2,1,0:T(8,128)S(1)}, u32[]{:S(2)}, u32[]{:S(2)}) collective-permute-start(f32[10,128,128]{2,1,0:T(8,128)S(1)} %get-tuple-element.18), channel_id=1, source_target_pairs={{0,1},{1,2},{2,3},{3,4},{4,5},{5,6},{6,7},{7,8},{8,9},{9,10},{10,1... | collective-permute-start | bytes 1966088 | tf_op jit(solution)/shard_map/ppermute | solution.py:389
  9.6 18.1 %collective-permute-start.1 = (f32[10,128,128]{2,1,0:T(8,128)}, f32[10,128,128]{2,1,0:T(8,128)}, u32[]{:S(2)}, u32[]{:S(2)}) collective-permute-start(f32[10,128,128]{2,1,0:T(8,128)} %get-tuple-element.19), channel_id=1, source_target_pairs={{1,0},{2,1},{3,2},{4,3},{5,4},{6,5},{7,6},{8,7},{9,8},{10,9},{11,1... | collective-permute-start | bytes 1966088 | tf_op jit(solution)/shard_map/ppermute | solution.py:389
  10.9 26.7 %collective-permute-start.2 = (f32[8,128,128]{2,1,0:T(8,128)}, f32[8,128,128]{2,1,0:T(8,128)}, u32[]{:S(2)}, u32[]{:S(2)}) collective-permute-start(f32[8,128,128]{2,1,0:T(8,128)} %get-tuple-element.20), channel_id=1, source_target_pairs={{0,1},{1,2},{2,3},{3,4},{4,5},{5,6},{6,7},{7,8},{8,9},{9,10},{10,1... | collective-permute-start | bytes 1572872 | tf_op jit(solution)/shard_map/ppermute | solution.py:389
  15.9 22.8 %collective-permute-start.3 = (f32[8,128,128]{2,1,0:T(8,128)}, f32[8,128,128]{2,1,0:T(8,128)}, u32[]{:S(2)}, u32[]{:S(2)}) collective-permute-start(f32[8,128,128]{2,1,0:T(8,128)} %get-tuple-element.21), channel_id=1, source_target_pairs={{1,0},{2,1},{3,2},{4,3},{5,4},{6,5},{7,6},{8,7},{9,8},{10,9},{11,1... | collective-permute-start | bytes 1572872 | tf_op jit(solution)/shard_map/ppermute | solution.py:389
  17.2 18.5 %collective-permute-start.4 = (f32[7,128,128]{2,1,0:T(8,128)}, f32[7,128,128]{2,1,0:T(8,128)}, u32[]{:S(2)}, u32[]{:S(2)}) collective-permute-start(f32[7,128,128]{2,1,0:T(8,128)} %get-tuple-element.22), channel_id=1, source_target_pairs={{0,16},{16,32},{32,48},{48,64},{64,80},{80,96},{96,112},{1,17},{17... | collective-permute-start | bytes 1376264 | tf_op jit(solution)/shard_map/ppermute | solution.py:389
  23.0 14.6 %collective-permute-start.5 = (f32[7,128,128]{2,1,0:T(8,128)S(1)}, f32[7,128,128]{2,1,0:T(8,128)}, u32[]{:S(2)}, u32[]{:S(2)}) collective-permute-start(f32[7,128,128]{2,1,0:T(8,128)S(1)} %get-tuple-element.23), channel_id=1, source_target_pairs={{16,0},{32,16},{48,32},{64,48},{80,64},{96,80},{112,96},{17,1},{33... | collective-permute-start | bytes 1376264 | tf_op jit(solution)/shard_map/ppermute | solution.py:389
  30.0 13.5 %collective-permute-start.6 = (f32[10,128,128]{2,1,0:T(8,128)}, f32[10,128,128]{2,1,0:T(8,128)}, u32[]{:S(2)}, u32[]{:S(2)}) collective-permute-start(f32[10,128,128]{2,1,0:T(8,128)} %get-tuple-element.29), channel_id=1, source_target_pairs={{0,16},{16,32},{32,48},{48,64},{64,80},{80,96},{96,112},{1,17},{17... | collective-permute-start | bytes 1966088 | tf_op jit(solution)/shard_map/ppermute | solution.py:389
  35.7 12.2 %collective-permute-start.7 = (f32[10,128,128]{2,1,0:T(8,128)}, f32[10,128,128]{2,1,0:T(8,128)}, u32[]{:S(2)}, u32[]{:S(2)}) collective-permute-start(f32[10,128,128]{2,1,0:T(8,128)} %get-tuple-element.30), channel_id=1, source_target_pairs={{16,0},{32,16},{48,32},{64,48},{80,64},{96,80},{112,96},{17,1},{33... | collective-permute-start | bytes 1966088 | tf_op jit(solution)/shard_map/ppermute | solution.py:389

commit v4 on v3

--- a/solution.py
+++ b/solution.py
@@ -39,7 +39,7 @@
 OWN = {u: own_list(u) for u in (1, -1)}
 
 
-PACKED = (FIRST[1], FIRST[-1], SECOND[1], SECOND[-1], OWN[1], OWN[-1])
+PACKED = (FIRST[1], FIRST[-1], SECOND[1], SECOND[-1])
 
 
 def masked_blocks(mask, blocks):
@@ -63,16 +63,20 @@
             yield row, o, blocks[row, 0, o] * jnp.concatenate(rows, axis=0)
 
 
-def pack_kernel(mask, blocks, rhs, *sends):
+def place_blocks(mask, blocks, rhs, targets):
     for row, o, value in masked_blocks(mask, blocks):
-        for ref, entries in zip(sends, PACKED):
+        for ref, entries in targets:
             for place, listed in enumerate(entries):
                 if listed == (row, True, o):
                     ref[place] = value
-    for ref, entries in zip(sends, PACKED):
+    for ref, entries in targets:
         for place, (row, is_coupling, o) in enumerate(entries):
             if not is_coupling:
                 ref[place] = rhs[row, 0, o]
+
+
+def pack_kernel(mask, blocks, rhs, *sends):
+    place_blocks(mask, blocks, rhs, list(zip(sends, PACKED)))
 
 
 def pack(blocks, mask, rhs):
@@ -81,28 +85,29 @@
         pack_kernel,
         out_shape=out,
         in_specs=[pl.BlockSpec(memory_space=pltpu.VMEM)] + [pl.BlockSpec(memory_space=pltpu.VMEM)] * 2,
-        out_specs=[pl.BlockSpec(memory_space=pltpu.VMEM)] * 6,
+        out_specs=[pl.BlockSpec(memory_space=pltpu.VMEM)] * 4,
         compiler_params=pltpu.CompilerParams(vmem_limit_bytes=8 * 2**20),
         name="pack",
     )(mask, blocks, rhs)
 
 
-def relay_kernel(rap, ram, up, down):
-    up[:5] = rap[5:]
-    up[5:] = ram[5:]
-    down[:5] = rap[:5]
-    down[5:] = ram[:5]
-
-
-def relay(rap, ram):
+def relay_kernel(mask, blocks, rhs, rap, ram, up, down):
+    place_blocks(mask, blocks, rhs, [(up, OWN[1]), (down, OWN[-1])])
+    up[7:12] = rap[5:]
+    up[12:] = ram[5:]
+    down[7:12] = rap[:5]
+    down[12:] = ram[:5]
+
+
+def relay(*arrays):
     return pl.pallas_call(
         relay_kernel,
-        out_shape=[jax.ShapeDtypeStruct((10, B, B), F32)] * 2,
-        in_specs=[pl.BlockSpec(memory_space=pltpu.VMEM)] * 2,
+        out_shape=[jax.ShapeDtypeStruct((17, B, B), F32)] * 2,
+        in_specs=[pl.BlockSpec(memory_space=pltpu.VMEM)] * 5,
         out_specs=[pl.BlockSpec(memory_space=pltpu.VMEM)] * 2,
         compiler_params=pltpu.CompilerParams(vmem_limit_bytes=8 * 2**20),
         name="relay",
-    )(rap, ram)
+    )(*arrays)
 
 
 def split(value):
@@ -202,17 +207,13 @@
     return slice(place * B, (place + 1) * B)
 
 
-def prepare_kernel(rap, ram, rbp, rbm, rxp, rxm, mask, blocks, rhs, middle_h, middle_l, outer_h, outer_l, start):
+def prepare_kernel(rap, ram, rbp, rbm, mask, blocks, rhs, middle_h, middle_l, start):
     def put(h, c, is_coupling, o, value):
         if is_coupling:
             high, low = split(value)
             lanes = coupling_lanes(h, c, o)
-            if h in (1, 2):
-                middle_h[h - 1, c, :, lanes] = high
-                middle_l[h - 1, c, :, lanes] = low
-            else:
-                outer_h[h // 3, :, lanes] = high
-                outer_l[h // 3, :, lanes] = low
+            middle_h[h - 1, c, :, lanes] = high
+            middle_l[h - 1, c, :, lanes] = low
         else:
             g = h + o // 3 - 2
             if 0 <= g <= 1:
@@ -222,9 +223,6 @@
         for ref, entries in ((ref_a, FIRST[v]), (ref_b, SECOND[v])):
             for place, (row, is_coupling, o) in enumerate(entries):
                 put(row + 1, 1 - v, is_coupling, o, ref[place])
-    for u, ref in ((1, rxp), (-1, rxm)):
-        for place, (row, is_coupling, o) in enumerate(OWN[u]):
-            put(0 if u > 0 else 3, 1, is_coupling, o, ref[place])
     for row, o, value in masked_blocks(mask, blocks):
         put(row + 1, 1, True, o, value)
     for row, u in ((0, 0), (1, 0), (0, 1), (1, -1)):
@@ -232,36 +230,39 @@
 
 
 def prepare(*arrays):
-    shapes = [((2, 3, B, 9 * B), BF16)] * 2 + [((2, B, 6 * B), BF16)] * 2 + [((2, 9, B, B), F32)]
+    shapes = [((2, 3, B, 9 * B), BF16)] * 2 + [((2, 9, B, B), F32)]
     return pl.pallas_call(
         prepare_kernel,
         out_shape=[jax.ShapeDtypeStruct(*shape) for shape in shapes],
         in_specs=[pl.BlockSpec(memory_space=pltpu.VMEM)] * len(arrays),
         out_specs=[pl.BlockSpec(memory_space=pltpu.VMEM)] * len(shapes),
-        compiler_params=pltpu.CompilerParams(vmem_limit_bytes=16 * 2**20),
+        compiler_params=pltpu.CompilerParams(vmem_limit_bytes=12 * 2**20),
         cost_estimate=pl.CostEstimate(flops=10**12, bytes_accessed=10**9, transcendentals=10**9),
         name="prepare",
     )(*arrays)
 
 
 def solve_kernel(
-    middle_h, middle_l, outer_h, outer_l, start, fxp, fxm, limits, out, corner_h, corner_l, *scratch
+    middle_h, middle_l, start, fxp, fxm, limits, out, outer_h, outer_l, *scratch
 ):
     fields = (scratch[0:3], scratch[3:6])
     later = scratch[6:]
-    corners = {}
+    outer = {}
     for u, ref in ((1, fxp), (-1, fxm)):
+        h = 0 if u > 0 else 3
+        for place, (row, is_coupling, o) in enumerate(OWN[u]):
+            outer[h, 1, is_coupling, o] = (ref, place)
         part = 5 if u > 0 else 0
         for side, v in ((0, 1), (1, -1)):
             for place in range(5):
-                corners[0 if u > 0 else 3, 1 - v, *FIRST[v][part + place][1:]] = (ref, side * 5 + place)
+                outer[h, 1 - v, *FIRST[v][part + place][1:]] = (ref, 7 + side * 5 + place)
 
     def power(slot, g, m):
         if slot > 0:
             return later[slot - 1][g, m * B : (m + 1) * B, :]
         h, c = g + m // 3, m % 3
-        found = corners.get((h, c, False, off(1 - m // 3, 1 - c)))
-        if found is not None and h in (0, 3):
+        found = outer.get((h, c, False, off(1 - m // 3, 1 - c)))
+        if found is not None:
             return found[0][found[1]]
         return start[g, m]
 
@@ -281,11 +282,11 @@
         if slot < POWERS - 1:
             put_field(slot, g, h, c, value)
 
-    for (h, c, is_coupling, o), (ref, place) in corners.items():
+    for (h, c, is_coupling, o), (ref, place) in outer.items():
         if is_coupling:
             high, low = split(ref[place])
-            corner_h[h // 3, c // 2, :, coupling_lanes(h, c, o)] = high
-            corner_l[h // 3, c // 2, :, coupling_lanes(h, c, o)] = low
+            outer_h[h // 3, c, :, coupling_lanes(h, c, o)] = high
+            outer_l[h // 3, c, :, coupling_lanes(h, c, o)] = low
     for g in range(2):
         for m in range(9):
             put_field(0, g, g + m // 3, m % 3, power(0, g, m))
@@ -293,9 +294,7 @@
     def weights(h, c):
         if h in (1, 2):
             return middle_h.at[h - 1, c], middle_l.at[h - 1, c]
-        if c == 1:
-            return outer_h.at[h // 3], outer_l.at[h // 3]
-        return corner_h.at[h // 3, c // 2], corner_l.at[h // 3, c // 2]
+        return outer_h.at[h // 3, c], outer_l.at[h // 3, c]
 
     def apply(slot):
         for h in range(4):
@@ -369,13 +368,13 @@
         in_specs=[pl.BlockSpec(memory_space=pltpu.VMEM)] * len(arrays),
         out_specs=pl.BlockSpec(memory_space=pltpu.VMEM),
         scratch_shapes=[
-            pltpu.VMEM((2, 2, B, 4 * B), BF16),
-            pltpu.VMEM((2, 2, B, 4 * B), BF16),
+            pltpu.VMEM((2, 3, B, 6 * B), BF16),
+            pltpu.VMEM((2, 3, B, 6 * B), BF16),
             *fields,
             *fields,
             *[pltpu.VMEM((2, 9 * B, B), F32) for _ in range(POWERS - 1)],
         ],
-        compiler_params=pltpu.CompilerParams(vmem_limit_bytes=24 * 2**20),
+        compiler_params=pltpu.CompilerParams(vmem_limit_bytes=20 * 2**20),
         name="solve",
     )(*arrays)
 
@@ -391,17 +390,15 @@
 
 def shards(blocks, pair_mask, rhs_rows, counts):
     mask = jnp.transpose(pair_mask, (0, 1, 3, 4, 2)).reshape(-1, 9)
-    sap, sam, sbp, sbm, oxp, oxm = pack(blocks, mask, rhs_rows)
+    sap, sam, sbp, sbm = pack(blocks, mask, rhs_rows)
     rap = shift(sap, "gy", 1)
     ram = shift(sam, "gy", -1)
-    rxp = shift(oxp, "gx", 1)
-    rxm = shift(oxm, "gx", -1)
     rbp = shift(sbp, "gy", 1)
     rbm = shift(sbm, "gy", -1)
-    up, down = relay(rap, ram)
+    up, down = relay(mask, blocks, rhs_rows, rap, ram)
     fxp = shift(up, "gx", 1)
     fxm = shift(down, "gx", -1)
-    prepared = prepare(rap, ram, rbp, rbm, rxp, rxm, mask, blocks, rhs_rows)
+    prepared = prepare(rap, ram, rbp, rbm, mask, blocks, rhs_rows)
     orbitals = B // pair_mask.shape[-1]
     limits = jnp.repeat(counts, orbitals, axis=-1).reshape(2, B).astype(F32)
     return solve(*prepared, fxp, fxm, limits)

time: 62.9 us -> 68 us (1.081)
  waiting for transfers between devices: 9.2 us -> 23.2 us
  starting transfers between devices: 28.6 us -> 19.9 us
    ppermute x8 -> x6, waiting for transfers between devices: 9.2 us -> 23.2 us  [shift(): return lax.ppermute(value, axis, pairs)]
    ppermute x8 -> x6, starting transfers between devices: 28.6 us -> 19.9 us  [shift(): return lax.ppermute(value, axis, pairs)]
  transfers between devices with their start and end apart: 8 -> 6, of which waited for: 4 -> 5; matrix products, arithmetic and copies ran while one was open for 0% -> 0% of each run, Pallas kernels for 8% -> 7%
where the time goes in v4:
time: 68 us; the launch traced here: 67.6 us
  waiting for transfers between devices  23.2 us (34%)
  Pallas kernels  20.9 us (31%)
  starting transfers between devices  19.9 us (29%)
  local copies, waits for them, and re-layouts  3.55 us (5%)
    ppermute x6, waiting for transfers between devices, shift(): return lax.ppermute(value, axis, pairs)  23.2 us
    ppermute x6, starting transfers between devices, shift(): return lax.ppermute(value, axis, pairs)  19.9 us
    pallas_call x1, Pallas kernels, solve(): pl.pallas_call(solve_kernel, out_shape=jax.ShapeDtypeStruct((2, 1, 9, B,...  14.4 us
    unnamed x14, local copies, waits for them, and re-layouts  3.39 us
    pallas_call x1, Pallas kernels, relay(): pl.pallas_call(relay_kernel, out_shape=[jax.ShapeDtypeStruct((17, B, B),...  2.71 us
    pallas_call x1, Pallas kernels, prepare(): pl.pallas_call(prepare_kernel, out_shape=[jax.ShapeDtypeStruct(*shape) fo...  2.08 us
    pallas_call x1, Pallas kernels, pack(): pl.pallas_call(pack_kernel, out_shape=out, in_specs=[pl.BlockSpec(memory_...  1.71 us
  transfers between devices with their start and end apart: 6, of which 5 were waited for; matrix products, arithmetic and copies ran while one was open for 0% of the time, Pallas kernels for 7%

profile of v4, /device:TPU:1, one launch (start us, length us, event | category | flops | bytes accessed | tf_op | source)
XLA Modules:
  0.0 67.6 jit_solution(16971402042536666458)
XLA Ops:
  0.0 0.0 copy-start
  0.0 1.3 %copy-done = f32[2,1,9,128,128]{4,3,2,1,0:T(8,128)S(1)} copy-done((f32[2,1,9,128,128]{4,3,2,1,0:T(8,128)S(1)}, f32[2,1,9,128,128]{4,3,2,1,0:T(8,128)}, u32[]{:S(2)}) %copy-start) | copy-done | bytes 1179672
  1.3 0.0 copy-start.2
  1.3 1.3 %copy-done.2 = f32[2,1,9,128,128]{4,3,2,1,0:T(8,128)S(1)} copy-done((f32[2,1,9,128,128]{4,3,2,1,0:T(8,128)S(1)}, f32[2,1,9,128,128]{4,3,2,1,0:T(8,128)}, u32[]{:S(2)}) %copy-start.2) | copy-done | bytes 1179672
  2.5 0.0 copy-start.4
  2.5 0.8 %copy-done.4 = s32[2,1,9,8,8]{2,4,3,1,0:T(8,128)S(1)} copy-done((s32[2,1,9,8,8]{2,4,3,1,0:T(8,128)S(1)}, s32[2,1,9,8,8]{2,4,3,1,0:T(8,128)}, u32[]{:S(2)}) %copy-start.4) | copy-done | bytes 4632
  3.4 0.0 copy-start.6
  3.4 0.0 copy-start.1
  3.4 0.0 copy-start.3
  3.4 0.0 copy-start.5
  3.4 1.7 %pack.1 = (f32[10,128,128]{2,1,0:T(8,128)}, f32[10,128,128]{2,1,0:T(8,128)}, f32[8,128,128]{2,1,0:T(8,128)}, f32[8,128,128]{2,1,0:T(8,128)}) custom-call(s32[128,9]{1,0:T(8,128)S(1)} %bitcast.4, f32[2,1,9,128,128]{4,3,2,1,0:T(8,128)S(1)} %copy-done, f32[2,1,9,128,128]{4,3,2,1,0:T(8,128)S(1)} %copy-done.2), custom_call_target="tpu_custom_call" | custom-call | tf_op jit(solution)/shard_map/pack/pallas_call | solution.py:84
  5.1 4.4 %collective-permute-start = (f32[10,128,128]{2,1,0:T(8,128)}, f32[10,128,128]{2,1,0:T(8,128)S(1)}, u32[]{:S(2)}, u32[]{:S(2)}) collective-permute-start(f32[10,128,128]{2,1,0:T(8,128)} %get-tuple-element.14), channel_id=1, source_target_pairs={{0,1},{1,2},{2,3},{3,4},{4,5},{5,6},{6,7},{7,8},{8,9},{9,10},{10,1... | collective-permute-start | bytes 1966088 | tf_op jit(solution)/shard_map/ppermute | solution.py:388
  9.5 1.3 %collective-permute-start.1 = (f32[10,128,128]{2,1,0:T(8,128)}, f32[10,128,128]{2,1,0:T(8,128)}, u32[]{:S(2)}, u32[]{:S(2)}) collective-permute-start(f32[10,128,128]{2,1,0:T(8,128)} %get-tuple-element.15), channel_id=1, source_target_pairs={{1,0},{2,1},{3,2},{4,3},{5,4},{6,5},{7,6},{8,7},{9,8},{10,9},{11,1... | collective-permute-start | bytes 1966088 | tf_op jit(solution)/shard_map/ppermute | solution.py:388
  10.8 5.0 %collective-permute-start.2 = (f32[8,128,128]{2,1,0:T(8,128)}, f32[8,128,128]{2,1,0:T(8,128)}, u32[]{:S(2)}, u32[]{:S(2)}) collective-permute-start(f32[8,128,128]{2,1,0:T(8,128)} %get-tuple-element.16), channel_id=1, source_target_pairs={{0,1},{1,2},{2,3},{3,4},{4,5},{5,6},{6,7},{7,8},{8,9},{9,10},{10,1... | collective-permute-start | bytes 1572872 | tf_op jit(solution)/shard_map/ppermute | solution.py:388
  15.8 1.3 %collective-permute-start.3 = (f32[8,128,128]{2,1,0:T(8,128)}, f32[8,128,128]{2,1,0:T(8,128)}, u32[]{:S(2)}, u32[]{:S(2)}) collective-permute-start(f32[8,128,128]{2,1,0:T(8,128)} %get-tuple-element.17), channel_id=1, source_target_pairs={{1,0},{2,1},{3,2},{4,3},{5,4},{6,5},{7,6},{8,7},{9,8},{10,9},{11,1... | collective-permute-start | bytes 1572872 | tf_op jit(solution)/shard_map/ppermute | solution.py:388
  17.1 0.0 copy-done.6
  17.1 0.1 broadcast_in_dim.3
  17.2 0.1 convert_element_type.9.limits
  17.2 5.9 %collective-permute-done.rap = f32[10,128,128]{2,1,0:T(8,128)S(1)} collective-permute-done((f32[10,128,128]{2,1,0:T(8,128)}, f32[10,128,128]{2,1,0:T(8,128)S(1)}, u32[]{:S(2)}, u32[]{:S(2)}) %collective-permute-start) | collective-permute-done | bytes 655392 | tf_op jit(solution)/shard_map/ppermute | solution.py:388
  23.2 4.1 %collective-permute-done.1.ram = f32[10,128,128]{2,1,0:T(8,128)} collective-permute-done((f32[10,128,128]{2,1,0:T(8,128)}, f32[10,128,128]{2,1,0:T(8,128)}, u32[]{:S(2)}, u32[]{:S(2)}) %collective-permute-start.1) | collective-permute-done | bytes 655392 | tf_op jit(solution)/shard_map/ppermute | solution.py:388
  27.3 0.0 copy-done.1
  27.3 0.0 copy-done.3
  27.3 0.0 copy-done.5
  27.3 2.7 %relay.1 = (f32[17,128,128]{2,1,0:T(8,128)}, f32[17,128,128]{2,1,0:T(8,128)}) custom-call(s32[128,9]{1,0:T(8,128)S(1)} %bitcast.5, f32[2,1,9,128,128]{4,3,2,1,0:T(8,128)S(1)} %copy-done.1, f32[2,1,9,128,128]{4,3,2,1,0:T(8,128)S(1)} %copy-done.3, f32[10,128,128]{2,1,0:T(8,128)S(1)} %collective-permute-done.rap, f32[10,128,128]{2,1,0:T(8,128)} %collective-permute-done.1.ram), custom_call_target="tpu_custom_call" | custom-call | tf_op jit(solution)/shard_map/relay/pallas_call | solution.py:103
  30.0 6.0 %collective-permute-start.4 = (f32[17,128,128]{2,1,0:T(8,128)}, f32[17,128,128]{2,1,0:T(8,128)}, u32[]{:S(2)}, u32[]{:S(2)}) collective-permute-start(f32[17,128,128]{2,1,0:T(8,128)} %get-tuple-element.21), channel_id=1, source_target_pairs={{0,16},{16,32},{32,48},{48,64},{64,80},{80,96},{96,112},{1,17},{17... | collective-permute-start | bytes 3342344 | tf_op jit(solution)/shard_map/ppermute | solution.py:388
  36.0 1.9 %collective-permute-start.5 = (f32[17,128,128]{2,1,0:T(8,128)}, f32[17,128,128]{2,1,0:T(8,128)}, u32[]{:S(2)}, u32[]{:S(2)}) collective-permute-start(f32[17,128,128]{2,1,0:T(8,128)} %get-tuple-element.22), channel_id=1, source_target_pairs={{16,0},{32,16},{48,32},{64,48},{80,64},{96,80},{112,96},{17,1},{33... | collective-permute-start | bytes 3342344 | tf_op jit(solution)/shard_map/ppermute | solution.py:388
  38.0 0.0 collective-permute-done.2.rbp
  38.0 0.6 collective-permute-done.3.rbm
  38.6 2.1 %prepare.1 = (bf16[2,3,128,1152]{3,2,1,0:T(8,128)(2,1)S(1)}, bf16[2,3,128,1152]{3,2,1,0:T(8,128)(2,1)S(1)}, f32[2,9,128,128]{3,2,1,0:T(8,128)S(1)}) custom-call(f32[10,128,128]{2,1,0:T(8,128)S(1)} %collective-permute-done.rap, f32[10,128,128]{2,1,0:T(8,128)} %collective-permute-done.1.ram, f32[8,128,128]{2,1,0:T(8,128)} %collective-permute-done.2.rbp, ...), custom_call_target="tpu_custom_call" | custom-call | flops 999999995904 | bytes 1000000000 | tf_op jit(solution)/shard_map/prepare/pallas_call | solution.py:234
  40.6 8.1 %collective-permute-done.4.fxp = f32[17,128,128]{2,1,0:T(8,128)} collective-permute-done((f32[17,128,128]{2,1,0:T(8,128)}, f32[17,128,128]{2,1,0:T(8,128)}, u32[]{:S(2)}, u32[]{:S(2)}) %collective-permute-start.4) | collective-permute-done | bytes 1114144 | tf_op jit(solution)/shard_map/ppermute | solution.py:388
  48.8 4.4 %collective-permute-done.5.fxm = f32[17,128,128]{2,1,0:T(8,128)} collective-permute-done((f32[17,128,128]{2,1,0:T(8,128)}, f32[17,128,128]{2,1,0:T(8,128)}, u32[]{:S(2)}, u32[]{:S(2)}) %collective-permute-start.5) | collective-permute-done | bytes 1114144 | tf_op jit(solution)/shard_map/ppermute | solution.py:388
  53.2 14.4 %solve.1 = f32[2,1,9,128,128]{4,3,2,1,0:T(8,128)} custom-call(bf16[2,3,128,1152]{3,2,1,0:T(8,128)(2,1)S(1)} %get-tuple-element.18.middle_h, bf16[2,3,128,1152]{3,2,1,0:T(8,128)(2,1)S(1)} %get-tuple-element.19.middle_l, f32[2,9,128,128]{3,2,1,0:T(8,128)S(1)} %get-tuple-element.20.start, f32[17,128,128]{2,1,0:T(8,128)} %collective-permute-done.4.fxp, ...), custom_call_target="tpu_custom_call" | custom-call | tf_op jit(solution)/shard_map/solve/pallas_call | solution.py:365
  (1 shorter events, 0.0 us)
Async XLA Ops:
  0.0 1.3 %copy-start = (f32[2,1,9,128,128]{4,3,2,1,0:T(8,128)S(1)}, f32[2,1,9,128,128]{4,3,2,1,0:T(8,128)}, u32[]{:S(2)}) copy-start(f32[2,1,9,128,128]{4,3,2,1,0:T(8,128)} %blocks.5) | copy-start | bytes 3538948
  1.3 1.3 %copy-start.2 = (f32[2,1,9,128,128]{4,3,2,1,0:T(8,128)S(1)}, f32[2,1,9,128,128]{4,3,2,1,0:T(8,128)}, u32[]{:S(2)}) copy-start(f32[2,1,9,128,128]{4,3,2,1,0:T(8,128)} %rhs.5) | copy-start | bytes 3538948
  2.5 0.8 %copy-start.4 = (s32[2,1,9,8,8]{2,4,3,1,0:T(8,128)S(1)}, s32[2,1,9,8,8]{2,4,3,1,0:T(8,128)}, u32[]{:S(2)}) copy-start(s32[2,1,9,8,8]{2,4,3,1,0:T(8,128)} %param.5) | copy-start | bytes 13828
  3.4 13.7 %copy-start.6 = (s32[2,1,8]{2,1,0:T(1,128)S(1)}, s32[2,1,8]{2,1,0:T(1,128)}, u32[]{:S(2)}) copy-start(s32[2,1,8]{2,1,0:T(1,128)} %param.7) | copy-start | bytes 196
  3.4 23.9 %copy-start.1 = (f32[2,1,9,128,128]{4,3,2,1,0:T(8,128)S(1)}, f32[2,1,9,128,128]{4,3,2,1,0:T(8,128)}, u32[]{:S(2)}) copy-start(f32[2,1,9,128,128]{4,3,2,1,0:T(8,128)} %blocks.5) | copy-start | bytes 3538948
  3.4 23.9 %copy-start.3 = (f32[2,1,9,128,128]{4,3,2,1,0:T(8,128)S(1)}, f32[2,1,9,128,128]{4,3,2,1,0:T(8,128)}, u32[]{:S(2)}) copy-start(f32[2,1,9,128,128]{4,3,2,1,0:T(8,128)} %rhs.5) | copy-start | bytes 3538948
  3.4 23.9 %copy-start.5 = (s32[2,1,9,8,8]{2,4,3,1,0:T(8,128)S(1)}, s32[2,1,9,8,8]{2,4,3,1,0:T(8,128)}, u32[]{:S(2)}) copy-start(s32[2,1,9,8,8]{2,4,3,1,0:T(8,128)} %param.5) | copy-start | bytes 13828
  5.1 18.1 %collective-permute-start = (f32[10,128,128]{2,1,0:T(8,128)}, f32[10,128,128]{2,1,0:T(8,128)S(1)}, u32[]{:S(2)}, u32[]{:S(2)}) collective-permute-start(f32[10,128,128]{2,1,0:T(8,128)} %get-tuple-element.14), channel_id=1, source_target_pairs={{0,1},{1,2},{2,3},{3,4},{4,5},{5,6},{6,7},{7,8},{8,9},{9,10},{10,1... | collective-permute-start | bytes 1966088 | tf_op jit(solution)/shard_map/ppermute | solution.py:388
  9.5 17.8 %collective-permute-start.1 = (f32[10,128,128]{2,1,0:T(8,128)}, f32[10,128,128]{2,1,0:T(8,128)}, u32[]{:S(2)}, u32[]{:S(2)}) collective-permute-start(f32[10,128,128]{2,1,0:T(8,128)} %get-tuple-element.15), channel_id=1, source_target_pairs={{1,0},{2,1},{3,2},{4,3},{5,4},{6,5},{7,6},{8,7},{9,8},{10,9},{11,1... | collective-permute-start | bytes 1966088 | tf_op jit(solution)/shard_map/ppermute | solution.py:388
  10.8 27.2 %collective-permute-start.2 = (f32[8,128,128]{2,1,0:T(8,128)}, f32[8,128,128]{2,1,0:T(8,128)}, u32[]{:S(2)}, u32[]{:S(2)}) collective-permute-start(f32[8,128,128]{2,1,0:T(8,128)} %get-tuple-element.16), channel_id=1, source_target_pairs={{0,1},{1,2},{2,3},{3,4},{4,5},{5,6},{6,7},{7,8},{8,9},{9,10},{10,1... | collective-permute-start | bytes 1572872 | tf_op jit(solution)/shard_map/ppermute | solution.py:388
  15.8 22.8 %collective-permute-start.3 = (f32[8,128,128]{2,1,0:T(8,128)}, f32[8,128,128]{2,1,0:T(8,128)}, u32[]{:S(2)}, u32[]{:S(2)}) collective-permute-start(f32[8,128,128]{2,1,0:T(8,128)} %get-tuple-element.17), channel_id=1, source_target_pairs={{1,0},{2,1},{3,2},{4,3},{5,4},{6,5},{7,6},{8,7},{9,8},{10,9},{11,1... | collective-permute-start | bytes 1572872 | tf_op jit(solution)/shard_map/ppermute | solution.py:388
  30.0 18.7 %collective-permute-start.4 = (f32[17,128,128]{2,1,0:T(8,128)}, f32[17,128,128]{2,1,0:T(8,128)}, u32[]{:S(2)}, u32[]{:S(2)}) collective-permute-start(f32[17,128,128]{2,1,0:T(8,128)} %get-tuple-element.21), channel_id=1, source_target_pairs={{0,16},{16,32},{32,48},{48,64},{64,80},{80,96},{96,112},{1,17},{17... | collective-permute-start | bytes 3342344 | tf_op jit(solution)/shard_map/ppermute | solution.py:388
  36.0 17.1 %collective-permute-start.5 = (f32[17,128,128]{2,1,0:T(8,128)}, f32[17,128,128]{2,1,0:T(8,128)}, u32[]{:S(2)}, u32[]{:S(2)}) collective-permute-start(f32[17,128,128]{2,1,0:T(8,128)} %get-tuple-element.22), channel_id=1, source_target_pairs={{16,0},{32,16},{48,32},{64,48},{80,64},{96,80},{112,96},{17,1},{33... | collective-permute-start | bytes 3342344 | tf_op jit(solution)/shard_map/ppermute | solution.py:388

commit v5 on v3

--- a/solution.py
+++ b/solution.py
@@ -202,43 +202,63 @@
     return slice(place * B, (place + 1) * B)
 
 
-def prepare_kernel(rap, ram, rbp, rbm, rxp, rxm, mask, blocks, rhs, middle_h, middle_l, outer_h, outer_l, start):
+def prepare_kernel(rap, ram, rbp, rbm, above, mask, blocks, rhs, middle_h, middle_l, start):
     def put(h, c, is_coupling, o, value):
         if is_coupling:
             high, low = split(value)
             lanes = coupling_lanes(h, c, o)
-            if h in (1, 2):
-                middle_h[h - 1, c, :, lanes] = high
-                middle_l[h - 1, c, :, lanes] = low
-            else:
-                outer_h[h // 3, :, lanes] = high
-                outer_l[h // 3, :, lanes] = low
+            middle_h[h - 1, c, :, lanes] = high
+            middle_l[h - 1, c, :, lanes] = low
         else:
             g = h + o // 3 - 2
             if 0 <= g <= 1:
                 start[g, 3 * (h - g) + c] = value
 
+    start[0, 1] = above[0]
+    start[1, 7] = above[1]
     for v, ref_a, ref_b in ((1, rap, rbp), (-1, ram, rbm)):
         for ref, entries in ((ref_a, FIRST[v]), (ref_b, SECOND[v])):
             for place, (row, is_coupling, o) in enumerate(entries):
                 put(row + 1, 1 - v, is_coupling, o, ref[place])
-    for u, ref in ((1, rxp), (-1, rxm)):
-        for place, (row, is_coupling, o) in enumerate(OWN[u]):
-            put(0 if u > 0 else 3, 1, is_coupling, o, ref[place])
     for row, o, value in masked_blocks(mask, blocks):
         put(row + 1, 1, True, o, value)
     for row, u in ((0, 0), (1, 0), (0, 1), (1, -1)):
         put(row + 1, 1, False, off(u, 0), rhs[row, 0, off(u, 0)])
 
 
+def outer_kernel(rxp, rxm, outer_h, outer_l, right):
+    for u, ref in ((1, rxp), (-1, rxm)):
+        h = 0 if u > 0 else 3
+        for place, (row, is_coupling, o) in enumerate(OWN[u]):
+            if is_coupling:
+                high, low = split(ref[place])
+                outer_h[h // 3, :, coupling_lanes(h, 1, o)] = high
+                outer_l[h // 3, :, coupling_lanes(h, 1, o)] = low
+            else:
+                right[h // 3] = ref[place]
+
+
+def outer(*arrays):
+    shapes = [((2, B, 6 * B), BF16)] * 2 + [((2, B, B), F32)]
+    return pl.pallas_call(
+        outer_kernel,
+        out_shape=[jax.ShapeDtypeStruct(*shape) for shape in shapes],
+        in_specs=[pl.BlockSpec(memory_space=pltpu.VMEM)] * len(arrays),
+        out_specs=[pl.BlockSpec(memory_space=pltpu.VMEM)] * len(shapes),
+        compiler_params=pltpu.CompilerParams(vmem_limit_bytes=8 * 2**20),
+        cost_estimate=pl.CostEstimate(flops=10**9, bytes_accessed=10**6, transcendentals=0),
+        name="outer",
+    )(*arrays)
+
+
 def prepare(*arrays):
-    shapes = [((2, 3, B, 9 * B), BF16)] * 2 + [((2, B, 6 * B), BF16)] * 2 + [((2, 9, B, B), F32)]
+    shapes = [((2, 3, B, 9 * B), BF16)] * 2 + [((2, 9, B, B), F32)]
     return pl.pallas_call(
         prepare_kernel,
         out_shape=[jax.ShapeDtypeStruct(*shape) for shape in shapes],
         in_specs=[pl.BlockSpec(memory_space=pltpu.VMEM)] * len(arrays),
         out_specs=[pl.BlockSpec(memory_space=pltpu.VMEM)] * len(shapes),
-        compiler_params=pltpu.CompilerParams(vmem_limit_bytes=16 * 2**20),
+        compiler_params=pltpu.CompilerParams(vmem_limit_bytes=12 * 2**20),
         cost_estimate=pl.CostEstimate(flops=10**12, bytes_accessed=10**9, transcendentals=10**9),
         name="prepare",
     )(*arrays)
@@ -375,7 +395,7 @@
             *fields,
             *[pltpu.VMEM((2, 9 * B, B), F32) for _ in range(POWERS - 1)],
         ],
-        compiler_params=pltpu.CompilerParams(vmem_limit_bytes=24 * 2**20),
+        compiler_params=pltpu.CompilerParams(vmem_limit_bytes=20 * 2**20),
         name="solve",
     )(*arrays)
 
@@ -401,10 +421,11 @@
     up, down = relay(rap, ram)
     fxp = shift(up, "gx", 1)
     fxm = shift(down, "gx", -1)
-    prepared = prepare(rap, ram, rbp, rbm, rxp, rxm, mask, blocks, rhs_rows)
+    outer_h, outer_l, above = outer(rxp, rxm)
+    middle_h, middle_l, start = prepare(rap, ram, rbp, rbm, above, mask, blocks, rhs_rows)
     orbitals = B // pair_mask.shape[-1]
     limits = jnp.repeat(counts, orbitals, axis=-1).reshape(2, B).astype(F32)
-    return solve(*prepared, fxp, fxm, limits)
+    return solve(middle_h, middle_l, outer_h, outer_l, start, fxp, fxm, limits)
 
 
 def solution(mesh):

time: 62.9 us -> 62 us (0.986)
  starting transfers between devices: 28.6 us -> 22.7 us
  waiting for transfers between devices: 9.2 us -> 13.7 us
  local copies, waits for them, and re-layouts: 3.55 us -> 5.35 us
  Pallas kernels: 20.9 us -> 19.6 us
    ppermute x8, starting transfers between devices: 28.6 us -> 22.7 us  [shift(): return lax.ppermute(value, axis, pairs)]
    ppermute x8, waiting for transfers between devices: 9.2 us -> 13.7 us  [shift(): return lax.ppermute(value, axis, pairs)]
    unnamed x14 -> x18, local copies, waits for them, and re-layouts: 3.39 us -> 5.19 us
    pallas_call x0 -> x1, Pallas kernels: none -> 1.25 us  [outer(): pl.pallas_call(outer_kernel, out_shape=[jax.ShapeDtypeStruct(*shape) for...]
    pallas_call x1, Pallas kernels: 2.23 us -> 1.15 us  [relay(): pl.pallas_call(relay_kernel, out_shape=[jax.ShapeDtypeStruct((10, B, B),...]
  transfers between devices with their start and end apart: 8 -> 8, of which waited for: 4 -> 5; matrix products, arithmetic and copies ran while one was open for 0% -> 0% of each run, Pallas kernels for 8% -> 7%
where the time goes in v5:
time: 62 us; the launch traced here: 61.5 us
  starting transfers between devices  22.7 us (37%)
  Pallas kernels  19.6 us (32%)
  waiting for transfers between devices  13.7 us (22%)
  local copies, waits for them, and re-layouts  5.35 us (9%)
    ppermute x8, starting transfers between devices, shift(): return lax.ppermute(value, axis, pairs)  22.7 us
    pallas_call x1, Pallas kernels, solve(): pl.pallas_call(solve_kernel, out_shape=jax.ShapeDtypeStruct((2, 1, 9, B,...  14 us
    ppermute x8, waiting for transfers between devices, shift(): return lax.ppermute(value, axis, pairs)  13.7 us
    unnamed x18, local copies, waits for them, and re-layouts  5.19 us
    pallas_call x1, Pallas kernels, prepare(): pl.pallas_call(prepare_kernel, out_shape=[jax.ShapeDtypeStruct(*shape) fo...  1.89 us
    pallas_call x1, Pallas kernels, pack(): pl.pallas_call(pack_kernel, out_shape=out, in_specs=[pl.BlockSpec(memory_...  1.31 us
    pallas_call x1, Pallas kernels, outer(): pl.pallas_call(outer_kernel, out_shape=[jax.ShapeDtypeStruct(*shape) for...  1.25 us
  transfers between devices with their start and end apart: 8, of which 5 were waited for; matrix products, arithmetic and copies ran while one was open for 0% of the time, Pallas kernels for 7%

profile of v5, /device:TPU:1, one launch (start us, length us, event | category | flops | bytes accessed | tf_op | source)
XLA Modules:
  0.0 61.5 jit_solution(382874321873892550)
XLA Ops:
  0.0 0.0 copy-start
  0.0 1.3 %copy-done = f32[2,1,9,128,128]{4,3,2,1,0:T(8,128)S(1)} copy-done((f32[2,1,9,128,128]{4,3,2,1,0:T(8,128)S(1)}, f32[2,1,9,128,128]{4,3,2,1,0:T(8,128)}, u32[]{:S(2)}) %copy-start) | copy-done | bytes 1179672
  1.3 0.0 copy-start.2
  1.3 1.3 %copy-done.2 = f32[2,1,9,128,128]{4,3,2,1,0:T(8,128)S(1)} copy-done((f32[2,1,9,128,128]{4,3,2,1,0:T(8,128)S(1)}, f32[2,1,9,128,128]{4,3,2,1,0:T(8,128)}, u32[]{:S(2)}) %copy-start.2) | copy-done | bytes 1179672
  2.5 0.0 copy-start.4
  2.5 0.8 %copy-done.4 = s32[2,1,9,8,8]{2,4,3,1,0:T(8,128)S(1)} copy-done((s32[2,1,9,8,8]{2,4,3,1,0:T(8,128)S(1)}, s32[2,1,9,8,8]{2,4,3,1,0:T(8,128)}, u32[]{:S(2)}) %copy-start.4) | copy-done | bytes 4632
  3.4 0.0 copy-start.8
  3.4 1.3 %pack.1 = (f32[10,128,128]{2,1,0:T(8,128)S(1)}, f32[10,128,128]{2,1,0:T(8,128)S(1)}, f32[8,128,128]{2,1,0:T(8,128)}, f32[8,128,128]{2,1,0:T(8,128)S(1)}, f32[7,1...) custom-call(s32[128,9]{1,0:T(8,128)S(1)} %bitcast.4, f32[2,1,9,128,128]{4,3,2,1,0:T(8,128)S(1)} %copy-done, ...), custom_call_target="tpu_custom_call" | custom-call | tf_op jit(solution)/shard_map/pack/pallas_call | solution.py:80
  4.7 4.5 %collective-permute-start.4 = (f32[7,128,128]{2,1,0:T(8,128)S(1)}, f32[7,128,128]{2,1,0:T(8,128)S(1)}, u32[]{:S(2)}, u32[]{:S(2)}) collective-permute-start(f32[7,128,128]{2,1,0:T(8,128)S(1)} %get-tuple-element.23), channel_id=1, source_target_pairs={{0,16},{16,32},{32,48},{48,64},{64,80},{80,96},{96,112},{1,17},{17... | collective-permute-start | bytes 1376264 | tf_op jit(solution)/shard_map/ppermute | solution.py:409
  9.2 3.6 %collective-permute-start = (f32[10,128,128]{2,1,0:T(8,128)S(1)}, f32[10,128,128]{2,1,0:T(8,128)S(1)}, u32[]{:S(2)}, u32[]{:S(2)}) collective-permute-start(f32[10,128,128]{2,1,0:T(8,128)S(1)} %get-tuple-element.19), channel_id=1, source_target_pairs={{0,1},{1,2},{2,3},{3,4},{4,5},{5,6},{6,7},{7,8},{8,9},{9,10},{10,1... | collective-permute-start | bytes 1966088 | tf_op jit(solution)/shard_map/ppermute | solution.py:409
  12.8 1.3 %collective-permute-start.1 = (f32[10,128,128]{2,1,0:T(8,128)S(1)}, f32[10,128,128]{2,1,0:T(8,128)S(1)}, u32[]{:S(2)}, u32[]{:S(2)}) collective-permute-start(f32[10,128,128]{2,1,0:T(8,128)S(1)} %get-tuple-element.20), channel_id=1, source_target_pairs={{1,0},{2,1},{3,2},{4,3},{5,4},{6,5},{7,6},{8,7},{9,8},{10,9},{11,1... | collective-permute-start | bytes 1966088 | tf_op jit(solution)/shard_map/ppermute | solution.py:409
  14.1 1.9 %collective-permute-start.5 = (f32[7,128,128]{2,1,0:T(8,128)}, f32[7,128,128]{2,1,0:T(8,128)}, u32[]{:S(2)}, u32[]{:S(2)}) collective-permute-start(f32[7,128,128]{2,1,0:T(8,128)} %get-tuple-element.24), channel_id=1, source_target_pairs={{16,0},{32,16},{48,32},{64,48},{80,64},{96,80},{112,96},{17,1},{33... | collective-permute-start | bytes 1376264 | tf_op jit(solution)/shard_map/ppermute | solution.py:409
  16.0 5.0 %collective-permute-start.2 = (f32[8,128,128]{2,1,0:T(8,128)}, f32[8,128,128]{2,1,0:T(8,128)}, u32[]{:S(2)}, u32[]{:S(2)}) collective-permute-start(f32[8,128,128]{2,1,0:T(8,128)} %get-tuple-element.21), channel_id=1, source_target_pairs={{0,1},{1,2},{2,3},{3,4},{4,5},{5,6},{6,7},{7,8},{8,9},{9,10},{10,1... | collective-permute-start | bytes 1572872 | tf_op jit(solution)/shard_map/ppermute | solution.py:409
  21.0 0.0 collective-permute-done.4.rxp
  21.0 0.0 copy-start.6
  21.0 0.8 %copy-done.6 = f32[7,128,128]{2,1,0:T(8,128)} copy-done((f32[7,128,128]{2,1,0:T(8,128)}, f32[7,128,128]{2,1,0:T(8,128)S(1)}, u32[]{:S(2)}) %copy-start.6) | copy-done | bytes 458776
  21.8 1.3 %collective-permute-start.3 = (f32[8,128,128]{2,1,0:T(8,128)S(1)}, f32[8,128,128]{2,1,0:T(8,128)}, u32[]{:S(2)}, u32[]{:S(2)}) collective-permute-start(f32[8,128,128]{2,1,0:T(8,128)S(1)} %get-tuple-element.22), channel_id=1, source_target_pairs={{1,0},{2,1},{3,2},{4,3},{5,4},{6,5},{7,6},{8,7},{9,8},{10,9},{11,1... | collective-permute-start | bytes 1572872 | tf_op jit(solution)/shard_map/ppermute | solution.py:409
  23.0 0.0 copy-done.8
  23.1 0.1 broadcast_in_dim.3
  23.1 0.1 convert_element_type.9.limits
  23.2 1.2 %collective-permute-done.5.rxm = f32[7,128,128]{2,1,0:T(8,128)} collective-permute-done((f32[7,128,128]{2,1,0:T(8,128)}, f32[7,128,128]{2,1,0:T(8,128)}, u32[]{:S(2)}, u32[]{:S(2)}) %collective-permute-start.5) | collective-permute-done | bytes 458784 | tf_op jit(solution)/shard_map/ppermute | solution.py:409
  24.4 0.0 copy-start.7
  24.4 1.0 %copy-done.7 = f32[7,128,128]{2,1,0:T(8,128)S(1)} copy-done((f32[7,128,128]{2,1,0:T(8,128)S(1)}, f32[7,128,128]{2,1,0:T(8,128)}, u32[]{:S(2)}) %copy-start.7) | copy-done | bytes 458776
  25.4 0.0 copy-start.3
  25.4 1.2 %outer.1 = (bf16[2,128,768]{2,1,0:T(8,128)(2,1)S(1)}, bf16[2,128,768]{2,1,0:T(8,128)(2,1)S(1)}, f32[2,128,128]{2,1,0:T(8,128)S(1)}) custom-call(f32[7,128,128]{2,1,0:T(8,128)S(1)} %copy-done.7, f32[7,128,128]{2,1,0:T(8,128)} %collective-permute-done.5.rxm), custom_call_target="tpu_custom_call" | custom-call | flops 1000000000 | bytes 1000000 | tf_op jit(solution)/shard_map/outer/pallas_call | solution.py:243
  26.7 0.0 copy-start.1
  26.7 0.0 copy-start.5
  26.7 0.6 collective-permute-done.rap
  27.2 4.4 %collective-permute-done.1.ram = f32[10,128,128]{2,1,0:T(8,128)S(1)} collective-permute-done((f32[10,128,128]{2,1,0:T(8,128)S(1)}, f32[10,128,128]{2,1,0:T(8,128)S(1)}, u32[]{:S(2)}, u32[]{:S(2)}) %collective-permute-start.1) | collective-permute-done | bytes 655392 | tf_op jit(solution)/shard_map/ppermute | solution.py:409
  31.6 1.1 %relay.1 = (f32[10,128,128]{2,1,0:T(8,128)}, f32[10,128,128]{2,1,0:T(8,128)}) custom-call(f32[10,128,128]{2,1,0:T(8,128)S(1)} %collective-permute-done.rap, f32[10,128,128]{2,1,0:T(8,128)S(1)} %collective-permute-done.1.ram), custom_call_target="tpu_custom_call" | custom-call | tf_op jit(solution)/shard_map/relay/pallas_call | solution.py:98
  32.8 2.4 %collective-permute-start.6 = (f32[10,128,128]{2,1,0:T(8,128)}, f32[10,128,128]{2,1,0:T(8,128)}, u32[]{:S(2)}, u32[]{:S(2)}) collective-permute-start(f32[10,128,128]{2,1,0:T(8,128)} %get-tuple-element.31), channel_id=1, source_target_pairs={{0,16},{16,32},{32,48},{48,64},{64,80},{80,96},{96,112},{1,17},{17... | collective-permute-start | bytes 1966088 | tf_op jit(solution)/shard_map/ppermute | solution.py:409
  35.2 2.7 %collective-permute-start.7 = (f32[10,128,128]{2,1,0:T(8,128)}, f32[10,128,128]{2,1,0:T(8,128)}, u32[]{:S(2)}, u32[]{:S(2)}) collective-permute-start(f32[10,128,128]{2,1,0:T(8,128)} %get-tuple-element.32), channel_id=1, source_target_pairs={{16,0},{32,16},{48,32},{64,48},{80,64},{96,80},{112,96},{17,1},{33... | collective-permute-start | bytes 1966088 | tf_op jit(solution)/shard_map/ppermute | solution.py:409
  38.0 0.0 collective-permute-done.2.rbp
  38.0 4.0 %collective-permute-done.3.rbm = f32[8,128,128]{2,1,0:T(8,128)} collective-permute-done((f32[8,128,128]{2,1,0:T(8,128)S(1)}, f32[8,128,128]{2,1,0:T(8,128)}, u32[]{:S(2)}, u32[]{:S(2)}) %collective-permute-start.3) | collective-permute-done | bytes 524320 | tf_op jit(solution)/shard_map/ppermute | solution.py:409
  42.0 0.0 copy-done.3
  42.0 0.0 copy-done.1
  42.0 0.0 copy-done.5
  42.0 1.9 %prepare.1 = (bf16[2,3,128,1152]{3,2,1,0:T(8,128)(2,1)S(1)}, bf16[2,3,128,1152]{3,2,1,0:T(8,128)(2,1)S(1)}, f32[2,9,128,128]{3,2,1,0:T(8,128)S(1)}) custom-call(f32[10,128,128]{2,1,0:T(8,128)S(1)} %collective-permute-done.rap, f32[10,128,128]{2,1,0:T(8,128)S(1)} %collective-permute-done.1.ram, f32[8,128,128]{2,1,0:T(8,128)} %collective-permute-done.2.rbp, ...), custom_call_target="tpu_custom_call" | custom-call | flops 999999995904 | bytes 1000000000 | tf_op jit(solution)/shard_map/prepare/pallas_call | solution.py:256
  43.9 0.0 collective-permute-done.6.fxp
  43.9 3.5 %collective-permute-done.7.fxm = f32[10,128,128]{2,1,0:T(8,128)} collective-permute-done((f32[10,128,128]{2,1,0:T(8,128)}, f32[10,128,128]{2,1,0:T(8,128)}, u32[]{:S(2)}, u32[]{:S(2)}) %collective-permute-start.7) | collective-permute-done | bytes 655392 | tf_op jit(solution)/shard_map/ppermute | solution.py:409
  47.4 14.0 %solve.1 = f32[2,1,9,128,128]{4,3,2,1,0:T(8,128)} custom-call(bf16[2,3,128,1152]{3,2,1,0:T(8,128)(2,1)S(1)} %get-tuple-element.26.middle_h, bf16[2,3,128,1152]{3,2,1,0:T(8,128)(2,1)S(1)} %get-tuple-element.27.middle_l, bf16[2,128,768]{2,1,0:T(8,128)(2,1)S(1)} %get-tuple-element.28.outer_h, bf16[2,128,768]{2,1,0:T(8,128)(2,1)S(1)} %get-tuple-element.29.outer_l, ...), custom_call_target="tpu_custom_call" | custom-call | tf_op jit(solution)/shard_map/solve/pallas_call | solution.py:386
  (1 shorter events, 0.0 us)
Async XLA Ops:
  0.0 1.3 %copy-start = (f32[2,1,9,128,128]{4,3,2,1,0:T(8,128)S(1)}, f32[2,1,9,128,128]{4,3,2,1,0:T(8,128)}, u32[]{:S(2)}) copy-start(f32[2,1,9,128,128]{4,3,2,1,0:T(8,128)} %blocks.3) | copy-start | bytes 3538948
  1.3 1.3 %copy-start.2 = (f32[2,1,9,128,128]{4,3,2,1,0:T(8,128)S(1)}, f32[2,1,9,128,128]{4,3,2,1,0:T(8,128)}, u32[]{:S(2)}) copy-start(f32[2,1,9,128,128]{4,3,2,1,0:T(8,128)} %rhs.3) | copy-start | bytes 3538948
  2.5 0.8 %copy-start.4 = (s32[2,1,9,8,8]{2,4,3,1,0:T(8,128)S(1)}, s32[2,1,9,8,8]{2,4,3,1,0:T(8,128)}, u32[]{:S(2)}) copy-start(s32[2,1,9,8,8]{2,4,3,1,0:T(8,128)} %param.5) | copy-start | bytes 13828
  3.4 19.7 %copy-start.8 = (s32[2,1,8]{2,1,0:T(1,128)S(1)}, s32[2,1,8]{2,1,0:T(1,128)}, u32[]{:S(2)}) copy-start(s32[2,1,8]{2,1,0:T(1,128)} %param.7) | copy-start | bytes 196
  4.7 16.3 %collective-permute-start.4 = (f32[7,128,128]{2,1,0:T(8,128)S(1)}, f32[7,128,128]{2,1,0:T(8,128)S(1)}, u32[]{:S(2)}, u32[]{:S(2)}) collective-permute-start(f32[7,128,128]{2,1,0:T(8,128)S(1)} %get-tuple-element.23), channel_id=1, source_target_pairs={{0,16},{16,32},{32,48},{48,64},{64,80},{80,96},{96,112},{1,17},{17... | collective-permute-start | bytes 1376264 | tf_op jit(solution)/shard_map/ppermute | solution.py:409
  9.2 18.0 %collective-permute-start = (f32[10,128,128]{2,1,0:T(8,128)S(1)}, f32[10,128,128]{2,1,0:T(8,128)S(1)}, u32[]{:S(2)}, u32[]{:S(2)}) collective-permute-start(f32[10,128,128]{2,1,0:T(8,128)S(1)} %get-tuple-element.19), channel_id=1, source_target_pairs={{0,1},{1,2},{2,3},{3,4},{4,5},{5,6},{6,7},{7,8},{8,9},{9,10},{10,1... | collective-permute-start | bytes 1966088 | tf_op jit(solution)/shard_map/ppermute | solution.py:409
  12.8 18.8 %collective-permute-start.1 = (f32[10,128,128]{2,1,0:T(8,128)S(1)}, f32[10,128,128]{2,1,0:T(8,128)S(1)}, u32[]{:S(2)}, u32[]{:S(2)}) collective-permute-start(f32[10,128,128]{2,1,0:T(8,128)S(1)} %get-tuple-element.20), channel_id=1, source_target_pairs={{1,0},{2,1},{3,2},{4,3},{5,4},{6,5},{7,6},{8,7},{9,8},{10,9},{11,1... | collective-permute-start | bytes 1966088 | tf_op jit(solution)/shard_map/ppermute | solution.py:409
  14.1 10.3 %collective-permute-start.5 = (f32[7,128,128]{2,1,0:T(8,128)}, f32[7,128,128]{2,1,0:T(8,128)}, u32[]{:S(2)}, u32[]{:S(2)}) collective-permute-start(f32[7,128,128]{2,1,0:T(8,128)} %get-tuple-element.24), channel_id=1, source_target_pairs={{16,0},{32,16},{48,32},{64,48},{80,64},{96,80},{112,96},{17,1},{33... | collective-permute-start | bytes 1376264 | tf_op jit(solution)/shard_map/ppermute | solution.py:409
  16.0 21.9 %collective-permute-start.2 = (f32[8,128,128]{2,1,0:T(8,128)}, f32[8,128,128]{2,1,0:T(8,128)}, u32[]{:S(2)}, u32[]{:S(2)}) collective-permute-start(f32[8,128,128]{2,1,0:T(8,128)} %get-tuple-element.21), channel_id=1, source_target_pairs={{0,1},{1,2},{2,3},{3,4},{4,5},{5,6},{6,7},{7,8},{8,9},{9,10},{10,1... | collective-permute-start | bytes 1572872 | tf_op jit(solution)/shard_map/ppermute | solution.py:409
  21.0 0.8 %copy-start.6 = (f32[7,128,128]{2,1,0:T(8,128)}, f32[7,128,128]{2,1,0:T(8,128)S(1)}, u32[]{:S(2)}) copy-start(f32[7,128,128]{2,1,0:T(8,128)S(1)} %collective-permute-done.4.rxp) | copy-start | bytes 1376260
  21.8 20.2 %collective-permute-start.3 = (f32[8,128,128]{2,1,0:T(8,128)S(1)}, f32[8,128,128]{2,1,0:T(8,128)}, u32[]{:S(2)}, u32[]{:S(2)}) collective-permute-start(f32[8,128,128]{2,1,0:T(8,128)S(1)} %get-tuple-element.22), channel_id=1, source_target_pairs={{1,0},{2,1},{3,2},{4,3},{5,4},{6,5},{7,6},{8,7},{9,8},{10,9},{11,1... | collective-permute-start | bytes 1572872 | tf_op jit(solution)/shard_map/ppermute | solution.py:409
  24.4 1.0 %copy-start.7 = (f32[7,128,128]{2,1,0:T(8,128)S(1)}, f32[7,128,128]{2,1,0:T(8,128)}, u32[]{:S(2)}) copy-start(f32[7,128,128]{2,1,0:T(8,128)} %copy-done.6) | copy-start | bytes 1376260
  25.4 16.6 %copy-start.3 = (f32[2,1,9,128,128]{4,3,2,1,0:T(8,128)S(1)}, f32[2,1,9,128,128]{4,3,2,1,0:T(8,128)}, u32[]{:S(2)}) copy-start(f32[2,1,9,128,128]{4,3,2,1,0:T(8,128)} %rhs.3) | copy-start | bytes 3538948
  26.7 15.3 %copy-start.1 = (f32[2,1,9,128,128]{4,3,2,1,0:T(8,128)S(1)}, f32[2,1,9,128,128]{4,3,2,1,0:T(8,128)}, u32[]{:S(2)}) copy-start(f32[2,1,9,128,128]{4,3,2,1,0:T(8,128)} %blocks.3) | copy-start | bytes 3538948
  26.7 15.3 %copy-start.5 = (s32[2,1,9,8,8]{2,4,3,1,0:T(8,128)S(1)}, s32[2,1,9,8,8]{2,4,3,1,0:T(8,128)}, u32[]{:S(2)}) copy-start(s32[2,1,9,8,8]{2,4,3,1,0:T(8,128)} %param.5) | copy-start | bytes 13828
  32.8 11.1 %collective-permute-start.6 = (f32[10,128,128]{2,1,0:T(8,128)}, f32[10,128,128]{2,1,0:T(8,128)}, u32[]{:S(2)}, u32[]{:S(2)}) collective-permute-start(f32[10,128,128]{2,1,0:T(8,128)} %get-tuple-element.31), channel_id=1, source_target_pairs={{0,16},{16,32},{32,48},{48,64},{64,80},{80,96},{96,112},{1,17},{17... | collective-permute-start | bytes 1966088 | tf_op jit(solution)/shard_map/ppermute | solution.py:409
  35.2 12.2 %collective-permute-start.7 = (f32[10,128,128]{2,1,0:T(8,128)}, f32[10,128,128]{2,1,0:T(8,128)}, u32[]{:S(2)}, u32[]{:S(2)}) collective-permute-start(f32[10,128,128]{2,1,0:T(8,128)} %get-tuple-element.32), channel_id=1, source_target_pairs={{16,0},{32,16},{48,32},{64,48},{80,64},{96,80},{112,96},{17,1},{33... | collective-permute-start | bytes 1966088 | tf_op jit(solution)/shard_map/ppermute | solution.py:409

commit v6 on v5

--- a/solution.py
+++ b/solution.py
@@ -8,6 +8,7 @@
 ITERS = 3
 B = 128
 POWERS = 2 * ITERS + 1
+EXACT = 3
 F32 = jnp.float32
 BF16 = jnp.bfloat16
 
@@ -265,7 +266,7 @@
 
 
 def solve_kernel(
-    middle_h, middle_l, outer_h, outer_l, start, fxp, fxm, limits, out, corner_h, corner_l, *scratch
+    middle_h, middle_l, outer_h, outer_l, start, fxp, fxm, limits, out, corner_h, corner_l, gram_ref, *scratch
 ):
     fields = (scratch[0:3], scratch[3:6])
     later = scratch[6:]
@@ -285,7 +286,7 @@
             return found[0][found[1]]
         return start[g, m]
 
-    def put_field(slot, g, h, c, value):
+    def put_field(slot, g, h, c, value, short=False):
         high, low = split(value)
         for target in range(3):
             c_low, c_high = COLUMNS[target]
@@ -293,13 +294,14 @@
                 first = (h * (c_high - c_low) + c - c_low) * B
                 ref = fields[slot % 2][target]
                 ref[first : first + B, (1 + g) * B : (2 + g) * B] = high
-                ref[first : first + B, 3 * g * B : (3 * g + 1) * B] = low
-
-    def put_vector(slot, g, h, c, value):
+                if not short:
+                    ref[first : first + B, 3 * g * B : (3 * g + 1) * B] = low
+
+    def put_vector(slot, g, h, c, value, short=False):
         m = 3 * (h - g) + c
         later[slot - 1][g, m * B : (m + 1) * B, :] = value
         if slot < POWERS - 1:
-            put_field(slot, g, h, c, value)
+            put_field(slot, g, h, c, value, short)
 
     for (h, c, is_coupling, o), (ref, place) in corners.items():
         if is_coupling:
@@ -317,7 +319,7 @@
             return outer_h.at[h // 3], outer_l.at[h // 3]
         return corner_h.at[h // 3, c // 2], corner_l.at[h // 3, c // 2]
 
-    def apply(slot):
+    def apply(slot, short):
         for h in range(4):
             for c in range(3):
                 field = fields[slot % 2][c]
@@ -331,6 +333,18 @@
                     return jnp.dot(left, right, preferred_element_type=F32)
 
                 values = {}
+                if short:
+                    if h in (1, 2):
+                        both = product(wh, 1, 3, 1, 3)
+                        values = {0: both[:, :B], 1: both[:, B:]}
+                        g, other = (0, 0) if h == 1 else (1, 3)
+                        values[g] = values[g] + product(wh, other, other + 1, 1 + g, 2 + g)
+                    else:
+                        g = h // 3
+                        values[g] = product(wh, *ROWS[h], 1 + g, 2 + g)
+                    for g in values:
+                        put_vector(slot + 1, g, h, c, values[g], True)
+                    continue
                 for g in range(2):
                     if 0 <= h - g <= 2:
                         low, high = max(ROWS[h][0], g), min(ROWS[h][1], g + 3)
@@ -348,8 +362,6 @@
                 for g in values:
                     put_vector(slot + 1, g, h, c, values[g])
 
-    partial = {}
-
     def grams(slot):
         for g in range(2):
             totals = [None] * (slot + 1)
@@ -359,19 +371,24 @@
                     term = jnp.sum((here * power(i, g, m)).reshape(16, 8, B), axis=0)
                     totals[i] = term if totals[i] is None else totals[i] + term
             for i in range(slot + 1):
-                partial[slot, i, g] = jnp.sum(totals[i], axis=0, keepdims=True)
-
-    for slot in range(POWERS - 1):
-        apply(slot)
+                gram_ref[slot, i, g : g + 1, :] = jnp.sum(totals[i], axis=0, keepdims=True)
+
+    for slot in range(EXACT):
+        apply(slot, False)
         grams(slot)
-    grams(POWERS - 1)
-    gram = [
-        [
-            jnp.concatenate([partial[max(i, j), min(i, j), g] for g in range(2)], axis=0)
-            for j in range(POWERS)
-        ]
-        for i in range(POWERS)
-    ]
+    size, before, first = (gram_ref[i, i] for i in (EXACT - 1, EXACT - 2, 0))
+    small = jnp.logical_and(size <= 0.0256 * first, size <= 0.2 * before)
+    all_small = jnp.min(small.astype(F32)) > 0.5
+
+    def rest(short):
+        for slot in range(EXACT, POWERS - 1):
+            apply(slot, short)
+            grams(slot)
+        grams(POWERS - 1)
+
+    pl.when(all_small)(lambda: rest(True))
+    pl.when(jnp.logical_not(all_small))(lambda: rest(False))
+    gram = [[gram_ref[max(i, j), min(i, j)] for j in range(POWERS)] for i in range(POWERS)]
     x = tfqmr(gram, limits[...])
     for g in range(2):
         for m in range(9):
@@ -391,6 +408,7 @@
         scratch_shapes=[
             pltpu.VMEM((2, 2, B, 4 * B), BF16),
             pltpu.VMEM((2, 2, B, 4 * B), BF16),
+            pltpu.VMEM((POWERS, POWERS, 2, B), F32),
             *fields,
             *fields,
             *[pltpu.VMEM((2, 9 * B, B), F32) for _ in range(POWERS - 1)],

time: 62 us -> 59.7 us (0.963)
  Pallas kernels: 19.6 us -> 17.4 us
    pallas_call x1, Pallas kernels: 14 us -> 11.8 us  [solve(): pl.pallas_call(solve_kernel, out_shape=jax.ShapeDtypeStruct((2, 1, 9, B,...]
where the time goes in v6:
time: 59.7 us; the launch traced here: 59.2 us
  starting transfers between devices  22.7 us (38%)
  Pallas kernels  17.4 us (29%)
  waiting for transfers between devices  13.7 us (23%)
  local copies, waits for them, and re-layouts  5.35 us (9%)
    ppermute x8, starting transfers between devices, shift(): return lax.ppermute(value, axis, pairs)  22.7 us
    ppermute x8, waiting for transfers between devices, shift(): return lax.ppermute(value, axis, pairs)  13.7 us
    pallas_call x1, Pallas kernels, solve(): pl.pallas_call(solve_kernel, out_shape=jax.ShapeDtypeStruct((2, 1, 9, B,...  11.8 us
    unnamed x18, local copies, waits for them, and re-layouts  5.19 us
    pallas_call x1, Pallas kernels, prepare(): pl.pallas_call(prepare_kernel, out_shape=[jax.ShapeDtypeStruct(*shape) fo...  1.89 us
    pallas_call x1, Pallas kernels, pack(): pl.pallas_call(pack_kernel, out_shape=out, in_specs=[pl.BlockSpec(memory_...  1.31 us
    pallas_call x1, Pallas kernels, outer(): pl.pallas_call(outer_kernel, out_shape=[jax.ShapeDtypeStruct(*shape) for...  1.25 us
  transfers between devices with their start and end apart: 8, of which 5 were waited for; matrix products, arithmetic and copies ran while one was open for 0% of the time, Pallas kernels for 7%

profile of v6, /device:TPU:1, one launch (start us, length us, event | category | flops | bytes accessed | tf_op | source)
XLA Modules:
  0.0 59.2 jit_solution(5729860751598590390)
XLA Ops:
  0.0 0.0 copy-start
  0.0 1.3 %copy-done = f32[2,1,9,128,128]{4,3,2,1,0:T(8,128)S(1)} copy-done((f32[2,1,9,128,128]{4,3,2,1,0:T(8,128)S(1)}, f32[2,1,9,128,128]{4,3,2,1,0:T(8,128)}, u32[]{:S(2)}) %copy-start) | copy-done | bytes 1179672
  1.3 0.0 copy-start.2
  1.3 1.3 %copy-done.2 = f32[2,1,9,128,128]{4,3,2,1,0:T(8,128)S(1)} copy-done((f32[2,1,9,128,128]{4,3,2,1,0:T(8,128)S(1)}, f32[2,1,9,128,128]{4,3,2,1,0:T(8,128)}, u32[]{:S(2)}) %copy-start.2) | copy-done | bytes 1179672
  2.5 0.0 copy-start.4
  2.5 0.8 %copy-done.4 = s32[2,1,9,8,8]{2,4,3,1,0:T(8,128)S(1)} copy-done((s32[2,1,9,8,8]{2,4,3,1,0:T(8,128)S(1)}, s32[2,1,9,8,8]{2,4,3,1,0:T(8,128)}, u32[]{:S(2)}) %copy-start.4) | copy-done | bytes 4632
  3.4 0.0 copy-start.8
  3.4 1.3 %pack.1 = (f32[10,128,128]{2,1,0:T(8,128)S(1)}, f32[10,128,128]{2,1,0:T(8,128)S(1)}, f32[8,128,128]{2,1,0:T(8,128)}, f32[8,128,128]{2,1,0:T(8,128)S(1)}, f32[7,1...) custom-call(s32[128,9]{1,0:T(8,128)S(1)} %bitcast.4, f32[2,1,9,128,128]{4,3,2,1,0:T(8,128)S(1)} %copy-done, ...), custom_call_target="tpu_custom_call" | custom-call | tf_op jit(solution)/shard_map/pack/pallas_call | solution.py:81
  4.7 4.5 %collective-permute-start.4 = (f32[7,128,128]{2,1,0:T(8,128)S(1)}, f32[7,128,128]{2,1,0:T(8,128)S(1)}, u32[]{:S(2)}, u32[]{:S(2)}) collective-permute-start(f32[7,128,128]{2,1,0:T(8,128)S(1)} %get-tuple-element.23), channel_id=1, source_target_pairs={{0,16},{16,32},{32,48},{48,64},{64,80},{80,96},{96,112},{1,17},{17... | collective-permute-start | bytes 1376264 | tf_op jit(solution)/shard_map/ppermute | solution.py:427
  9.2 3.6 %collective-permute-start = (f32[10,128,128]{2,1,0:T(8,128)S(1)}, f32[10,128,128]{2,1,0:T(8,128)S(1)}, u32[]{:S(2)}, u32[]{:S(2)}) collective-permute-start(f32[10,128,128]{2,1,0:T(8,128)S(1)} %get-tuple-element.19), channel_id=1, source_target_pairs={{0,1},{1,2},{2,3},{3,4},{4,5},{5,6},{6,7},{7,8},{8,9},{9,10},{10,1... | collective-permute-start | bytes 1966088 | tf_op jit(solution)/shard_map/ppermute | solution.py:427
  12.8 1.3 %collective-permute-start.1 = (f32[10,128,128]{2,1,0:T(8,128)S(1)}, f32[10,128,128]{2,1,0:T(8,128)S(1)}, u32[]{:S(2)}, u32[]{:S(2)}) collective-permute-start(f32[10,128,128]{2,1,0:T(8,128)S(1)} %get-tuple-element.20), channel_id=1, source_target_pairs={{1,0},{2,1},{3,2},{4,3},{5,4},{6,5},{7,6},{8,7},{9,8},{10,9},{11,1... | collective-permute-start | bytes 1966088 | tf_op jit(solution)/shard_map/ppermute | solution.py:427
  14.1 1.9 %collective-permute-start.5 = (f32[7,128,128]{2,1,0:T(8,128)}, f32[7,128,128]{2,1,0:T(8,128)}, u32[]{:S(2)}, u32[]{:S(2)}) collective-permute-start(f32[7,128,128]{2,1,0:T(8,128)} %get-tuple-element.24), channel_id=1, source_target_pairs={{16,0},{32,16},{48,32},{64,48},{80,64},{96,80},{112,96},{17,1},{33... | collective-permute-start | bytes 1376264 | tf_op jit(solution)/shard_map/ppermute | solution.py:427
  16.0 5.0 %collective-permute-start.2 = (f32[8,128,128]{2,1,0:T(8,128)}, f32[8,128,128]{2,1,0:T(8,128)}, u32[]{:S(2)}, u32[]{:S(2)}) collective-permute-start(f32[8,128,128]{2,1,0:T(8,128)} %get-tuple-element.21), channel_id=1, source_target_pairs={{0,1},{1,2},{2,3},{3,4},{4,5},{5,6},{6,7},{7,8},{8,9},{9,10},{10,1... | collective-permute-start | bytes 1572872 | tf_op jit(solution)/shard_map/ppermute | solution.py:427
  21.0 0.0 collective-permute-done.4.rxp
  21.0 0.0 copy-start.6
  21.0 0.8 %copy-done.6 = f32[7,128,128]{2,1,0:T(8,128)} copy-done((f32[7,128,128]{2,1,0:T(8,128)}, f32[7,128,128]{2,1,0:T(8,128)S(1)}, u32[]{:S(2)}) %copy-start.6) | copy-done | bytes 458776
  21.8 1.3 %collective-permute-start.3 = (f32[8,128,128]{2,1,0:T(8,128)S(1)}, f32[8,128,128]{2,1,0:T(8,128)}, u32[]{:S(2)}, u32[]{:S(2)}) collective-permute-start(f32[8,128,128]{2,1,0:T(8,128)S(1)} %get-tuple-element.22), channel_id=1, source_target_pairs={{1,0},{2,1},{3,2},{4,3},{5,4},{6,5},{7,6},{8,7},{9,8},{10,9},{11,1... | collective-permute-start | bytes 1572872 | tf_op jit(solution)/shard_map/ppermute | solution.py:427
  23.0 0.0 copy-done.8
  23.1 0.1 broadcast_in_dim.3
  23.1 0.1 convert_element_type.9.limits
  23.2 1.2 %collective-permute-done.5.rxm = f32[7,128,128]{2,1,0:T(8,128)} collective-permute-done((f32[7,128,128]{2,1,0:T(8,128)}, f32[7,128,128]{2,1,0:T(8,128)}, u32[]{:S(2)}, u32[]{:S(2)}) %collective-permute-start.5) | collective-permute-done | bytes 458784 | tf_op jit(solution)/shard_map/ppermute | solution.py:427
  24.4 0.0 copy-start.7
  24.4 1.0 %copy-done.7 = f32[7,128,128]{2,1,0:T(8,128)S(1)} copy-done((f32[7,128,128]{2,1,0:T(8,128)S(1)}, f32[7,128,128]{2,1,0:T(8,128)}, u32[]{:S(2)}) %copy-start.7) | copy-done | bytes 458776
  25.4 0.0 copy-start.3
  25.4 1.2 %outer.1 = (bf16[2,128,768]{2,1,0:T(8,128)(2,1)S(1)}, bf16[2,128,768]{2,1,0:T(8,128)(2,1)S(1)}, f32[2,128,128]{2,1,0:T(8,128)S(1)}) custom-call(f32[7,128,128]{2,1,0:T(8,128)S(1)} %copy-done.7, f32[7,128,128]{2,1,0:T(8,128)} %collective-permute-done.5.rxm), custom_call_target="tpu_custom_call" | custom-call | flops 1000000000 | bytes 1000000 | tf_op jit(solution)/shard_map/outer/pallas_call | solution.py:244
  26.7 0.0 copy-start.1
  26.7 0.0 copy-start.5
  26.7 0.6 collective-permute-done.rap
  27.2 4.4 %collective-permute-done.1.ram = f32[10,128,128]{2,1,0:T(8,128)S(1)} collective-permute-done((f32[10,128,128]{2,1,0:T(8,128)S(1)}, f32[10,128,128]{2,1,0:T(8,128)S(1)}, u32[]{:S(2)}, u32[]{:S(2)}) %collective-permute-start.1) | collective-permute-done | bytes 655392 | tf_op jit(solution)/shard_map/ppermute | solution.py:427
  31.6 1.1 %relay.1 = (f32[10,128,128]{2,1,0:T(8,128)}, f32[10,128,128]{2,1,0:T(8,128)}) custom-call(f32[10,128,128]{2,1,0:T(8,128)S(1)} %collective-permute-done.rap, f32[10,128,128]{2,1,0:T(8,128)S(1)} %collective-permute-done.1.ram), custom_call_target="tpu_custom_call" | custom-call | tf_op jit(solution)/shard_map/relay/pallas_call | solution.py:99
  32.8 2.4 %collective-permute-start.6 = (f32[10,128,128]{2,1,0:T(8,128)}, f32[10,128,128]{2,1,0:T(8,128)}, u32[]{:S(2)}, u32[]{:S(2)}) collective-permute-start(f32[10,128,128]{2,1,0:T(8,128)} %get-tuple-element.31), channel_id=1, source_target_pairs={{0,16},{16,32},{32,48},{48,64},{64,80},{80,96},{96,112},{1,17},{17... | collective-permute-start | bytes 1966088 | tf_op jit(solution)/shard_map/ppermute | solution.py:427
  35.2 2.7 %collective-permute-start.7 = (f32[10,128,128]{2,1,0:T(8,128)}, f32[10,128,128]{2,1,0:T(8,128)}, u32[]{:S(2)}, u32[]{:S(2)}) collective-permute-start(f32[10,128,128]{2,1,0:T(8,128)} %get-tuple-element.32), channel_id=1, source_target_pairs={{16,0},{32,16},{48,32},{64,48},{80,64},{96,80},{112,96},{17,1},{33... | collective-permute-start | bytes 1966088 | tf_op jit(solution)/shard_map/ppermute | solution.py:427
  38.0 0.0 collective-permute-done.2.rbp
  38.0 4.0 %collective-permute-done.3.rbm = f32[8,128,128]{2,1,0:T(8,128)} collective-permute-done((f32[8,128,128]{2,1,0:T(8,128)S(1)}, f32[8,128,128]{2,1,0:T(8,128)}, u32[]{:S(2)}, u32[]{:S(2)}) %collective-permute-start.3) | collective-permute-done | bytes 524320 | tf_op jit(solution)/shard_map/ppermute | solution.py:427
  42.0 0.0 copy-done.3
  42.0 0.0 copy-done.1
  42.0 0.0 copy-done.5
  42.0 1.9 %prepare.1 = (bf16[2,3,128,1152]{3,2,1,0:T(8,128)(2,1)S(1)}, bf16[2,3,128,1152]{3,2,1,0:T(8,128)(2,1)S(1)}, f32[2,9,128,128]{3,2,1,0:T(8,128)S(1)}) custom-call(f32[10,128,128]{2,1,0:T(8,128)S(1)} %collective-permute-done.rap, f32[10,128,128]{2,1,0:T(8,128)S(1)} %collective-permute-done.1.ram, f32[8,128,128]{2,1,0:T(8,128)} %collective-permute-done.2.rbp, ...), custom_call_target="tpu_custom_call" | custom-call | flops 999999995904 | bytes 1000000000 | tf_op jit(solution)/shard_map/prepare/pallas_call | solution.py:257
  43.9 0.0 collective-permute-done.6.fxp
  43.9 3.5 %collective-permute-done.7.fxm = f32[10,128,128]{2,1,0:T(8,128)} collective-permute-done((f32[10,128,128]{2,1,0:T(8,128)}, f32[10,128,128]{2,1,0:T(8,128)}, u32[]{:S(2)}, u32[]{:S(2)}) %collective-permute-start.7) | collective-permute-done | bytes 655392 | tf_op jit(solution)/shard_map/ppermute | solution.py:427
  47.4 11.8 %solve.1 = f32[2,1,9,128,128]{4,3,2,1,0:T(8,128)} custom-call(bf16[2,3,128,1152]{3,2,1,0:T(8,128)(2,1)S(1)} %get-tuple-element.26.middle_h, bf16[2,3,128,1152]{3,2,1,0:T(8,128)(2,1)S(1)} %get-tuple-element.27.middle_l, bf16[2,128,768]{2,1,0:T(8,128)(2,1)S(1)} %get-tuple-element.28.outer_h, bf16[2,128,768]{2,1,0:T(8,128)(2,1)S(1)} %get-tuple-element.29.outer_l, ...), custom_call_target="tpu_custom_call" | custom-call | tf_op jit(solution)/shard_map/solve/pallas_call | solution.py:403
  (1 shorter events, 0.0 us)
Async XLA Ops:
  0.0 1.3 %copy-start = (f32[2,1,9,128,128]{4,3,2,1,0:T(8,128)S(1)}, f32[2,1,9,128,128]{4,3,2,1,0:T(8,128)}, u32[]{:S(2)}) copy-start(f32[2,1,9,128,128]{4,3,2,1,0:T(8,128)} %blocks.3) | copy-start | bytes 3538948
  1.3 1.3 %copy-start.2 = (f32[2,1,9,128,128]{4,3,2,1,0:T(8,128)S(1)}, f32[2,1,9,128,128]{4,3,2,1,0:T(8,128)}, u32[]{:S(2)}) copy-start(f32[2,1,9,128,128]{4,3,2,1,0:T(8,128)} %rhs.3) | copy-start | bytes 3538948
  2.5 0.8 %copy-start.4 = (s32[2,1,9,8,8]{2,4,3,1,0:T(8,128)S(1)}, s32[2,1,9,8,8]{2,4,3,1,0:T(8,128)}, u32[]{:S(2)}) copy-start(s32[2,1,9,8,8]{2,4,3,1,0:T(8,128)} %param.5) | copy-start | bytes 13828
  3.4 19.7 %copy-start.8 = (s32[2,1,8]{2,1,0:T(1,128)S(1)}, s32[2,1,8]{2,1,0:T(1,128)}, u32[]{:S(2)}) copy-start(s32[2,1,8]{2,1,0:T(1,128)} %param.7) | copy-start | bytes 196
  4.7 16.3 %collective-permute-start.4 = (f32[7,128,128]{2,1,0:T(8,128)S(1)}, f32[7,128,128]{2,1,0:T(8,128)S(1)}, u32[]{:S(2)}, u32[]{:S(2)}) collective-permute-start(f32[7,128,128]{2,1,0:T(8,128)S(1)} %get-tuple-element.23), channel_id=1, source_target_pairs={{0,16},{16,32},{32,48},{48,64},{64,80},{80,96},{96,112},{1,17},{17... | collective-permute-start | bytes 1376264 | tf_op jit(solution)/shard_map/ppermute | solution.py:427
  9.2 18.0 %collective-permute-start = (f32[10,128,128]{2,1,0:T(8,128)S(1)}, f32[10,128,128]{2,1,0:T(8,128)S(1)}, u32[]{:S(2)}, u32[]{:S(2)}) collective-permute-start(f32[10,128,128]{2,1,0:T(8,128)S(1)} %get-tuple-element.19), channel_id=1, source_target_pairs={{0,1},{1,2},{2,3},{3,4},{4,5},{5,6},{6,7},{7,8},{8,9},{9,10},{10,1... | collective-permute-start | bytes 1966088 | tf_op jit(solution)/shard_map/ppermute | solution.py:427
  12.8 18.8 %collective-permute-start.1 = (f32[10,128,128]{2,1,0:T(8,128)S(1)}, f32[10,128,128]{2,1,0:T(8,128)S(1)}, u32[]{:S(2)}, u32[]{:S(2)}) collective-permute-start(f32[10,128,128]{2,1,0:T(8,128)S(1)} %get-tuple-element.20), channel_id=1, source_target_pairs={{1,0},{2,1},{3,2},{4,3},{5,4},{6,5},{7,6},{8,7},{9,8},{10,9},{11,1... | collective-permute-start | bytes 1966088 | tf_op jit(solution)/shard_map/ppermute | solution.py:427
  14.1 10.3 %collective-permute-start.5 = (f32[7,128,128]{2,1,0:T(8,128)}, f32[7,128,128]{2,1,0:T(8,128)}, u32[]{:S(2)}, u32[]{:S(2)}) collective-permute-start(f32[7,128,128]{2,1,0:T(8,128)} %get-tuple-element.24), channel_id=1, source_target_pairs={{16,0},{32,16},{48,32},{64,48},{80,64},{96,80},{112,96},{17,1},{33... | collective-permute-start | bytes 1376264 | tf_op jit(solution)/shard_map/ppermute | solution.py:427
  16.0 21.9 %collective-permute-start.2 = (f32[8,128,128]{2,1,0:T(8,128)}, f32[8,128,128]{2,1,0:T(8,128)}, u32[]{:S(2)}, u32[]{:S(2)}) collective-permute-start(f32[8,128,128]{2,1,0:T(8,128)} %get-tuple-element.21), channel_id=1, source_target_pairs={{0,1},{1,2},{2,3},{3,4},{4,5},{5,6},{6,7},{7,8},{8,9},{9,10},{10,1... | collective-permute-start | bytes 1572872 | tf_op jit(solution)/shard_map/ppermute | solution.py:427
  21.0 0.8 %copy-start.6 = (f32[7,128,128]{2,1,0:T(8,128)}, f32[7,128,128]{2,1,0:T(8,128)S(1)}, u32[]{:S(2)}) copy-start(f32[7,128,128]{2,1,0:T(8,128)S(1)} %collective-permute-done.4.rxp) | copy-start | bytes 1376260
  21.8 20.2 %collective-permute-start.3 = (f32[8,128,128]{2,1,0:T(8,128)S(1)}, f32[8,128,128]{2,1,0:T(8,128)}, u32[]{:S(2)}, u32[]{:S(2)}) collective-permute-start(f32[8,128,128]{2,1,0:T(8,128)S(1)} %get-tuple-element.22), channel_id=1, source_target_pairs={{1,0},{2,1},{3,2},{4,3},{5,4},{6,5},{7,6},{8,7},{9,8},{10,9},{11,1... | collective-permute-start | bytes 1572872 | tf_op jit(solution)/shard_map/ppermute | solution.py:427
  24.4 1.0 %copy-start.7 = (f32[7,128,128]{2,1,0:T(8,128)S(1)}, f32[7,128,128]{2,1,0:T(8,128)}, u32[]{:S(2)}) copy-start(f32[7,128,128]{2,1,0:T(8,128)} %copy-done.6) | copy-start | bytes 1376260
  25.4 16.6 %copy-start.3 = (f32[2,1,9,128,128]{4,3,2,1,0:T(8,128)S(1)}, f32[2,1,9,128,128]{4,3,2,1,0:T(8,128)}, u32[]{:S(2)}) copy-start(f32[2,1,9,128,128]{4,3,2,1,0:T(8,128)} %rhs.3) | copy-start | bytes 3538948
  26.7 15.3 %copy-start.1 = (f32[2,1,9,128,128]{4,3,2,1,0:T(8,128)S(1)}, f32[2,1,9,128,128]{4,3,2,1,0:T(8,128)}, u32[]{:S(2)}) copy-start(f32[2,1,9,128,128]{4,3,2,1,0:T(8,128)} %blocks.3) | copy-start | bytes 3538948
  26.7 15.3 %copy-start.5 = (s32[2,1,9,8,8]{2,4,3,1,0:T(8,128)S(1)}, s32[2,1,9,8,8]{2,4,3,1,0:T(8,128)}, u32[]{:S(2)}) copy-start(s32[2,1,9,8,8]{2,4,3,1,0:T(8,128)} %param.5) | copy-start | bytes 13828
  32.8 11.1 %collective-permute-start.6 = (f32[10,128,128]{2,1,0:T(8,128)}, f32[10,128,128]{2,1,0:T(8,128)}, u32[]{:S(2)}, u32[]{:S(2)}) collective-permute-start(f32[10,128,128]{2,1,0:T(8,128)} %get-tuple-element.31), channel_id=1, source_target_pairs={{0,16},{16,32},{32,48},{48,64},{64,80},{80,96},{96,112},{1,17},{17... | collective-permute-start | bytes 1966088 | tf_op jit(solution)/shard_map/ppermute | solution.py:427
  35.2 12.2 %collective-permute-start.7 = (f32[10,128,128]{2,1,0:T(8,128)}, f32[10,128,128]{2,1,0:T(8,128)}, u32[]{:S(2)}, u32[]{:S(2)}) collective-permute-start(f32[10,128,128]{2,1,0:T(8,128)} %get-tuple-element.32), channel_id=1, source_target_pairs={{16,0},{32,16},{48,32},{64,48},{80,64},{96,80},{112,96},{17,1},{33... | collective-permute-start | bytes 1966088 | tf_op jit(solution)/shard_map/ppermute | solution.py:427

commit v7 on v6

--- a/solution.py
+++ b/solution.py
@@ -203,57 +203,37 @@
     return slice(place * B, (place + 1) * B)
 
 
-def prepare_kernel(rap, ram, rbp, rbm, above, mask, blocks, rhs, middle_h, middle_l, start):
+def prepare_kernel(rap, ram, rbp, rbm, rxp, rxm, mask, blocks, rhs, middle_h, middle_l, outer_h, outer_l, start):
     def put(h, c, is_coupling, o, value):
         if is_coupling:
             high, low = split(value)
             lanes = coupling_lanes(h, c, o)
-            middle_h[h - 1, c, :, lanes] = high
-            middle_l[h - 1, c, :, lanes] = low
+            if h in (1, 2):
+                middle_h[h - 1, c, :, lanes] = high
+                middle_l[h - 1, c, :, lanes] = low
+            else:
+                outer_h[h // 3, :, lanes] = high
+                outer_l[h // 3, :, lanes] = low
         else:
             g = h + o // 3 - 2
             if 0 <= g <= 1:
                 start[g, 3 * (h - g) + c] = value
 
-    start[0, 1] = above[0]
-    start[1, 7] = above[1]
     for v, ref_a, ref_b in ((1, rap, rbp), (-1, ram, rbm)):
         for ref, entries in ((ref_a, FIRST[v]), (ref_b, SECOND[v])):
             for place, (row, is_coupling, o) in enumerate(entries):
                 put(row + 1, 1 - v, is_coupling, o, ref[place])
+    for u, ref in ((1, rxp), (-1, rxm)):
+        for place, (row, is_coupling, o) in enumerate(OWN[u]):
+            put(0 if u > 0 else 3, 1, is_coupling, o, ref[place])
     for row, o, value in masked_blocks(mask, blocks):
         put(row + 1, 1, True, o, value)
     for row, u in ((0, 0), (1, 0), (0, 1), (1, -1)):
         put(row + 1, 1, False, off(u, 0), rhs[row, 0, off(u, 0)])
 
 
-def outer_kernel(rxp, rxm, outer_h, outer_l, right):
-    for u, ref in ((1, rxp), (-1, rxm)):
-        h = 0 if u > 0 else 3
-        for place, (row, is_coupling, o) in enumerate(OWN[u]):
-            if is_coupling:
-                high, low = split(ref[place])
-                outer_h[h // 3, :, coupling_lanes(h, 1, o)] = high
-                outer_l[h // 3, :, coupling_lanes(h, 1, o)] = low
-            else:
-                right[h // 3] = ref[place]
-
-
-def outer(*arrays):
-    shapes = [((2, B, 6 * B), BF16)] * 2 + [((2, B, B), F32)]
-    return pl.pallas_call(
-        outer_kernel,
-        out_shape=[jax.ShapeDtypeStruct(*shape) for shape in shapes],
-        in_specs=[pl.BlockSpec(memory_space=pltpu.VMEM)] * len(arrays),
-        out_specs=[pl.BlockSpec(memory_space=pltpu.VMEM)] * len(shapes),
-        compiler_params=pltpu.CompilerParams(vmem_limit_bytes=8 * 2**20),
-        cost_estimate=pl.CostEstimate(flops=10**9, bytes_accessed=10**6, transcendentals=0),
-        name="outer",
-    )(*arrays)
-
-
 def prepare(*arrays):
-    shapes = [((2, 3, B, 9 * B), BF16)] * 2 + [((2, 9, B, B), F32)]
+    shapes = [((2, 3, B, 9 * B), BF16)] * 2 + [((2, B, 6 * B), BF16)] * 2 + [((2, 9, B, B), F32)]
     return pl.pallas_call(
         prepare_kernel,
         out_shape=[jax.ShapeDtypeStruct(*shape) for shape in shapes],
@@ -439,11 +419,10 @@
     up, down = relay(rap, ram)
     fxp = shift(up, "gx", 1)
     fxm = shift(down, "gx", -1)
-    outer_h, outer_l, above = outer(rxp, rxm)
-    middle_h, middle_l, start = prepare(rap, ram, rbp, rbm, above, mask, blocks, rhs_rows)
+    prepared = prepare(rap, ram, rbp, rbm, rxp, rxm, mask, blocks, rhs_rows)
     orbitals = B // pair_mask.shape[-1]
     limits = jnp.repeat(counts, orbitals, axis=-1).reshape(2, B).astype(F32)
-    return solve(middle_h, middle_l, outer_h, outer_l, start, fxp, fxm, limits)
+    return solve(*prepared, fxp, fxm, limits)
 
 
 def solution(mesh):

time: 59.7 us -> 60.2 us (level)
  starting transfers between devices: 22.7 us -> 28.6 us
  waiting for transfers between devices: 13.7 us -> 9.2 us
  local copies, waits for them, and re-layouts: 5.35 us -> 3.55 us
  Pallas kernels: 17.4 us -> 18.3 us
    ppermute x8, starting transfers between devices: 22.7 us -> 28.6 us  [shift(): return lax.ppermute(value, axis, pairs)]
    ppermute x8, waiting for transfers between devices: 13.7 us -> 9.2 us  [shift(): return lax.ppermute(value, axis, pairs)]
    unnamed x18 -> x14, local copies, waits for them, and re-layouts: 5.19 us -> 3.39 us
    pallas_call x1 -> x0, Pallas kernels: 1.25 us -> none  [outer(): pl.pallas_call(outer_kernel, out_shape=[jax.ShapeDtypeStruct(*shape) for...]
    pallas_call x1, Pallas kernels: 1.15 us -> 2.23 us  [relay(): pl.pallas_call(relay_kernel, out_shape=[jax.ShapeDtypeStruct((10, B, B),...]
  transfers between devices with their start and end apart: 8 -> 8, of which waited for: 5 -> 4; matrix products, arithmetic and copies ran while one was open for 0% -> 0% of each run, Pallas kernels for 7% -> 8%
where the time goes in v7:
time: 60.2 us; the launch traced here: 59.7 us
  starting transfers between devices  28.6 us (48%)
  Pallas kernels  18.3 us (30%)
  waiting for transfers between devices  9.2 us (15%)
  local copies, waits for them, and re-layouts  3.55 us (6%)
    ppermute x8, starting transfers between devices, shift(): return lax.ppermute(value, axis, pairs)  28.6 us
    pallas_call x1, Pallas kernels, solve(): pl.pallas_call(solve_kernel, out_shape=jax.ShapeDtypeStruct((2, 1, 9, B,...  11.8 us
    ppermute x8, waiting for transfers between devices, shift(): return lax.ppermute(value, axis, pairs)  9.2 us
    unnamed x14, local copies, waits for them, and re-layouts  3.39 us
    pallas_call x1, Pallas kernels, prepare(): pl.pallas_call(prepare_kernel, out_shape=[jax.ShapeDtypeStruct(*shape) fo...  2.49 us
    pallas_call x1, Pallas kernels, relay(): pl.pallas_call(relay_kernel, out_shape=[jax.ShapeDtypeStruct((10, B, B),...  2.23 us
    pallas_call x1, Pallas kernels, pack(): pl.pallas_call(pack_kernel, out_shape=out, in_specs=[pl.BlockSpec(memory_...  1.7 us
  transfers between devices with their start and end apart: 8, of which 4 were waited for; matrix products, arithmetic and copies ran while one was open for 0% of the time, Pallas kernels for 8%

profile of v7, /device:TPU:1, one launch (start us, length us, event | category | flops | bytes accessed | tf_op | source)
XLA Modules:
  0.0 59.7 jit_solution(4252091216557305294)
XLA Ops:
  0.0 0.0 copy-start
  0.0 1.3 %copy-done = f32[2,1,9,128,128]{4,3,2,1,0:T(8,128)S(1)} copy-done((f32[2,1,9,128,128]{4,3,2,1,0:T(8,128)S(1)}, f32[2,1,9,128,128]{4,3,2,1,0:T(8,128)}, u32[]{:S(2)}) %copy-start) | copy-done | bytes 1179672
  1.3 0.0 copy-start.2
  1.3 1.3 %copy-done.2 = f32[2,1,9,128,128]{4,3,2,1,0:T(8,128)S(1)} copy-done((f32[2,1,9,128,128]{4,3,2,1,0:T(8,128)S(1)}, f32[2,1,9,128,128]{4,3,2,1,0:T(8,128)}, u32[]{:S(2)}) %copy-start.2) | copy-done | bytes 1179672
  2.5 0.0 copy-start.4
  2.5 0.8 %copy-done.4 = s32[2,1,9,8,8]{2,4,3,1,0:T(8,128)S(1)} copy-done((s32[2,1,9,8,8]{2,4,3,1,0:T(8,128)S(1)}, s32[2,1,9,8,8]{2,4,3,1,0:T(8,128)}, u32[]{:S(2)}) %copy-start.4) | copy-done | bytes 4632
  3.4 0.0 copy-start.6
  3.4 0.0 copy-start.3
  3.4 1.7 %pack.1 = (f32[10,128,128]{2,1,0:T(8,128)S(1)}, f32[10,128,128]{2,1,0:T(8,128)}, f32[8,128,128]{2,1,0:T(8,128)}, f32[8,128,128]{2,1,0:T(8,128)}, f32[7,128,128]{2,1,0:T(8,128)}, /*index=5*/f32[7,128,128]{2,1,0:T(8,128)S(1)}) custom-call(s32[128,9]{1,0:T(8,128)S(1)} %bitcast.4, f32[2,1,9,128,128]{4,3,2,1,0:T(8,128)S(1)} %copy-done, ...), custom_call_target="tpu_custom_call" | custom-call | tf_op jit(solution)/shard_map/pack/pallas_call | solution.py:81
  5.1 0.0 copy-start.1
  5.1 0.0 copy-start.5
  5.1 4.5 %collective-permute-start = (f32[10,128,128]{2,1,0:T(8,128)S(1)}, f32[10,128,128]{2,1,0:T(8,128)S(1)}, u32[]{:S(2)}, u32[]{:S(2)}) collective-permute-start(f32[10,128,128]{2,1,0:T(8,128)S(1)} %get-tuple-element.18), channel_id=1, source_target_pairs={{0,1},{1,2},{2,3},{3,4},{4,5},{5,6},{6,7},{7,8},{8,9},{9,10},{10,1... | collective-permute-start | bytes 1966088 | tf_op jit(solution)/shard_map/ppermute | solution.py:407
  9.6 1.3 %collective-permute-start.1 = (f32[10,128,128]{2,1,0:T(8,128)}, f32[10,128,128]{2,1,0:T(8,128)}, u32[]{:S(2)}, u32[]{:S(2)}) collective-permute-start(f32[10,128,128]{2,1,0:T(8,128)} %get-tuple-element.19), channel_id=1, source_target_pairs={{1,0},{2,1},{3,2},{4,3},{5,4},{6,5},{7,6},{8,7},{9,8},{10,9},{11,1... | collective-permute-start | bytes 1966088 | tf_op jit(solution)/shard_map/ppermute | solution.py:407
  10.9 4.9 %collective-permute-start.2 = (f32[8,128,128]{2,1,0:T(8,128)}, f32[8,128,128]{2,1,0:T(8,128)}, u32[]{:S(2)}, u32[]{:S(2)}) collective-permute-start(f32[8,128,128]{2,1,0:T(8,128)} %get-tuple-element.20), channel_id=1, source_target_pairs={{0,1},{1,2},{2,3},{3,4},{4,5},{5,6},{6,7},{7,8},{8,9},{9,10},{10,1... | collective-permute-start | bytes 1572872 | tf_op jit(solution)/shard_map/ppermute | solution.py:407
  15.9 1.3 %collective-permute-start.3 = (f32[8,128,128]{2,1,0:T(8,128)}, f32[8,128,128]{2,1,0:T(8,128)}, u32[]{:S(2)}, u32[]{:S(2)}) collective-permute-start(f32[8,128,128]{2,1,0:T(8,128)} %get-tuple-element.21), channel_id=1, source_target_pairs={{1,0},{2,1},{3,2},{4,3},{5,4},{6,5},{7,6},{8,7},{9,8},{10,9},{11,1... | collective-permute-start | bytes 1572872 | tf_op jit(solution)/shard_map/ppermute | solution.py:407
  17.2 4.4 %collective-permute-start.4 = (f32[7,128,128]{2,1,0:T(8,128)}, f32[7,128,128]{2,1,0:T(8,128)}, u32[]{:S(2)}, u32[]{:S(2)}) collective-permute-start(f32[7,128,128]{2,1,0:T(8,128)} %get-tuple-element.22), channel_id=1, source_target_pairs={{0,16},{16,32},{32,48},{48,64},{64,80},{80,96},{96,112},{1,17},{17... | collective-permute-start | bytes 1376264 | tf_op jit(solution)/shard_map/ppermute | solution.py:407
  21.6 1.4 %collective-permute-done.rap = f32[10,128,128]{2,1,0:T(8,128)S(1)} collective-permute-done((f32[10,128,128]{2,1,0:T(8,128)S(1)}, f32[10,128,128]{2,1,0:T(8,128)S(1)}, u32[]{:S(2)}, u32[]{:S(2)}) %collective-permute-start) | collective-permute-done | bytes 655392 | tf_op jit(solution)/shard_map/ppermute | solution.py:407
  23.0 4.6 %collective-permute-start.5 = (f32[7,128,128]{2,1,0:T(8,128)S(1)}, f32[7,128,128]{2,1,0:T(8,128)}, u32[]{:S(2)}, u32[]{:S(2)}) collective-permute-start(f32[7,128,128]{2,1,0:T(8,128)S(1)} %get-tuple-element.23), channel_id=1, source_target_pairs={{16,0},{32,16},{48,32},{64,48},{80,64},{96,80},{112,96},{17,1},{33... | collective-permute-start | bytes 1376264 | tf_op jit(solution)/shard_map/ppermute | solution.py:407
  27.6 0.0 copy-done.6
  27.6 0.1 broadcast_in_dim.3
  27.7 0.1 convert_element_type.9.limits
  27.7 0.0 collective-permute-done.1.ram
  27.8 2.2 %relay.1 = (f32[10,128,128]{2,1,0:T(8,128)}, f32[10,128,128]{2,1,0:T(8,128)}) custom-call(f32[10,128,128]{2,1,0:T(8,128)S(1)} %collective-permute-done.rap, f32[10,128,128]{2,1,0:T(8,128)} %collective-permute-done.1.ram), custom_call_target="tpu_custom_call" | custom-call | tf_op jit(solution)/shard_map/relay/pallas_call | solution.py:99
  30.0 5.7 %collective-permute-start.6 = (f32[10,128,128]{2,1,0:T(8,128)}, f32[10,128,128]{2,1,0:T(8,128)}, u32[]{:S(2)}, u32[]{:S(2)}) collective-permute-start(f32[10,128,128]{2,1,0:T(8,128)} %get-tuple-element.29), channel_id=1, source_target_pairs={{0,16},{16,32},{32,48},{48,64},{64,80},{80,96},{96,112},{1,17},{17... | collective-permute-start | bytes 1966088 | tf_op jit(solution)/shard_map/ppermute | solution.py:407
  35.7 0.0 collective-permute-done.4.rxp
  35.7 1.9 %collective-permute-start.7 = (f32[10,128,128]{2,1,0:T(8,128)}, f32[10,128,128]{2,1,0:T(8,128)}, u32[]{:S(2)}, u32[]{:S(2)}) collective-permute-start(f32[10,128,128]{2,1,0:T(8,128)} %get-tuple-element.30), channel_id=1, source_target_pairs={{16,0},{32,16},{48,32},{64,48},{80,64},{96,80},{112,96},{17,1},{33... | collective-permute-start | bytes 1966088 | tf_op jit(solution)/shard_map/ppermute | solution.py:407
  37.6 0.0 collective-permute-done.5.rxm
  37.6 0.0 collective-permute-done.2.rbp
  37.6 1.0 %collective-permute-done.3.rbm = f32[8,128,128]{2,1,0:T(8,128)} collective-permute-done((f32[8,128,128]{2,1,0:T(8,128)}, f32[8,128,128]{2,1,0:T(8,128)}, u32[]{:S(2)}, u32[]{:S(2)}) %collective-permute-start.3) | collective-permute-done | bytes 524320 | tf_op jit(solution)/shard_map/ppermute | solution.py:407
  38.7 0.0 copy-done.3
  38.7 0.0 copy-done.1
  38.7 0.0 copy-done.5
  38.7 2.5 %prepare.1 = (bf16[2,3,128,1152]{3,2,1,0:T(8,128)(2,1)S(1)}, bf16[2,3,128,1152]{3,2,1,0:T(8,128)(2,1)S(1)}, bf16[2,128,768]{2,1,0:T(8,128)(2,1)S(1)}, bf16[2,128...) custom-call(f32[10,128,128]{2,1,0:T(8,128)S(1)} %collective-permute-done.rap, f32[10,128,128]{2,1,0:T(8,128)} %collective-permute-done.1.ram, ...), custom_call_target="tpu_custom_call" | custom-call | flops 999999995904 | bytes 1000000000 | tf_op jit(solution)/shard_map/prepare/pallas_call | solution.py:237
  41.2 2.3 %collective-permute-done.6.fxp = f32[10,128,128]{2,1,0:T(8,128)} collective-permute-done((f32[10,128,128]{2,1,0:T(8,128)}, f32[10,128,128]{2,1,0:T(8,128)}, u32[]{:S(2)}, u32[]{:S(2)}) %collective-permute-start.6) | collective-permute-done | bytes 655392 | tf_op jit(solution)/shard_map/ppermute | solution.py:407
  43.5 4.4 %collective-permute-done.7.fxm = f32[10,128,128]{2,1,0:T(8,128)} collective-permute-done((f32[10,128,128]{2,1,0:T(8,128)}, f32[10,128,128]{2,1,0:T(8,128)}, u32[]{:S(2)}, u32[]{:S(2)}) %collective-permute-start.7) | collective-permute-done | bytes 655392 | tf_op jit(solution)/shard_map/ppermute | solution.py:407
  47.9 11.8 %solve.1 = f32[2,1,9,128,128]{4,3,2,1,0:T(8,128)} custom-call(bf16[2,3,128,1152]{3,2,1,0:T(8,128)(2,1)S(1)} %get-tuple-element.24.middle_h, bf16[2,3,128,1152]{3,2,1,0:T(8,128)(2,1)S(1)} %get-tuple-element.25.middle_l, bf16[2,128,768]{2,1,0:T(8,128)(2,1)S(1)} %get-tuple-element.26.outer_h, bf16[2,128,768]{2,1,0:T(8,128)(2,1)S(1)} %get-tuple-element.27.outer_l, ...), custom_call_target="tpu_custom_call" | custom-call | tf_op jit(solution)/shard_map/solve/pallas_call | solution.py:383
  (1 shorter events, 0.0 us)
Async XLA Ops:
  0.0 1.3 %copy-start = (f32[2,1,9,128,128]{4,3,2,1,0:T(8,128)S(1)}, f32[2,1,9,128,128]{4,3,2,1,0:T(8,128)}, u32[]{:S(2)}) copy-start(f32[2,1,9,128,128]{4,3,2,1,0:T(8,128)} %blocks.3) | copy-start | bytes 3538948
  1.3 1.3 %copy-start.2 = (f32[2,1,9,128,128]{4,3,2,1,0:T(8,128)S(1)}, f32[2,1,9,128,128]{4,3,2,1,0:T(8,128)}, u32[]{:S(2)}) copy-start(f32[2,1,9,128,128]{4,3,2,1,0:T(8,128)} %rhs.3) | copy-start | bytes 3538948
  2.5 0.8 %copy-start.4 = (s32[2,1,9,8,8]{2,4,3,1,0:T(8,128)S(1)}, s32[2,1,9,8,8]{2,4,3,1,0:T(8,128)}, u32[]{:S(2)}) copy-start(s32[2,1,9,8,8]{2,4,3,1,0:T(8,128)} %param.5) | copy-start | bytes 13828
  3.4 24.2 %copy-start.6 = (s32[2,1,8]{2,1,0:T(1,128)S(1)}, s32[2,1,8]{2,1,0:T(1,128)}, u32[]{:S(2)}) copy-start(s32[2,1,8]{2,1,0:T(1,128)} %param.7) | copy-start | bytes 196
  3.4 35.3 %copy-start.3 = (f32[2,1,9,128,128]{4,3,2,1,0:T(8,128)S(1)}, f32[2,1,9,128,128]{4,3,2,1,0:T(8,128)}, u32[]{:S(2)}) copy-start(f32[2,1,9,128,128]{4,3,2,1,0:T(8,128)} %rhs.3) | copy-start | bytes 3538948
  5.1 33.6 %copy-start.1 = (f32[2,1,9,128,128]{4,3,2,1,0:T(8,128)S(1)}, f32[2,1,9,128,128]{4,3,2,1,0:T(8,128)}, u32[]{:S(2)}) copy-start(f32[2,1,9,128,128]{4,3,2,1,0:T(8,128)} %blocks.3) | copy-start | bytes 3538948
  5.1 33.6 %copy-start.5 = (s32[2,1,9,8,8]{2,4,3,1,0:T(8,128)S(1)}, s32[2,1,9,8,8]{2,4,3,1,0:T(8,128)}, u32[]{:S(2)}) copy-start(s32[2,1,9,8,8]{2,4,3,1,0:T(8,128)} %param.5) | copy-start | bytes 13828
  5.1 17.9 %collective-permute-start = (f32[10,128,128]{2,1,0:T(8,128)S(1)}, f32[10,128,128]{2,1,0:T(8,128)S(1)}, u32[]{:S(2)}, u32[]{:S(2)}) collective-permute-start(f32[10,128,128]{2,1,0:T(8,128)S(1)} %get-tuple-element.18), channel_id=1, source_target_pairs={{0,1},{1,2},{2,3},{3,4},{4,5},{5,6},{6,7},{7,8},{8,9},{9,10},{10,1... | collective-permute-start | bytes 1966088 | tf_op jit(solution)/shard_map/ppermute | solution.py:407
  9.6 18.1 %collective-permute-start.1 = (f32[10,128,128]{2,1,0:T(8,128)}, f32[10,128,128]{2,1,0:T(8,128)}, u32[]{:S(2)}, u32[]{:S(2)}) collective-permute-start(f32[10,128,128]{2,1,0:T(8,128)} %get-tuple-element.19), channel_id=1, source_target_pairs={{1,0},{2,1},{3,2},{4,3},{5,4},{6,5},{7,6},{8,7},{9,8},{10,9},{11,1... | collective-permute-start | bytes 1966088 | tf_op jit(solution)/shard_map/ppermute | solution.py:407
  10.9 26.7 %collective-permute-start.2 = (f32[8,128,128]{2,1,0:T(8,128)}, f32[8,128,128]{2,1,0:T(8,128)}, u32[]{:S(2)}, u32[]{:S(2)}) collective-permute-start(f32[8,128,128]{2,1,0:T(8,128)} %get-tuple-element.20), channel_id=1, source_target_pairs={{0,1},{1,2},{2,3},{3,4},{4,5},{5,6},{6,7},{7,8},{8,9},{9,10},{10,1... | collective-permute-start | bytes 1572872 | tf_op jit(solution)/shard_map/ppermute | solution.py:407
  15.9 22.8 %collective-permute-start.3 = (f32[8,128,128]{2,1,0:T(8,128)}, f32[8,128,128]{2,1,0:T(8,128)}, u32[]{:S(2)}, u32[]{:S(2)}) collective-permute-start(f32[8,128,128]{2,1,0:T(8,128)} %get-tuple-element.21), channel_id=1, source_target_pairs={{1,0},{2,1},{3,2},{4,3},{5,4},{6,5},{7,6},{8,7},{9,8},{10,9},{11,1... | collective-permute-start | bytes 1572872 | tf_op jit(solution)/shard_map/ppermute | solution.py:407
  17.2 18.5 %collective-permute-start.4 = (f32[7,128,128]{2,1,0:T(8,128)}, f32[7,128,128]{2,1,0:T(8,128)}, u32[]{:S(2)}, u32[]{:S(2)}) collective-permute-start(f32[7,128,128]{2,1,0:T(8,128)} %get-tuple-element.22), channel_id=1, source_target_pairs={{0,16},{16,32},{32,48},{48,64},{64,80},{80,96},{96,112},{1,17},{17... | collective-permute-start | bytes 1376264 | tf_op jit(solution)/shard_map/ppermute | solution.py:407
  23.0 14.6 %collective-permute-start.5 = (f32[7,128,128]{2,1,0:T(8,128)S(1)}, f32[7,128,128]{2,1,0:T(8,128)}, u32[]{:S(2)}, u32[]{:S(2)}) collective-permute-start(f32[7,128,128]{2,1,0:T(8,128)S(1)} %get-tuple-element.23), channel_id=1, source_target_pairs={{16,0},{32,16},{48,32},{64,48},{80,64},{96,80},{112,96},{17,1},{33... | collective-permute-start | bytes 1376264 | tf_op jit(solution)/shard_map/ppermute | solution.py:407
  30.0 13.5 %collective-permute-start.6 = (f32[10,128,128]{2,1,0:T(8,128)}, f32[10,128,128]{2,1,0:T(8,128)}, u32[]{:S(2)}, u32[]{:S(2)}) collective-permute-start(f32[10,128,128]{2,1,0:T(8,128)} %get-tuple-element.29), channel_id=1, source_target_pairs={{0,16},{16,32},{32,48},{48,64},{64,80},{80,96},{96,112},{1,17},{17... | collective-permute-start | bytes 1966088 | tf_op jit(solution)/shard_map/ppermute | solution.py:407
  35.7 12.2 %collective-permute-start.7 = (f32[10,128,128]{2,1,0:T(8,128)}, f32[10,128,128]{2,1,0:T(8,128)}, u32[]{:S(2)}, u32[]{:S(2)}) collective-permute-start(f32[10,128,128]{2,1,0:T(8,128)} %get-tuple-element.30), channel_id=1, source_target_pairs={{16,0},{32,16},{48,32},{64,48},{80,64},{96,80},{112,96},{17,1},{33... | collective-permute-start | bytes 1966088 | tf_op jit(solution)/shard_map/ppermute | solution.py:407

commit v8 on v6

--- a/solution.py
+++ b/solution.py
@@ -247,7 +247,7 @@
         in_specs=[pl.BlockSpec(memory_space=pltpu.VMEM)] * len(arrays),
         out_specs=[pl.BlockSpec(memory_space=pltpu.VMEM)] * len(shapes),
         compiler_params=pltpu.CompilerParams(vmem_limit_bytes=8 * 2**20),
-        cost_estimate=pl.CostEstimate(flops=10**9, bytes_accessed=10**6, transcendentals=0),
+        cost_estimate=pl.CostEstimate(flops=0, bytes_accessed=0, transcendentals=0),
         name="outer",
     )(*arrays)
 

time: 59.7 us -> 64.6 us (1.082)
  the two profiles are of different devices: /device:TPU:1 before, /device:TPU:25 now
where the time goes in v8:
time: 64.6 us; the launch traced here: 64 us
  starting transfers between devices  26 us (40%)
  Pallas kernels  19.2 us (30%)
  waiting for transfers between devices  15.1 us (23%)
  local copies, waits for them, and re-layouts  3.55 us (5%)
    ppermute x8, starting transfers between devices, shift(): return lax.ppermute(value, axis, pairs)  26 us
    ppermute x8, waiting for transfers between devices, shift(): return lax.ppermute(value, axis, pairs)  15.1 us
    pallas_call x1, Pallas kernels, solve(): pl.pallas_call(solve_kernel, out_shape=jax.ShapeDtypeStruct((2, 1, 9, B,...  11.8 us
    unnamed x14, local copies, waits for them, and re-layouts  3.39 us
    pallas_call x1, Pallas kernels, relay(): pl.pallas_call(relay_kernel, out_shape=[jax.ShapeDtypeStruct((10, B, B),...  2.22 us
    pallas_call x1, Pallas kernels, prepare(): pl.pallas_call(prepare_kernel, out_shape=[jax.ShapeDtypeStruct(*shape) fo...  2.09 us
    pallas_call x1, Pallas kernels, pack(): pl.pallas_call(pack_kernel, out_shape=out, in_specs=[pl.BlockSpec(memory_...  1.92 us
  transfers between devices with their start and end apart: 8, of which 3 were waited for; matrix products, arithmetic and copies ran while one was open for 0% of the time, Pallas kernels for 9%

profile of v8, /device:TPU:25, one launch (start us, length us, event | category | flops | bytes accessed | tf_op | source)
XLA Modules:
  0.0 64.0 jit_solution(5963087927437640998)
XLA Ops:
  0.0 0.0 copy-start
  0.0 1.3 %copy-done = f32[2,1,9,128,128]{4,3,2,1,0:T(8,128)S(1)} copy-done((f32[2,1,9,128,128]{4,3,2,1,0:T(8,128)S(1)}, f32[2,1,9,128,128]{4,3,2,1,0:T(8,128)}, u32[]{:S(2)}) %copy-start) | copy-done | bytes 1179672
  1.3 0.0 copy-start.2
  1.3 1.3 %copy-done.2 = f32[2,1,9,128,128]{4,3,2,1,0:T(8,128)S(1)} copy-done((f32[2,1,9,128,128]{4,3,2,1,0:T(8,128)S(1)}, f32[2,1,9,128,128]{4,3,2,1,0:T(8,128)}, u32[]{:S(2)}) %copy-start.2) | copy-done | bytes 1179672
  2.5 0.0 copy-start.4
  2.5 0.8 %copy-done.4 = s32[2,1,9,8,8]{2,4,3,1,0:T(8,128)S(1)} copy-done((s32[2,1,9,8,8]{2,4,3,1,0:T(8,128)S(1)}, s32[2,1,9,8,8]{2,4,3,1,0:T(8,128)}, u32[]{:S(2)}) %copy-start.4) | copy-done | bytes 4632
  3.4 0.0 copy-start.6
  3.4 0.0 copy-start.3
  3.4 1.9 %pack.1 = (f32[10,128,128]{2,1,0:T(8,128)}, f32[10,128,128]{2,1,0:T(8,128)}, f32[8,128,128]{2,1,0:T(8,128)}, f32[8,128,128]{2,1,0:T(8,128)}, f32[7,128,128]{2,1,0:T(8,128)S(1)}, /*index=5*/f32[7,128,128]{2,1,0:T(8,128)}) custom-call(s32[128,9]{1,0:T(8,128)S(1)} %bitcast.4, f32[2,1,9,128,128]{4,3,2,1,0:T(8,128)S(1)} %copy-done, ...), custom_call_target="tpu_custom_call" | custom-call | tf_op jit(solution)/shard_map/pack/pallas_call | solution.py:81
  5.3 0.0 copy-start.1
  5.3 0.0 copy-start.5
  5.3 3.8 %collective-permute-start.4 = (f32[7,128,128]{2,1,0:T(8,128)S(1)}, f32[7,128,128]{2,1,0:T(8,128)S(1)}, u32[]{:S(2)}, u32[]{:S(2)}) collective-permute-start(f32[7,128,128]{2,1,0:T(8,128)S(1)} %get-tuple-element.23), channel_id=1, source_target_pairs={{0,16},{16,32},{32,48},{48,64},{64,80},{80,96},{96,112},{1,17},{17... | collective-permute-start | bytes 1376264 | tf_op jit(solution)/shard_map/ppermute | solution.py:427
  9.1 3.5 %collective-permute-start = (f32[10,128,128]{2,1,0:T(8,128)}, f32[10,128,128]{2,1,0:T(8,128)S(1)}, u32[]{:S(2)}, u32[]{:S(2)}) collective-permute-start(f32[10,128,128]{2,1,0:T(8,128)} %get-tuple-element.19), channel_id=1, source_target_pairs={{0,1},{1,2},{2,3},{3,4},{4,5},{5,6},{6,7},{7,8},{8,9},{9,10},{10,1... | collective-permute-start | bytes 1966088 | tf_op jit(solution)/shard_map/ppermute | solution.py:427
  12.7 4.2 %collective-permute-start.1 = (f32[10,128,128]{2,1,0:T(8,128)}, f32[10,128,128]{2,1,0:T(8,128)}, u32[]{:S(2)}, u32[]{:S(2)}) collective-permute-start(f32[10,128,128]{2,1,0:T(8,128)} %get-tuple-element.20), channel_id=1, source_target_pairs={{1,0},{2,1},{3,2},{4,3},{5,4},{6,5},{7,6},{8,7},{9,8},{10,9},{11,1... | collective-permute-start | bytes 1966088 | tf_op jit(solution)/shard_map/ppermute | solution.py:427
  16.9 1.9 %collective-permute-start.2 = (f32[8,128,128]{2,1,0:T(8,128)}, f32[8,128,128]{2,1,0:T(8,128)}, u32[]{:S(2)}, u32[]{:S(2)}) collective-permute-start(f32[8,128,128]{2,1,0:T(8,128)} %get-tuple-element.21), channel_id=1, source_target_pairs={{0,1},{1,2},{2,3},{3,4},{4,5},{5,6},{6,7},{7,8},{8,9},{9,10},{10,1... | collective-permute-start | bytes 1572872 | tf_op jit(solution)/shard_map/ppermute | solution.py:427
  18.8 5.5 %collective-permute-start.3 = (f32[8,128,128]{2,1,0:T(8,128)}, f32[8,128,128]{2,1,0:T(8,128)}, u32[]{:S(2)}, u32[]{:S(2)}) collective-permute-start(f32[8,128,128]{2,1,0:T(8,128)} %get-tuple-element.22), channel_id=1, source_target_pairs={{1,0},{2,1},{3,2},{4,3},{5,4},{6,5},{7,6},{8,7},{9,8},{10,9},{11,1... | collective-permute-start | bytes 1572872 | tf_op jit(solution)/shard_map/ppermute | solution.py:427
  24.3 0.0 collective-permute-done.4.rxp
  24.3 1.9 %collective-permute-start.5 = (f32[7,128,128]{2,1,0:T(8,128)}, f32[7,128,128]{2,1,0:T(8,128)}, u32[]{:S(2)}, u32[]{:S(2)}) collective-permute-start(f32[7,128,128]{2,1,0:T(8,128)} %get-tuple-element.24), channel_id=1, source_target_pairs={{16,0},{32,16},{48,32},{64,48},{80,64},{96,80},{112,96},{17,1},{33... | collective-permute-start | bytes 1376264 | tf_op jit(solution)/shard_map/ppermute | solution.py:427
  26.3 0.0 copy-done.6
  26.3 0.1 broadcast_in_dim.3
  26.3 0.1 convert_element_type.9.limits
  26.4 8.3 %collective-permute-done.5.rxm = f32[7,128,128]{2,1,0:T(8,128)} collective-permute-done((f32[7,128,128]{2,1,0:T(8,128)}, f32[7,128,128]{2,1,0:T(8,128)}, u32[]{:S(2)}, u32[]{:S(2)}) %collective-permute-start.5) | collective-permute-done | bytes 458784 | tf_op jit(solution)/shard_map/ppermute | solution.py:427
  34.7 1.1 %outer.1 = (bf16[2,128,768]{2,1,0:T(8,128)(2,1)S(1)}, bf16[2,128,768]{2,1,0:T(8,128)(2,1)S(1)}, f32[2,128,128]{2,1,0:T(8,128)S(1)}) custom-call(f32[7,128,128]{2,1,0:T(8,128)S(1)} %collective-permute-done.4.rxp, f32[7,128,128]{2,1,0:T(8,128)} %collective-permute-done.5.rxm), custom_call_target="tpu_custom_call" | custom-call | tf_op jit(solution)/shard_map/outer/pallas_call | solution.py:244
  35.9 0.0 collective-permute-done.rap
  35.9 0.0 collective-permute-done.1.ram
  35.9 2.2 %relay.1 = (f32[10,128,128]{2,1,0:T(8,128)}, f32[10,128,128]{2,1,0:T(8,128)}) custom-call(f32[10,128,128]{2,1,0:T(8,128)S(1)} %collective-permute-done.rap, f32[10,128,128]{2,1,0:T(8,128)} %collective-permute-done.1.ram), custom_call_target="tpu_custom_call" | custom-call | tf_op jit(solution)/shard_map/relay/pallas_call | solution.py:99
  38.1 1.9 %collective-permute-start.6 = (f32[10,128,128]{2,1,0:T(8,128)}, f32[10,128,128]{2,1,0:T(8,128)}, u32[]{:S(2)}, u32[]{:S(2)}) collective-permute-start(f32[10,128,128]{2,1,0:T(8,128)} %get-tuple-element.31), channel_id=1, source_target_pairs={{0,16},{16,32},{32,48},{48,64},{64,80},{80,96},{96,112},{1,17},{17... | collective-permute-start | bytes 1966088 | tf_op jit(solution)/shard_map/ppermute | solution.py:427
  40.0 3.2 %collective-permute-start.7 = (f32[10,128,128]{2,1,0:T(8,128)}, f32[10,128,128]{2,1,0:T(8,128)}, u32[]{:S(2)}, u32[]{:S(2)}) collective-permute-start(f32[10,128,128]{2,1,0:T(8,128)} %get-tuple-element.32), channel_id=1, source_target_pairs={{16,0},{32,16},{48,32},{64,48},{80,64},{96,80},{112,96},{17,1},{33... | collective-permute-start | bytes 1966088 | tf_op jit(solution)/shard_map/ppermute | solution.py:427
  43.3 0.0 collective-permute-done.2.rbp
  43.3 0.0 collective-permute-done.3.rbm
  43.3 0.0 copy-done.3
  43.3 0.0 copy-done.1
  43.3 0.0 copy-done.5
  43.3 2.1 %prepare.1 = (bf16[2,3,128,1152]{3,2,1,0:T(8,128)(2,1)S(1)}, bf16[2,3,128,1152]{3,2,1,0:T(8,128)(2,1)S(1)}, f32[2,9,128,128]{3,2,1,0:T(8,128)S(1)}) custom-call(f32[10,128,128]{2,1,0:T(8,128)S(1)} %collective-permute-done.rap, f32[10,128,128]{2,1,0:T(8,128)} %collective-permute-done.1.ram, f32[8,128,128]{2,1,0:T(8,128)} %collective-permute-done.2.rbp, ...), custom_call_target="tpu_custom_call" | custom-call | flops 999999995904 | bytes 1000000000 | tf_op jit(solution)/shard_map/prepare/pallas_call | solution.py:257
  45.4 2.4 %collective-permute-done.6.fxp = f32[10,128,128]{2,1,0:T(8,128)} collective-permute-done((f32[10,128,128]{2,1,0:T(8,128)}, f32[10,128,128]{2,1,0:T(8,128)}, u32[]{:S(2)}, u32[]{:S(2)}) %collective-permute-start.6) | collective-permute-done | bytes 655392 | tf_op jit(solution)/shard_map/ppermute | solution.py:427
  47.9 4.4 %collective-permute-done.7.fxm = f32[10,128,128]{2,1,0:T(8,128)} collective-permute-done((f32[10,128,128]{2,1,0:T(8,128)}, f32[10,128,128]{2,1,0:T(8,128)}, u32[]{:S(2)}, u32[]{:S(2)}) %collective-permute-start.7) | collective-permute-done | bytes 655392 | tf_op jit(solution)/shard_map/ppermute | solution.py:427
  52.3 11.8 %solve.1 = f32[2,1,9,128,128]{4,3,2,1,0:T(8,128)} custom-call(bf16[2,3,128,1152]{3,2,1,0:T(8,128)(2,1)S(1)} %get-tuple-element.26.middle_h, bf16[2,3,128,1152]{3,2,1,0:T(8,128)(2,1)S(1)} %get-tuple-element.27.middle_l, bf16[2,128,768]{2,1,0:T(8,128)(2,1)S(1)} %get-tuple-element.28.outer_h, bf16[2,128,768]{2,1,0:T(8,128)(2,1)S(1)} %get-tuple-element.29.outer_l, ...), custom_call_target="tpu_custom_call" | custom-call | tf_op jit(solution)/shard_map/solve/pallas_call | solution.py:403
  (1 shorter events, 0.0 us)
Async XLA Ops:
  0.0 1.3 %copy-start = (f32[2,1,9,128,128]{4,3,2,1,0:T(8,128)S(1)}, f32[2,1,9,128,128]{4,3,2,1,0:T(8,128)}, u32[]{:S(2)}) copy-start(f32[2,1,9,128,128]{4,3,2,1,0:T(8,128)} %blocks.3) | copy-start | bytes 3538948
  1.3 1.3 %copy-start.2 = (f32[2,1,9,128,128]{4,3,2,1,0:T(8,128)S(1)}, f32[2,1,9,128,128]{4,3,2,1,0:T(8,128)}, u32[]{:S(2)}) copy-start(f32[2,1,9,128,128]{4,3,2,1,0:T(8,128)} %rhs.3) | copy-start | bytes 3538948
  2.5 0.8 %copy-start.4 = (s32[2,1,9,8,8]{2,4,3,1,0:T(8,128)S(1)}, s32[2,1,9,8,8]{2,4,3,1,0:T(8,128)}, u32[]{:S(2)}) copy-start(s32[2,1,9,8,8]{2,4,3,1,0:T(8,128)} %param.5) | copy-start | bytes 13828
  3.4 22.9 %copy-start.6 = (s32[2,1,8]{2,1,0:T(1,128)S(1)}, s32[2,1,8]{2,1,0:T(1,128)}, u32[]{:S(2)}) copy-start(s32[2,1,8]{2,1,0:T(1,128)} %param.7) | copy-start | bytes 196
  3.4 39.9 %copy-start.3 = (f32[2,1,9,128,128]{4,3,2,1,0:T(8,128)S(1)}, f32[2,1,9,128,128]{4,3,2,1,0:T(8,128)}, u32[]{:S(2)}) copy-start(f32[2,1,9,128,128]{4,3,2,1,0:T(8,128)} %rhs.3) | copy-start | bytes 3538948
  5.3 38.0 %copy-start.1 = (f32[2,1,9,128,128]{4,3,2,1,0:T(8,128)S(1)}, f32[2,1,9,128,128]{4,3,2,1,0:T(8,128)}, u32[]{:S(2)}) copy-start(f32[2,1,9,128,128]{4,3,2,1,0:T(8,128)} %blocks.3) | copy-start | bytes 3538948
  5.3 38.0 %copy-start.5 = (s32[2,1,9,8,8]{2,4,3,1,0:T(8,128)S(1)}, s32[2,1,9,8,8]{2,4,3,1,0:T(8,128)}, u32[]{:S(2)}) copy-start(s32[2,1,9,8,8]{2,4,3,1,0:T(8,128)} %param.5) | copy-start | bytes 13828
  5.3 19.0 %collective-permute-start.4 = (f32[7,128,128]{2,1,0:T(8,128)S(1)}, f32[7,128,128]{2,1,0:T(8,128)S(1)}, u32[]{:S(2)}, u32[]{:S(2)}) collective-permute-start(f32[7,128,128]{2,1,0:T(8,128)S(1)} %get-tuple-element.23), channel_id=1, source_target_pairs={{0,16},{16,32},{32,48},{48,64},{64,80},{80,96},{96,112},{1,17},{17... | collective-permute-start | bytes 1376264 | tf_op jit(solution)/shard_map/ppermute | solution.py:427
  9.1 26.8 %collective-permute-start = (f32[10,128,128]{2,1,0:T(8,128)}, f32[10,128,128]{2,1,0:T(8,128)S(1)}, u32[]{:S(2)}, u32[]{:S(2)}) collective-permute-start(f32[10,128,128]{2,1,0:T(8,128)} %get-tuple-element.19), channel_id=1, source_target_pairs={{0,1},{1,2},{2,3},{3,4},{4,5},{5,6},{6,7},{7,8},{8,9},{9,10},{10,1... | collective-permute-start | bytes 1966088 | tf_op jit(solution)/shard_map/ppermute | solution.py:427
  12.7 23.2 %collective-permute-start.1 = (f32[10,128,128]{2,1,0:T(8,128)}, f32[10,128,128]{2,1,0:T(8,128)}, u32[]{:S(2)}, u32[]{:S(2)}) collective-permute-start(f32[10,128,128]{2,1,0:T(8,128)} %get-tuple-element.20), channel_id=1, source_target_pairs={{1,0},{2,1},{3,2},{4,3},{5,4},{6,5},{7,6},{8,7},{9,8},{10,9},{11,1... | collective-permute-start | bytes 1966088 | tf_op jit(solution)/shard_map/ppermute | solution.py:427
  16.9 26.4 %collective-permute-start.2 = (f32[8,128,128]{2,1,0:T(8,128)}, f32[8,128,128]{2,1,0:T(8,128)}, u32[]{:S(2)}, u32[]{:S(2)}) collective-permute-start(f32[8,128,128]{2,1,0:T(8,128)} %get-tuple-element.21), channel_id=1, source_target_pairs={{0,1},{1,2},{2,3},{3,4},{4,5},{5,6},{6,7},{7,8},{8,9},{9,10},{10,1... | collective-permute-start | bytes 1572872 | tf_op jit(solution)/shard_map/ppermute | solution.py:427
  18.8 24.5 %collective-permute-start.3 = (f32[8,128,128]{2,1,0:T(8,128)}, f32[8,128,128]{2,1,0:T(8,128)}, u32[]{:S(2)}, u32[]{:S(2)}) collective-permute-start(f32[8,128,128]{2,1,0:T(8,128)} %get-tuple-element.22), channel_id=1, source_target_pairs={{1,0},{2,1},{3,2},{4,3},{5,4},{6,5},{7,6},{8,7},{9,8},{10,9},{11,1... | collective-permute-start | bytes 1572872 | tf_op jit(solution)/shard_map/ppermute | solution.py:427
  24.3 10.4 %collective-permute-start.5 = (f32[7,128,128]{2,1,0:T(8,128)}, f32[7,128,128]{2,1,0:T(8,128)}, u32[]{:S(2)}, u32[]{:S(2)}) collective-permute-start(f32[7,128,128]{2,1,0:T(8,128)} %get-tuple-element.24), channel_id=1, source_target_pairs={{16,0},{32,16},{48,32},{64,48},{80,64},{96,80},{112,96},{17,1},{33... | collective-permute-start | bytes 1376264 | tf_op jit(solution)/shard_map/ppermute | solution.py:427
  38.1 9.7 %collective-permute-start.6 = (f32[10,128,128]{2,1,0:T(8,128)}, f32[10,128,128]{2,1,0:T(8,128)}, u32[]{:S(2)}, u32[]{:S(2)}) collective-permute-start(f32[10,128,128]{2,1,0:T(8,128)} %get-tuple-element.31), channel_id=1, source_target_pairs={{0,16},{16,32},{32,48},{48,64},{64,80},{80,96},{96,112},{1,17},{17... | collective-permute-start | bytes 1966088 | tf_op jit(solution)/shard_map/ppermute | solution.py:427
  40.0 12.2 %collective-permute-start.7 = (f32[10,128,128]{2,1,0:T(8,128)}, f32[10,128,128]{2,1,0:T(8,128)}, u32[]{:S(2)}, u32[]{:S(2)}) collective-permute-start(f32[10,128,128]{2,1,0:T(8,128)} %get-tuple-element.32), channel_id=1, source_target_pairs={{16,0},{32,16},{48,32},{64,48},{80,64},{96,80},{112,96},{17,1},{33... | collective-permute-start | bytes 1966088 | tf_op jit(solution)/shard_map/ppermute | solution.py:427
